TPU v7x, 256 devices: a whole 4x4x8 slice. The times are simulated.
256 devices in a mesh: seg: 8 (over y_hi, x), blk: 32 (over z, y_lo, core).
Axes of the slice: x: 4, y: 4 (y_hi: 2, y_lo: 2; y = y_hi * 2 + y_lo), z: 8, core: 2. Of those that a mesh axis runs over, the one named last changes fastest.
Arguments:
- state: float32 [256, 4, 16, 2304], P(('seg', 'blk')), may hold values from -6 to 6
- metric: float32 [256, 9, 16, 2304], P(('seg', 'blk')), may hold values from -0.4 to 3, as said below
- block_map: int32 [256], replicated, may hold values from 0 to 255, as said below
- links: int32 [256, 6, 4], replicated, may hold values from -1 to 255, as said below
Outputs:
- advanced: float32 [256, 4, 16, 2304], P(('seg', 'blk'))
Inputs may be any that keep to these rules, and one draw needn't show every extreme that they name: A permutation of the block numbers; device slot d = s * 32 + p (segment s, position p along its chain) holds block block_map[d]. `links`: entries are (partner block or -1, partner face, r_i, r_x). Face 0 of the block at position p > 0 joins face 1 of the block at position p - 1 of the same segment, face 1 at p < 31 joins face 0 at p + 1, both with zero flags; faces 0 at p = 0 and 1 at p = 31 have partner -1. A block has at most one of faces 2 to 5 with a partner, and some blocks have one; that partner lies at the same position p in another segment, names this block and face back with the same flags. Unused fields of a face with partner -1 are 0. `metric`: entries 0, 4 and 8 of the second dimension are positive.
All inputs are finite; a program needn't handle non-finite values.
Results may differ from a plain program's by a relative error of at most 0.0003.
Values sent between devices are 32-bit elements; how exact they have to be, the bound alone decides.
No kernel may reach another device: no remote copies, remote signals or barrier semaphores. Data moves between devices by JAX's collectives and lax.ppermute only.
A program may use at most 64 MiB of HBM per device.

v0:
```python
import jax
import jax.numpy as jnp
from jax import lax
from jax.sharding import PartitionSpec as P

CROSS = 48


time_step = 0.05
viscosity = 0.2
compress = 1.0


def padded_2(array, sides, width):
    for axis, dim in sides:
        peers, length = (lax.axis_size(axis), array.shape[dim])
        up = [(i, (i + 1) % peers) for i in range(peers - 1)]
        down = [(j, i) for i, j in up]
        last = lax.slice_in_dim(array, length - width, length, axis=dim)
        initial = lax.slice_in_dim(array, 0, width, axis=dim)
        before = lax.ppermute(last, axis, up)
        after = lax.ppermute(initial, axis, down)
        array = jnp.concatenate([before, array, after], axis=dim)
    return array


def wall_mirror():
    return jnp.array([-1.0, -1.0, -1.0, 1.0], jnp.float32).reshape(4, 1, 1)


def shifted(extended, direction, offset):
    count = extended.shape[direction] - 4
    return lax.slice_in_dim(extended, offset, offset + count, axis=direction)


def slope(extended, direction):
    return (
        shifted(extended, direction, 0)
        - 8.0 * shifted(extended, direction, 1)
        + 8.0 * shifted(extended, direction, 3)
        - shifted(extended, direction, 4)
    ) / 12.0


def curvature(extended, direction):
    return (
        -shifted(extended, direction, 0)
        + 16.0 * shifted(extended, direction, 1)
        - 30.0 * shifted(extended, direction, 2)
        + 16.0 * shifted(extended, direction, 3)
        - shifted(extended, direction, 4)
    ) / 12.0


def rates(block_state, geometry, padded):
    slopes = [slope(padded[direction], direction + 1) for direction in range(3)]
    bends = [curvature(padded[direction], direction + 1) for direction in range(3)]
    contravariant = []
    metric_norms = []
    for direction in range(3):
        base = 3 * direction
        contravariant.append(
            geometry[base] * block_state[0]
            + geometry[base + 1] * block_state[1]
            + geometry[base + 2] * block_state[2]
        )
        metric_norms.append(
            geometry[base] * geometry[base]
            + geometry[base + 1] * geometry[base + 1]
            + geometry[base + 2] * geometry[base + 2]
        )
    results = []
    for component in range(3):
        convect = sum(
            (contravariant[direction] * slopes[direction][component] for direction in range(3))
        )
        gradient = sum(
            (geometry[3 * direction + component] * slopes[direction][3] for direction in range(3))
        )
        diffuse = sum(
            (metric_norms[direction] * bends[direction][component] for direction in range(3))
        )
        results.append(-convect - gradient + viscosity * diffuse)
    divergence = sum(
        (
            geometry[3 * direction + component] * slopes[direction][component]
            for direction in range(3)
            for component in range(3)
        )
    )
    results.append(-compress * divergence)
    return jnp.stack(results)


def lateral_faces(block_state):
    edge = block_state.shape[2]
    lower_j = jnp.stack([block_state[:, :, 0, :], block_state[:, :, 1, :]])
    upper_j = jnp.stack([block_state[:, :, edge - 1, :], block_state[:, :, edge - 2, :]])
    lower_k = jnp.stack([block_state[:, :, :, 0], block_state[:, :, :, 1]])
    upper_k = jnp.stack([block_state[:, :, :, edge - 1], block_state[:, :, :, edge - 2]])
    return jnp.stack([lower_j, upper_j, lower_k, upper_k])


def pad_lateral(block_state, ghost_layers):
    lower_j = jnp.stack([ghost_layers[0][1], ghost_layers[0][0]], axis=2)
    upper_j = jnp.stack([ghost_layers[1][0], ghost_layers[1][1]], axis=2)
    lower_k = jnp.stack([ghost_layers[2][1], ghost_layers[2][0]], axis=3)
    upper_k = jnp.stack([ghost_layers[3][0], ghost_layers[3][1]], axis=3)
    across_first = jnp.concatenate([lower_j, block_state, upper_j], axis=2)
    across_second = jnp.concatenate([lower_k, block_state, upper_k], axis=3)
    return (across_first, across_second)


def orient(layers, flip_along, flip_across):
    layers = jnp.where(flip_along == 1, jnp.flip(layers, 2), layers)
    return jnp.where(flip_across == 1, jnp.flip(layers, 3), layers)


def open_rows(block_state):
    mirror = -wall_mirror()
    lower = jnp.stack([mirror * block_state[:, 1], mirror * block_state[:, 0]], axis=1)
    upper = jnp.stack([mirror * block_state[:, -1], mirror * block_state[:, -2]], axis=1)
    return (lower, upper)


def device_of(block_map, block):
    return jnp.argmax(block_map == jnp.maximum(block, 0))


def on_device(state, metric, block_map, links):
    length = state.shape[2]
    current = state.reshape(4, length, CROSS, CROSS)
    geometry = metric.reshape(9, length, CROSS, CROSS)
    chain_size = lax.axis_size("blk")
    myself = lax.axis_index(("seg", "blk"))
    entries = links[block_map[myself]]
    joined = entries[2:, 0] >= 0
    junction = jnp.argmax(joined)
    partner_seg = device_of(block_map, entries[2 + junction, 0]) // chain_size
    flip_along = entries[2 + junction, 2]
    flip_across = entries[2 + junction, 3]

    def section_rates(block_state):
        along_vessel = padded_2(block_state, (("blk", 1),), 2)
        open_lower, open_upper = open_rows(block_state)
        lower = jnp.where(entries[0, 0] >= 0, along_vessel[:, :2], open_lower)
        upper = jnp.where(entries[1, 0] >= 0, along_vessel[:, length + 2 :], open_upper)
        along_vessel = jnp.concatenate([lower, block_state, upper], axis=1)
        face_layers = lateral_faces(block_state)
        outgoing = face_layers[junction]
        every_face = lax.all_gather(outgoing[None], "seg", axis=0, tiled=True)
        received = every_face[partner_seg]
        received = orient(received, flip_along, flip_across)
        ghost_layers = [
            jnp.where(joined[side], received, wall_mirror() * face_layers[side])
            for side in range(4)
        ]
        across_first, across_second = pad_lateral(block_state, ghost_layers)
        return rates(block_state, geometry, (along_vessel, across_first, across_second))

    first_section = current + time_step * section_rates(current)
    advanced = 0.5 * current + 0.5 * (first_section + time_step * section_rates(first_section))
    return advanced.reshape(state.shape)


def solution(mesh):
    in_specs = (P(("seg", "blk"), None, None, None), P(("seg", "blk"), None, None, None), P(), P())
    out_specs = P(("seg", "blk"), None, None, None)
    return jax.shard_map(
        on_device, mesh=mesh, in_specs=in_specs, out_specs=out_specs, check_vma=False
    )
```

profile of v0, /device:TPU:105, one launch (start us, length us, event | category | flops | bytes accessed | tf_op | source)
XLA Modules:
  0.0 222.6 jit_solution(836842974796536693)
XLA Ops:
  0.0 2.0 reshape.512
  2.1 0.8 fusion.49
  2.9 5.2 %collective-permute-start = (f32[4,2,48,48]{3,2,1,0:T(8,128)}, f32[4,2,48,48]{3,2,1,0:T(8,128)}, u32[]{:S(2)}, u32[]{:S(2)}) collective-permute-start(f32[4,2,48,48]{3,2,1,0:T(8,128)} %get-tuple-element.47), channel_id=1, source_target_pairs={{0,1},{1,2},{2,3},{3,4},{4,5},{5,6},{6,7},{7,8},{8,9},{9,10},{10,1... | collective-permute-start | bytes 221192 | tf_op jit(solution)/shard_map/ppermute | solution.py:21
  8.1 1.9 collective-permute-start.1
  12.9 0.7 bitcast_reduce_fusion
  13.6 3.4 %fusion.50 = (f32[4,16,48,1]{3,2,1,0:T(8,128)}, f32[4,16,48,1]{3,2,1,0:T(8,128)}, f32[4,16,48,1]{3,2,1,0:T(8,128)}, f32[4,16,48,1]{3,2,1,0:T(8,128)S(1)}) fusion(f32[4,16,48,48]{3,2,1,0:T(8,128)S(1)} %reshape.512), kind=kLoop, calls=%fused_computation.191 | loop fusion | bytes 98304 | tf_op jit(solution)/shard_map/slice | solution.py:100
  20.0 0.7 compare_reduce_fusion
  23.2 0.7 fusion.59
  24.5 2.0 copy.257
  26.4 2.0 copy.256
  28.4 2.0 copy.255
  31.7 29.9 %all_gather.6 = f32[8,2,4,16,48]{4,3,2,1,0:T(8,128)S(1)} all-gather(f32[1,2,4,16,48]{4,3,2,1,0:T(8,128)S(1)} %fusion.38), channel_id=1, replica_groups=mesh['seg'=8,'blk'=32] {'seg'}, dimensions={0}, use_global_device_ids=true | all-gather | bytes 221184 | tf_op jit(solution)/shard_map/all_gather | solution.py:151
  63.6 1.9 multiply_select_fusion.7
  66.1 1.7 copy.233
  67.9 1.7 copy.230
  69.6 1.8 copy.235
  71.4 7.5 %subtract_multiply_fusion.9 = f32[4,16,48,48]{3,2,1,0:T(8,128)} fusion(f32[4,16,48,48]{3,2,1,0:T(8,128)S(1)} %reshape.512, f32[4,16,48,1]{3,2,1,0:T(8,128)S(1)} %copy.231, f32[4,16,48,1]{3,2,1,0:T(8,128)} %copy.233, f32[4,16,48,1]{3,2,1,0:T(8,128)} %copy.230, f32[4,16,48,1]{3,2,1,0:T(8,128)} %copy.235), kind=kLoop, calls=%fused_computation.55 | loop fusion | flops 1769472 | bytes 1228800 | tf_op jit(solution)/shard_map/div | solution.py:37
  78.8 4.5 %subtract_multiply_fusion.6 = f32[4,16,48,48]{3,2,1,0:T(8,128)} fusion(f32[4,16,48,48]{3,2,1,0:T(8,128)S(1)} %reshape.512, f32[4,16,48,1]{3,2,1,0:T(8,128)S(1)} %copy.231, f32[4,16,48,1]{3,2,1,0:T(8,128)S(1)} %copy-done.20, f32[4,16,48,1]{3,2,1,0:T(8,128)S(1)} %copy-done.22, f32[4,16,48,1]{3,2,1,0:T(8,128)S(1)} %copy-done.24), kind=kLoop, calls=%fused_computation.52 | loop fusion | flops 2211840 | bytes 1228800 | tf_op jit(solution)/shard_map/div | solution.py:46
  83.3 2.3 %subtract_multiply_fusion.10 = f32[4,16,48,48]{3,2,1,0:T(8,128)} fusion(f32[4,16,48,48]{3,2,1,0:T(8,128)S(1)} %reshape.512, f32[4,16,1,48]{3,2,1,0:T(1,128)S(1)} %bitcast.159, f32[4,16,1,48]{3,2,1,0:T(1,128)S(1)} %bitcast.163, f32[4,16,1,48]{3,2,1,0:T(1,128)S(1)} %bitcast.157, f32[4,16,1,48]{3,2,1,0:T(1,128)S(1)} %bitcast.161), kind=kLoop, calls=%fused_computation.56 | loop fusion | flops 1769472 | bytes 1228800 | tf_op jit(solution)/shard_map/div | solution.py:37
  85.6 2.4 %subtract_multiply_fusion.7 = f32[4,16,48,48]{3,2,1,0:T(8,128)} fusion(f32[4,16,48,48]{3,2,1,0:T(8,128)S(1)} %reshape.512, f32[4,16,1,48]{3,2,1,0:T(1,128)S(1)} %bitcast.160, f32[4,16,1,48]{3,2,1,0:T(1,128)S(1)} %bitcast.164, f32[4,16,1,48]{3,2,1,0:T(1,128)S(1)} %bitcast.158, f32[4,16,1,48]{3,2,1,0:T(1,128)S(1)} %bitcast.162), kind=kLoop, calls=%fused_computation.53 | loop fusion | flops 2211840 | bytes 1228800 | tf_op jit(solution)/shard_map/div | solution.py:46
  88.0 0.8 fusion.53
  88.8 0.8 fusion.52
  90.1 1.0 squeeze.54
  91.3 1.2 squeeze.49
  92.5 1.1 squeeze.48
  93.7 1.0 squeeze.44
  94.7 1.1 squeeze.42
  95.8 2.0 squeeze.40
  97.8 0.8 slice_multiply_fusion.23
  100.5 1.9 squeeze.45
  102.3 1.9 squeeze.43
  104.2 1.9 squeeze.41
  106.1 1.1 maximum_select_fusion
  107.1 1.1 maximum_select_fusion.1
  108.3 1.1 subtract_multiply_fusion.8
  111.0 0.9 copy-done.32
  115.8 2.9 %slice_reduce_fusion.1 = (f32[4,16,48]{2,1,0:T(8,128)S(1)}, f32[4,16,48]{2,1,0:T(8,128)S(1)}, f32[4,16,48]{2,1,0:T(8,128)S(1)}, f32[4,16,48]{2,1,0:T(8,128)S(1)}) fusion(f32[4,16,48,48]{3,2,1,0:T(8,128)S(1)} %fusion.4), kind=kLoop, calls=%fused_computation.25 | loop fusion | bytes 98304 | tf_op jit(solution)/shard_map/slice | solution.py:100
  118.7 0.8 fusion.47
  119.5 0.9 slice_multiply_fusion.19
  120.5 29.6 %all_gather.7 = f32[8,2,4,16,48]{4,3,2,1,0:T(8,128)S(1)} all-gather(f32[1,2,4,16,48]{4,3,2,1,0:T(8,128)S(1)} %fusion.35), channel_id=1, replica_groups=mesh['seg'=8,'blk'=32] {'seg'}, dimensions={0}, use_global_device_ids=true | all-gather | bytes 221184 | tf_op jit(solution)/shard_map/all_gather | solution.py:151
  150.3 1.3 multiply_select_fusion.2
  151.5 2.6 %multiply_select_fusion.3 = (f32[2,4,16,48]{3,2,1,0:T(8,128)}, f32[2,4,16,48]{3,2,1,0:T(8,128)S(1)}, f32[2,4,16,48]{3,2,1,0:T(8,128)S(1)}) fusion(f32[2,4,16,48]{3,2,1,0:T(8,128)S(1)} %get-tuple-element.18, f32[1,4,16,48]{3,2,1,0:T(8,128)S(1)} %bitcast.184, f32[1,4,16,48]{3,2,1,0:T(8,128)S(1)} %bitcast.182, f32[4]{0:T(128)S(1)} %copy-done.54, pred[]{:T(512)} %bitcast.4, ...), kind=kLoop, calls=%fused_computation.154 | loop fusion | flops 55296 | bytes 172051 | tf_op jit(solution)/shard_map/jit(_where)/select_n | solution.py:155
  154.1 1.8 copy.245
  155.9 1.7 copy.247
  157.6 1.7 copy.244
  159.3 1.8 copy.249
  161.1 7.2 %subtract_multiply_fusion.3 = f32[4,16,48,48]{3,2,1,0:T(8,128)S(1)} fusion(f32[4,16,48,48]{3,2,1,0:T(8,128)S(1)} %fusion.4, f32[4,16,48,1]{3,2,1,0:T(8,128)} %copy.245, f32[4,16,48,1]{3,2,1,0:T(8,128)} %copy.247, f32[4,16,48,1]{3,2,1,0:T(8,128)} %copy.244, f32[4,16,48,1]{3,2,1,0:T(8,128)} %copy.249), kind=kLoop, calls=%fused_computation.49 | loop fusion | flops 1769472 | bytes 1228800 | tf_op jit(solution)/shard_map/div | solution.py:37
  168.4 4.5 %subtract_multiply_fusion = f32[4,16,48,48]{3,2,1,0:T(8,128)} fusion(f32[4,16,48,48]{3,2,1,0:T(8,128)S(1)} %fusion.4, f32[4,16,48,1]{3,2,1,0:T(8,128)S(1)} %copy-done.19, f32[4,16,48,1]{3,2,1,0:T(8,128)S(1)} %copy-done.21, f32[4,16,48,1]{3,2,1,0:T(8,128)S(1)} %copy-done.23, f32[4,16,48,1]{3,2,1,0:T(8,128)S(1)} %copy-done.25), kind=kLoop, calls=%fused_computation.46 | loop fusion | flops 2211840 | bytes 1228800 | tf_op jit(solution)/shard_map/div | solution.py:46
  172.9 17.4 %collective-permute-start.2 = (f32[4,2,48,48]{3,2,1,0:T(8,128)}, f32[4,2,48,48]{3,2,1,0:T(8,128)}, u32[]{:S(2)}, u32[]{:S(2)}) collective-permute-start(f32[4,2,48,48]{3,2,1,0:T(8,128)} %get-tuple-element.41), channel_id=1, source_target_pairs={{0,1},{1,2},{2,3},{3,4},{4,5},{5,6},{6,7},{7,8},{8,9},{9,10},{10,1... | collective-permute-start | bytes 221192 | tf_op jit(solution)/shard_map/ppermute | solution.py:21
  190.3 2.4 %subtract_multiply_fusion.1 = f32[4,16,48,48]{3,2,1,0:T(8,128)} fusion(f32[4,16,48,48]{3,2,1,0:T(8,128)S(1)} %fusion.4, f32[4,16,1,48]{3,2,1,0:T(1,128)S(1)} %bitcast.151, f32[4,16,1,48]{3,2,1,0:T(1,128)S(1)} %bitcast.155, f32[4,16,1,48]{3,2,1,0:T(1,128)S(1)} %bitcast.149, f32[4,16,1,48]{3,2,1,0:T(1,128)S(1)} %bitcast.153), kind=kLoop, calls=%fused_computation.47 | loop fusion | flops 2211840 | bytes 1228800 | tf_op jit(solution)/shard_map/div | solution.py:46
  192.7 2.3 %subtract_multiply_fusion.4 = f32[4,16,48,48]{3,2,1,0:T(8,128)} fusion(f32[4,16,48,48]{3,2,1,0:T(8,128)S(1)} %fusion.4, f32[4,16,1,48]{3,2,1,0:T(1,128)S(1)} %bitcast.152, f32[4,16,1,48]{3,2,1,0:T(1,128)S(1)} %bitcast.156, f32[4,16,1,48]{3,2,1,0:T(1,128)S(1)} %bitcast.150, f32[4,16,1,48]{3,2,1,0:T(1,128)S(1)} %bitcast.154), kind=kLoop, calls=%fused_computation.50 | loop fusion | flops 1769472 | bytes 1228800 | tf_op jit(solution)/shard_map/div | solution.py:37
  195.0 1.8 stack.120
  196.8 1.8 stack.119
  198.6 1.8 stack.118
  200.5 1.8 stack.117
  202.3 2.2 collective-permute-start.3
  204.5 1.1 maximum_select_fusion.2
  205.5 6.0 %collective-permute-done.3 = f32[4,2,48,48]{3,2,1,0:T(8,128)S(1)} collective-permute-done((f32[4,2,48,48]{3,2,1,0:T(8,128)}, f32[4,2,48,48]{3,2,1,0:T(8,128)S(1)}, u32[]{:S(2)}, u32[]{:S(2)}) %collective-permute-start.3) | collective-permute-done | bytes 73760 | tf_op jit(solution)/shard_map/ppermute | solution.py:22
  211.6 1.0 maximum_select_fusion.3
  212.6 1.1 subtract_multiply_fusion.2
  214.9 1.2 add_multiply_fusion
  216.1 0.7 copy-done.33
  217.3 1.4 fusion.19
  221.4 0.9 fusion.8
  (166 shorter events, 14.8 us)
Async XLA Ops:
  0.0 10.1 %copy-start.57 = (s32[256]{0:T(256)S(1)}, s32[256]{0:T(256)}, u32[]{:S(2)}) copy-start(s32[256]{0:T(256)} %param.16) | copy-start | bytes 3076
  0.0 12.6 %copy-start.55 = (s32[256,6,4]{0,2,1:T(4,128)S(1)}, s32[256,6,4]{0,2,1:T(4,128)}, u32[]{:S(2)}) copy-start(s32[256,6,4]{0,2,1:T(4,128)} %param.17) | copy-start | bytes 73732
  2.9 103.2 %collective-permute-start = (f32[4,2,48,48]{3,2,1,0:T(8,128)}, f32[4,2,48,48]{3,2,1,0:T(8,128)}, u32[]{:S(2)}, u32[]{:S(2)}) collective-permute-start(f32[4,2,48,48]{3,2,1,0:T(8,128)} %get-tuple-element.47), channel_id=1, source_target_pairs={{0,1},{1,2},{2,3},{3,4},{4,5},{5,6},{6,7},{7,8},{8,9},{9,10},{10,1... | collective-permute-start | bytes 221192 | tf_op jit(solution)/shard_map/ppermute | solution.py:21
  8.1 99.1 %collective-permute-start.1 = (f32[4,2,48,48]{3,2,1,0:T(8,128)}, f32[4,2,48,48]{3,2,1,0:T(8,128)}, u32[]{:S(2)}, u32[]{:S(2)}) collective-permute-start(f32[4,2,48,48]{3,2,1,0:T(8,128)} %get-tuple-element.46), channel_id=1, source_target_pairs={{1,0},{2,1},{3,2},{4,3},{5,4},{6,5},{7,6},{8,7},{9,8},{10,9},{11,1... | collective-permute-start | bytes 221192 | tf_op jit(solution)/shard_map/ppermute | solution.py:22
  30.4 32.6 %copy-start.54 = (f32[4]{0:T(128)S(1)}, f32[4]{0:T(128)}, u32[]{:S(2)}) copy-start(f32[4]{0:T(128)} %constant.143.clone) | copy-start | bytes 52
  71.4 7.5 %copy-start.20 = (f32[4,16,48,1]{3,2,1,0:T(8,128)S(1)}, f32[4,16,48,1]{3,2,1,0:T(8,128)}, u32[]{:S(2)}) copy-start(f32[4,16,48,1]{3,2,1,0:T(8,128)} %copy.233) | copy-start | bytes 36868
  71.4 7.5 %copy-start.22 = (f32[4,16,48,1]{3,2,1,0:T(8,128)S(1)}, f32[4,16,48,1]{3,2,1,0:T(8,128)}, u32[]{:S(2)}) copy-start(f32[4,16,48,1]{3,2,1,0:T(8,128)} %copy.230) | copy-start | bytes 36868
  71.4 7.5 %copy-start.24 = (f32[4,16,48,1]{3,2,1,0:T(8,128)S(1)}, f32[4,16,48,1]{3,2,1,0:T(8,128)}, u32[]{:S(2)}) copy-start(f32[4,16,48,1]{3,2,1,0:T(8,128)} %copy.235) | copy-start | bytes 36868
  85.6 2.4 %copy-start.36 = (f32[1,4,16,2304]{3,2,1,0:T(8,128)S(1)}, f32[1,4,16,2304]{3,2,1,0:T(8,128)}, u32[]{:S(2)}) copy-start(f32[1,4,16,2304]{3,2,1,0:T(8,128)} %param.14) | copy-start | bytes 1769476
  85.6 3.2 %copy-start.47 = (f32[1,9,16,2304]{3,2,1,0:T(8,128)S(1)}, f32[1,9,16,2304]{3,2,1,0:T(8,128)}, u32[]{:S(2)}) copy-start(f32[1,9,16,2304]{3,2,1,0:T(8,128)} %param.15) | copy-start | bytes 3981316
  89.9 23.7 %copy-start = (f32[1,16,48,48]{3,2,1,0:T(8,128)}, f32[1,16,48,48]{3,2,1,0:T(8,128)S(1)}, u32[]{:S(2)}) copy-start(f32[1,16,48,48]{3,2,1,0:T(8,128)S(1)} %squeeze.56) | copy-start | bytes 442372
  91.0 6.8 %copy-start.56 = (f32[4]{0:T(128)S(1)}, f32[4]{0:T(128)}, u32[]{:S(2)}) copy-start(f32[4]{0:T(128)} %constant.146) | copy-start | bytes 52
  91.3 22.3 %copy-start.4 = (f32[1,16,48,48]{3,2,1,0:T(8,128)}, f32[1,16,48,48]{3,2,1,0:T(8,128)S(1)}, u32[]{:S(2)}) copy-start(f32[1,16,48,48]{3,2,1,0:T(8,128)S(1)} %squeeze.50) | copy-start | bytes 442372
  92.5 21.5 %copy-start.2 = (f32[1,16,48,48]{3,2,1,0:T(8,128)}, f32[1,16,48,48]{3,2,1,0:T(8,128)S(1)}, u32[]{:S(2)}) copy-start(f32[1,16,48,48]{3,2,1,0:T(8,128)S(1)} %squeeze.49) | copy-start | bytes 442372
  95.8 18.2 %copy-start.6 = (f32[1,16,48,48]{3,2,1,0:T(8,128)}, f32[1,16,48,48]{3,2,1,0:T(8,128)S(1)}, u32[]{:S(2)}) copy-start(f32[1,16,48,48]{3,2,1,0:T(8,128)S(1)} %squeeze.42) | copy-start | bytes 442372
  108.2 1.2 copy-start.8
  108.2 1.5 copy-start.10
  108.2 2.0 copy-start.11
  108.2 2.0 copy-start.26
  108.2 2.1 copy-start.28
  108.3 2.3 %copy-start.30 = (f32[1,16,48,48]{3,2,1,0:T(8,128)S(1)}, f32[1,16,48,48]{3,2,1,0:T(8,128)}, u32[]{:S(2)}) copy-start(f32[1,16,48,48]{3,2,1,0:T(8,128)} %squeeze.40) | copy-start | bytes 442372
  110.5 1.4 copy-start.32
  110.5 2.0 copy-start.34
  110.5 2.1 copy-start.42
  110.5 2.2 copy-start.43
  110.5 2.3 %copy-start.44 = (f32[1,16,48,48]{3,2,1,0:T(8,128)S(1)}, f32[1,16,48,48]{3,2,1,0:T(8,128)}, u32[]{:S(2)}) copy-start(f32[1,16,48,48]{3,2,1,0:T(8,128)} %squeeze.41) | copy-start | bytes 442372
  111.0 4.0 %copy-start.38 = (f32[1,16,48,48]{3,2,1,0:T(8,128)}, f32[1,16,48,48]{3,2,1,0:T(8,128)S(1)}, u32[]{:S(2)}) copy-start(f32[1,16,48,48]{3,2,1,0:T(8,128)S(1)} %add_multiply_fusion.1) | copy-start | bytes 442372
  113.5 0.8 copy-start.13
  113.5 0.9 copy-start.15
  113.5 1.0 copy-start.17
  113.5 1.5 copy-start.39
  114.5 0.8 copy-start.41
  115.0 0.7 copy-start.40
  161.1 7.2 %copy-start.19 = (f32[4,16,48,1]{3,2,1,0:T(8,128)S(1)}, f32[4,16,48,1]{3,2,1,0:T(8,128)}, u32[]{:S(2)}) copy-start(f32[4,16,48,1]{3,2,1,0:T(8,128)} %copy.245) | copy-start | bytes 36868
  161.1 7.2 %copy-start.21 = (f32[4,16,48,1]{3,2,1,0:T(8,128)S(1)}, f32[4,16,48,1]{3,2,1,0:T(8,128)}, u32[]{:S(2)}) copy-start(f32[4,16,48,1]{3,2,1,0:T(8,128)} %copy.247) | copy-start | bytes 36868
  161.1 7.2 %copy-start.23 = (f32[4,16,48,1]{3,2,1,0:T(8,128)S(1)}, f32[4,16,48,1]{3,2,1,0:T(8,128)}, u32[]{:S(2)}) copy-start(f32[4,16,48,1]{3,2,1,0:T(8,128)} %copy.244) | copy-start | bytes 36868
  161.1 7.2 %copy-start.25 = (f32[4,16,48,1]{3,2,1,0:T(8,128)S(1)}, f32[4,16,48,1]{3,2,1,0:T(8,128)}, u32[]{:S(2)}) copy-start(f32[4,16,48,1]{3,2,1,0:T(8,128)} %copy.249) | copy-start | bytes 36868
  168.3 4.5 %copy-start.53 = (f32[2,4,16,48]{3,2,1,0:T(8,128)S(1)}, f32[2,4,16,48]{3,2,1,0:T(8,128)}, u32[]{:S(2)}) copy-start(f32[2,4,16,48]{3,2,1,0:T(8,128)} %get-tuple-element.68) | copy-start | bytes 73732
  168.3 4.5 %copy-start.52 = (f32[2,4,16,48]{3,2,1,0:T(8,128)S(1)}, f32[2,4,16,48]{3,2,1,0:T(8,128)}, u32[]{:S(2)}) copy-start(f32[2,4,16,48]{3,2,1,0:T(8,128)} %get-tuple-element.17) | copy-start | bytes 73732
  172.9 31.6 %collective-permute-start.2 = (f32[4,2,48,48]{3,2,1,0:T(8,128)}, f32[4,2,48,48]{3,2,1,0:T(8,128)}, u32[]{:S(2)}, u32[]{:S(2)}) collective-permute-start(f32[4,2,48,48]{3,2,1,0:T(8,128)} %get-tuple-element.41), channel_id=1, source_target_pairs={{0,1},{1,2},{2,3},{3,4},{4,5},{5,6},{6,7},{7,8},{8,9},{9,10},{10,1... | collective-permute-start | bytes 221192 | tf_op jit(solution)/shard_map/ppermute | solution.py:21
  202.3 9.3 %collective-permute-start.3 = (f32[4,2,48,48]{3,2,1,0:T(8,128)}, f32[4,2,48,48]{3,2,1,0:T(8,128)S(1)}, u32[]{:S(2)}, u32[]{:S(2)}) collective-permute-start(f32[4,2,48,48]{3,2,1,0:T(8,128)} %get-tuple-element.40), channel_id=1, source_target_pairs={{1,0},{2,1},{3,2},{4,3},{5,4},{6,5},{7,6},{8,7},{9,8},{10,9},{11,1... | collective-permute-start | bytes 221192 | tf_op jit(solution)/shard_map/ppermute | solution.py:22
  212.6 1.2 copy-start.1
  212.6 1.2 copy-start.3
  212.6 1.2 copy-start.5
  212.6 1.3 copy-start.7
  212.6 1.4 copy-start.9
  212.6 2.0 copy-start.12
  212.6 2.0 copy-start.27
  212.6 2.1 copy-start.29
  212.6 2.2 %copy-start.31 = (f32[1,16,48,48]{3,2,1,0:T(8,128)S(1)}, f32[1,16,48,48]{3,2,1,0:T(8,128)}, u32[]{:S(2)}) copy-start(f32[1,16,48,48]{3,2,1,0:T(8,128)} %squeeze.40) | copy-start | bytes 442372
  214.9 1.2 copy-start.14
  214.9 1.2 copy-start.16
  214.9 1.2 copy-start.18
  214.9 1.9 copy-start.33
  214.9 2.4 %copy-start.35 = (f32[4,16,48,48]{3,2,1,0:T(8,128)S(1)}, f32[4,16,48,48]{3,2,1,0:T(8,128)}, u32[]{:S(2)}) copy-start(f32[4,16,48,48]{3,2,1,0:T(8,128)} %subtract_multiply_fusion.1) | copy-start | bytes 1769476
  219.1 1.0 copy-start.46
  220.1 1.0 copy-start.45
  220.1 1.2 copy-start.37
  220.1 1.2 copy-start.48
  220.1 1.2 copy-start.49
  220.1 1.3 copy-start.50
  220.1 1.3 copy-start.51
where the time goes:
time: 227 us; the launch traced here: 223 us
  local copies, waits for them, and re-layouts  63.1 us (28%)
  blocking collectives  59.5 us (26%)
  other arithmetic  55.8 us (25%)
  starting transfers between devices  26.7 us (12%)
  between operations  11.5 us (5%)
  waiting for transfers between devices  6.05 us (3%)
    all_gather x2, blocking collectives, section_rates(): every_face = lax.all_gather(outgoing[None], 'seg', axis=0, tiled=True)  59.5 us
    ppermute x2, starting transfers between devices, padded_2(): before = lax.ppermute(last, axis, up)  22.6 us
    div x4, other arithmetic, slope(): (shifted(extended, direction, 0) - 8.0 * shifted(extended, direction, 1)...  19.2 us
    div x6, other arithmetic, curvature(): (-shifted(extended, direction, 0) + 16.0 * shifted(extended, direction, 1...  16 us
    unnamed x120, local copies, waits for them, and re-layouts  13.9 us
    another operation x8, local copies, waits for them, and re-layouts, rates(): return jnp.stack(results)  8.03 us
    another operation x6, local copies, waits for them, and re-layouts, pad_lateral(): upper_k = jnp.stack([ghost_layers[3][0], ghost_layers[3][1]], axis=3)  6.97 us
    select_n x4, other arithmetic, section_rates(): jnp.where(joined[side], received, wall_mirror() * face_layers[side])  6.42 us
  transfers between devices with their start and end apart: 4, of which 1 were waited for; matrix products, arithmetic and copies ran while one was open for 31% of the time, Pallas kernels for 0%

commit v1 on v0

v1 whole, which is shorter than its diff:
```python
import functools
import jax
import jax.numpy as jnp
from jax import lax
from jax.experimental import pallas as pl
from jax.experimental.pallas import tpu as pltpu
from jax.sharding import PartitionSpec as P

LEN, CROSS, CELLS, TILES = 16, 48, 2304, 18
SEGS, CHAIN = 8, 32
time_step = 0.05
viscosity = 0.2
compress = 1.0
SIGN = (-1.0, -1.0, -1.0, 1.0)
VMEM = pl.BlockSpec(memory_space=pltpu.VMEM)
SMEM = pl.BlockSpec(memory_space=pltpu.SMEM)


def lanes_of(rows=8):
    return lax.broadcasted_iota(jnp.int32, (rows, 128), 1)


def gather_lanes(values, index):
    parts = [
        jnp.take_along_axis(values[r : r + 8], index, axis=1, mode="promise_in_bounds")
        for r in range(0, values.shape[0], 8)
    ]
    return parts[0] if len(parts) == 1 else jnp.concatenate(parts, axis=0)


def reversed_rows(values):
    index = 7 - lax.broadcasted_iota(jnp.int32, (8, 128), 0)
    flip = lambda part: jnp.take_along_axis(part, index, axis=0, mode="promise_in_bounds")
    return jnp.concatenate([flip(values[8:16]), flip(values[0:8])], axis=0)


def joined_face(device, block_map, links):
    block = block_map[device]
    face, partner, along, across = jnp.int32(0), jnp.int32(-1), jnp.int32(0), jnp.int32(0)
    for side in range(2, 6):
        other = links[side, 0, block]
        here = other >= 0
        face = jnp.where(here, side, face)
        partner = jnp.where(here, other, partner)
        along = jnp.where(here, links[side, 2, block], along)
        across = jnp.where(here, links[side, 3, block], across)
    position = lax.rem(device, CHAIN)
    segment = jnp.int32(0)
    for s in range(SEGS):
        segment = jnp.where(block_map[s * CHAIN + position] == partner, s, segment)
    return face, segment, along, across


def face_source(face, across, first_layer):
    lane = lanes_of()
    layer = jnp.where(lane >= CROSS, 1, 0)
    place = lane - layer * CROSS
    place = jnp.where(across == 1, CROSS - 1 - place, place)
    depth = first_layer + layer
    depth = jnp.where((face == 3) | (face == 5), CROSS - 1 - depth, depth)
    return jnp.where(face <= 3, depth * CROSS + place, place * CROSS + depth)


def extract_faces(load, names, source, store, along):
    for name in names:
        found = jnp.zeros((LEN, 128), jnp.float32)
        for t in range(TILES):
            local = source - 128 * t
            inside = (local >= 0) & (local < 128)
            local = jnp.clip(local, 0, 127)
            tile = load(name, t)
            picked = gather_lanes(tile, local)
            found = jnp.where(jnp.concatenate([inside, inside], axis=0), picked, found)
        found = jnp.where(along == 1, reversed_rows(found), found)
        store(name, found)


def write_joint(load, joint_ref, face, along, across):
    def store(c, values):
        joint_ref[16 * c : 16 * c + 16, :] = values

    extract_faces(load, range(4), face_source(face, across, 0), store, along)


def write_chain(field, even_ref, odd_ref, position):
    even = lax.rem(position, 2) == 0
    for c in range(4):
        low, high = field[c, 0:2, :], field[c, LEN - 2 : LEN, :]
        even_ref[2 * c : 2 * c + 2, :] = jnp.where(even, high, low)
        odd_ref[2 * c : 2 * c + 2, :] = jnp.where(even, low, high)


def first_kernel(q, block_map, links, joint_ref, even_ref, odd_ref, meta):
    segment, position = lax.axis_index("seg"), lax.axis_index("blk")
    face, partner, along, across = joined_face(segment * CHAIN + position, block_map, links)
    mate = (segment + 4) % 8
    _, mate_partner, _, _ = joined_face(mate * CHAIN + position, block_map, links)
    meta[0] = face
    meta[1] = along
    meta[2] = across
    meta[3] = jnp.where(partner // 4 == segment // 4, (partner ^ segment) & 3, 0)
    meta[4] = (mate_partner ^ segment) & 3
    block = block_map[segment * CHAIN + position]
    meta[5] = jnp.where(links[0, 0, block] >= 0, 1, 0)
    meta[6] = jnp.where(links[1, 0, block] >= 0, 1, 0)
    meta[7] = position
    write_joint(lambda c, t: q[c, :, 128 * t : 128 * t + 128], joint_ref, face, along, across)
    write_chain(q, even_ref, odd_ref, position)


def pick_kernel(own, one, two, three, meta, out):
    choice = meta[4]
    for n, ref in enumerate((own, one, two, three)):

        @pl.when(choice == n)
        def _(ref=ref):
            out[...] = ref[...]


def shifted_lanes(before, here, after, shift):
    lane = lanes_of(LEN)
    if shift > 0:
        return jnp.where(
            lane < 128 - shift, pltpu.roll(here, 128 - shift, 1), pltpu.roll(after, 128 - shift, 1)
        )
    return jnp.where(lane >= -shift, pltpu.roll(here, -shift, 1), pltpu.roll(before, -shift, 1))


def shifted_rows(padded, shift):
    return pltpu.roll(padded, (-shift) % 32, 0)[8:24]


def differences(m2, m1, here, p1, p2):
    return 8.0 * (p1 - m1) - (p2 - m2)


def bends(m2, m1, here, p1, p2):
    return 16.0 * (p1 + m1) - (p2 + m2) - 30.0 * here


def advance(stencils, geometry):
    here = [stencils[c][0][2] for c in range(4)]
    moves = [-(time_step / 12.0) * geometry[n] for n in range(9)]
    result = list(here)
    fall = None
    for a in range(3):
        g = geometry[3 * a : 3 * a + 3]
        n = moves[3 * a : 3 * a + 3]
        speed = n[0] * here[0] + n[1] * here[1] + n[2] * here[2]
        spread = (viscosity * time_step / 12.0) * (g[0] * g[0] + g[1] * g[1] + g[2] * g[2])
        drop = differences(*stencils[3][a])
        for b in range(3):
            slope = differences(*stencils[b][a])
            result[b] = result[b] + speed * slope + n[b] * drop + spread * bends(*stencils[b][a])
            term = n[b] * slope
            fall = term if fall is None else fall + term
    result[3] = result[3] + compress * fall
    return result


def section(q, metric, joint, low, high, face, store):
    lane = lanes_of(LEN)
    load = lambda c, t: q[c, :, 128 * t : 128 * t + 128]
    before_first, after_last, ghosts = [], [], []
    for c in range(4):
        received = joint(c)
        ghosts.append(received)
        source = jnp.where(face == 2, received, SIGN[c] * load(c, 0))
        before_first.append(jnp.where(lane >= 80, pltpu.roll(source, 80, 1), pltpu.roll(source, 112, 1)))
        last = SIGN[c] * load(c, TILES - 1)
        wall = jnp.where(lane < CROSS, pltpu.roll(last, 48, 1), pltpu.roll(last, 16, 1))
        after_last.append(jnp.where(face == 3, received, wall))

    def tile(c, t):
        return before_first[c] if t < 0 else after_last[c] if t >= TILES else load(c, t)

    for t in range(TILES):
        flat = 128 * t + lane
        j = flat // CROSS
        k = flat - j * CROSS
        joined = ((face == 4) & (k < 2)) | ((face == 5) & (k >= 46))
        near = j[:8]
        far = jnp.where((k == 0) | (k == 47), j + CROSS, j)[:8]
        stencils = []
        for c in range(4):
            before, here, after = tile(c, t - 1), tile(c, t), tile(c, t + 1)
            rows = jnp.concatenate([low(c, t), here, high(c, t)], axis=0)
            along_i = [shifted_rows(rows, s) for s in (-2, -1)] + [here] + [shifted_rows(rows, s) for s in (1, 2)]
            along_j = [shifted_lanes(before, here, after, CROSS * s) if s else here for s in range(-2, 3)]
            raw = [shifted_lanes(before, here, after, s) if s else here for s in range(-2, 3)]
            first = jnp.where(joined, gather_lanes(ghosts[c], near), SIGN[c] * here)
            wall = SIGN[c] * jnp.where((k == 0) | (k == 46), raw[3], raw[1])
            second = jnp.where(joined, gather_lanes(ghosts[c], far), wall)
            along_k = [
                jnp.where(k < 2, second, raw[0]),
                jnp.where(k == 0, first, raw[1]),
                here,
                jnp.where(k == 47, first, raw[3]),
                jnp.where(k >= 46, second, raw[4]),
            ]
            stencils.append((along_i, along_j, along_k))
        store(t, advance(stencils, [metric[n, :, 128 * t : 128 * t + 128] for n in range(9)]))


def chain_ghosts(q, even_ref, odd_ref, low_ref, high_ref, meta):
    even = lax.rem(meta[7], 2) == 0
    has_low, has_high = meta[5] == 1, meta[6] == 1
    for c in range(4):
        rows = slice(2 * c, 2 * c + 2)
        from_even, from_odd = even_ref[rows, :], odd_ref[rows, :]
        mirror = -SIGN[c]
        low_ref[c, 6:8, :] = jnp.where(even, from_odd, from_even)
        high_ref[c, 0:2, :] = jnp.where(even, from_even, from_odd)

        @pl.when(jnp.logical_not(has_low))
        def _():
            low_ref[c, 7:8, :] = mirror * q[c, 0:1, :]
            low_ref[c, 6:7, :] = mirror * q[c, 1:2, :]

        @pl.when(jnp.logical_not(has_high))
        def _():
            high_ref[c, 0:1, :] = mirror * q[c, LEN - 1 : LEN, :]
            high_ref[c, 1:2, :] = mirror * q[c, LEN - 2 : LEN - 1, :]


def section_kernel(last, q, first, metric, one, two, three, mate, even_in, odd_in, meta, *rest):
    if last:
        out, low_ref, high_ref, ghost_ref = rest
    else:
        out, joint_ref, even_ref, odd_ref, low_ref, high_ref, ghost_ref = rest
    choice = meta[3]
    for n, ref in enumerate((mate, one, two, three)):

        @pl.when(choice == n)
        def _(ref=ref):
            ghost_ref[...] = ref[...]

    face = meta[0]
    chain_ghosts(q, even_in, odd_in, low_ref, high_ref, meta)

    def store(t, values):
        where = slice(128 * t, 128 * t + 128)
        for c in range(4):
            out[c, :, where] = 0.5 * first[c, :, where] + 0.5 * values[c] if last else values[c]

    tile = lambda ref: lambda c, t: ref[c, :, 128 * t : 128 * t + 128]
    section(q, metric, lambda c: ghost_ref[16 * c : 16 * c + 16, :], tile(low_ref), tile(high_ref), face, store)
    if not last:
        write_joint(lambda c, t: out[c, :, 128 * t : 128 * t + 128], joint_ref, face, meta[1], meta[2])
        write_chain(out, even_ref, odd_ref, meta[7])


f32 = functools.partial(jax.ShapeDtypeStruct, dtype=jnp.float32)
PARAMS = pltpu.CompilerParams(vmem_limit_bytes=48 * 1024 * 1024)


def exchange(joint, even, odd, meta):
    one, two, three = (
        lax.ppermute(joint, "seg", [(i, i ^ s) for i in range(SEGS)]) for s in (1, 2, 3)
    )
    from_even = lax.ppermute(even, "blk", [(i, i ^ 1) for i in range(CHAIN)])
    pairs = [(i, i + 1) for i in range(1, CHAIN - 1, 2)]
    from_odd = lax.ppermute(odd, "blk", pairs + [(b, a) for a, b in pairs])
    picked = pl.pallas_call(
        pick_kernel,
        out_shape=f32(joint.shape),
        in_specs=[VMEM] * 4 + [SMEM],
        out_specs=VMEM,
        compiler_params=PARAMS,
    )(joint, one, two, three, meta)
    mate = lax.ppermute(picked, "seg", [(i, i ^ 4) for i in range(SEGS)])
    return one, two, three, mate, from_even, from_odd


def on_device(state, metric, block_map, links):
    q = state.reshape(4, LEN, CELLS)
    geometry = metric.reshape(9, LEN, CELLS)
    links = jnp.transpose(links, (1, 2, 0))
    messages = [f32((64, 128)), f32((8, CELLS)), f32((8, CELLS))]
    joint, even, odd, meta = pl.pallas_call(
        first_kernel,
        out_shape=messages + [jax.ShapeDtypeStruct((8,), jnp.int32)],
        in_specs=[VMEM, SMEM, SMEM],
        out_specs=[VMEM] * 3 + [SMEM],
        compiler_params=PARAMS,
    )(q, block_map, links)
    scratch = [
        pltpu.VMEM((4, 8, CELLS), jnp.float32),
        pltpu.VMEM((4, 8, CELLS), jnp.float32),
        pltpu.VMEM((64, 128), jnp.float32),
    ]
    received = exchange(joint, even, odd, meta)
    q1, joint, even, odd = pl.pallas_call(
        functools.partial(section_kernel, False),
        out_shape=[f32((4, LEN, CELLS))] + messages,
        in_specs=[VMEM] * 9 + [SMEM],
        out_specs=[VMEM] * 4,
        scratch_shapes=scratch,
        compiler_params=PARAMS,
    )(q, q, geometry, *received, meta)
    received = exchange(joint, even, odd, meta)
    advanced = pl.pallas_call(
        functools.partial(section_kernel, True),
        out_shape=f32((4, LEN, CELLS)),
        in_specs=[VMEM] * 9 + [SMEM],
        out_specs=VMEM,
        scratch_shapes=scratch,
        compiler_params=PARAMS,
    )(q1, q, geometry, *received, meta)
    return advanced.reshape(state.shape)


def solution(mesh):
    in_specs = (P(("seg", "blk"), None, None, None), P(("seg", "blk"), None, None, None), P(), P())
    out_specs = P(("seg", "blk"), None, None, None)
    return jax.shard_map(
        on_device, mesh=mesh, in_specs=in_specs, out_specs=out_specs, check_vma=False
    )
```

time: 227 us -> 51.1 us (0.23)
  the two profiles are of different devices: /device:TPU:105 before, /device:TPU:184 now
where the time goes in v1:
time: 51.1 us; the launch traced here: 50.8 us
  starting transfers between devices  17.2 us (34%)
  waiting for transfers between devices  15.8 us (31%)
  Pallas kernels  12.8 us (25%)
  local copies, waits for them, and re-layouts  4.87 us (10%)
    ppermute x2, waiting for transfers between devices, exchange(): mate = lax.ppermute(picked, 'seg', [(i, i ^ 4) for i in range(SEGS)])  8.67 us
    ppermute x6, starting transfers between devices, exchange(): lax.ppermute(joint, 'seg', [(i, i ^ s) for i in range(SEGS)])  8.36 us
    ppermute x6, waiting for transfers between devices, exchange(): lax.ppermute(joint, 'seg', [(i, i ^ s) for i in range(SEGS)])  7.13 us
    ppermute x2, starting transfers between devices, exchange(): from_odd = lax.ppermute(odd, 'blk', pairs + [(b, a) for a, b in pairs])  6.33 us
    pallas_call x1, Pallas kernels, on_device(): pl.pallas_call(functools.partial(section_kernel, True), out_shape=f32((4,...  5.14 us
    unnamed x14, local copies, waits for them, and re-layouts  4.87 us
    pallas_call x1, Pallas kernels, on_device(): pl.pallas_call(functools.partial(section_kernel, False), out_shape=[f32((...  4.54 us
    ppermute x2, starting transfers between devices, exchange(): mate = lax.ppermute(picked, 'seg', [(i, i ^ 4) for i in range(SEGS)])  2.34 us
  transfers between devices with their start and end apart: 12, of which 6 were waited for; matrix products, arithmetic and copies ran while one was open for 0% of the time, Pallas kernels for 2%

profile of v1, /device:TPU:184, one launch (start us, length us, event | category | flops | bytes accessed | tf_op | source)
XLA Modules:
  0.0 50.8 jit_solution(108550397185359496)
XLA Ops:
  0.0 0.0 copy-start
  0.0 1.1 %copy-done = f32[1,4,16,2304]{3,2,1,0:T(8,128)S(1)} copy-done((f32[1,4,16,2304]{3,2,1,0:T(8,128)S(1)}, f32[1,4,16,2304]{3,2,1,0:T(8,128)}, u32[]{:S(2)}) %copy-start) | copy-done | bytes 589848
  1.1 0.0 copy-start.5
  1.1 0.7 %copy-done.5 = s32[256,6,4]{0,2,1:T(4,128)S(1)} copy-done((s32[256,6,4]{0,2,1:T(4,128)S(1)}, s32[256,6,4]{0,2,1:T(4,128)}, u32[]{:S(2)}) %copy-start.5) | copy-done | bytes 24600
  1.8 0.0 copy-start.6
  1.8 0.7 %copy-done.6 = s32[256]{0:T(256)S(1)} copy-done((s32[256]{0:T(256)S(1)}, s32[256]{0:T(256)}, u32[]{:S(2)}) %copy-start.6) | copy-done | bytes 1048
  2.5 2.0 %shard_map.46 = (f32[64,128]{1,0:T(8,128)S(1)}, f32[8,2304]{1,0:T(8,128)S(1)}, f32[8,2304]{1,0:T(8,128)S(1)}, s32[8]{0:T(128)S(1)}) custom-call(f32[4,16,2304]{2,1,0:T(8,128)S(1)} %bitcast.4, s32[256]{0:T(256)S(1)} %copy-done.6, s32[6,4,256]{2,1,0:T(4,128)S(1)} %bitcast.10), custom_call_target="tpu_custom_call" | custom-call | tf_op jit(solution)/shard_map/pallas_call | solution.py:280
  4.5 0.1 collective-permute-start.4
  4.6 2.7 %collective-permute-start.5 = (f32[8,2304]{1,0:T(8,128)S(1)}, f32[8,2304]{1,0:T(8,128)S(1)}, u32[]{:S(2)}, u32[]{:S(2)}) collective-permute-start(f32[8,2304]{1,0:T(8,128)S(1)} %get-tuple-element.16), channel_id=1, source_target_pairs={{1,2},{3,4},{5,6},{7,8},{9,10},{11,12},{13,14},{15,16},{17,18},{19... | collective-permute-start | bytes 221192 | tf_op jit(solution)/shard_map/ppermute | solution.py:263
  7.3 2.8 %collective-permute-start.2 = (f32[64,128]{1,0:T(8,128)S(1)}, f32[64,128]{1,0:T(8,128)S(1)}, u32[]{:S(2)}, u32[]{:S(2)}) collective-permute-start(f32[64,128]{1,0:T(8,128)S(1)} %get-tuple-element.13.own), channel_id=1, source_target_pairs={{0,96},{32,64},{64,32},{96,0},{128,224},{160,192},{192,160},{224,1... | collective-permute-start | bytes 98312 | tf_op jit(solution)/shard_map/ppermute | solution.py:259
  10.2 0.8 %collective-permute-start.1 = (f32[64,128]{1,0:T(8,128)S(1)}, f32[64,128]{1,0:T(8,128)S(1)}, u32[]{:S(2)}, u32[]{:S(2)}) collective-permute-start(f32[64,128]{1,0:T(8,128)S(1)} %get-tuple-element.13.own), channel_id=1, source_target_pairs={{0,64},{32,96},{64,0},{96,32},{128,192},{160,224},{192,128},{224,1... | collective-permute-start | bytes 98312 | tf_op jit(solution)/shard_map/ppermute | solution.py:259
  11.0 0.5 %collective-permute-start = (f32[64,128]{1,0:T(8,128)S(1)}, f32[64,128]{1,0:T(8,128)S(1)}, u32[]{:S(2)}, u32[]{:S(2)}) collective-permute-start(f32[64,128]{1,0:T(8,128)S(1)} %get-tuple-element.13.own), channel_id=1, source_target_pairs={{0,32},{32,0},{64,96},{96,64},{128,160},{160,128},{192,224},{224,1... | collective-permute-start | bytes 98312 | tf_op jit(solution)/shard_map/ppermute | solution.py:259
  11.5 1.0 %collective-permute-done.2.three = f32[64,128]{1,0:T(8,128)S(1)} collective-permute-done((f32[64,128]{1,0:T(8,128)S(1)}, f32[64,128]{1,0:T(8,128)S(1)}, u32[]{:S(2)}, u32[]{:S(2)}) %collective-permute-start.2) | collective-permute-done | bytes 32800 | tf_op jit(solution)/shard_map/ppermute | solution.py:259
  12.5 3.2 %collective-permute-done.1.two = f32[64,128]{1,0:T(8,128)S(1)} collective-permute-done((f32[64,128]{1,0:T(8,128)S(1)}, f32[64,128]{1,0:T(8,128)S(1)}, u32[]{:S(2)}, u32[]{:S(2)}) %collective-permute-start.1) | collective-permute-done | bytes 32800 | tf_op jit(solution)/shard_map/ppermute | solution.py:259
  15.7 0.0 collective-permute-done.one
  15.7 0.6 %shard_map.47 = f32[64,128]{1,0:T(8,128)S(1)} custom-call(f32[64,128]{1,0:T(8,128)S(1)} %get-tuple-element.13.own, f32[64,128]{1,0:T(8,128)S(1)} %collective-permute-done.one, f32[64,128]{1,0:T(8,128)S(1)} %collective-permute-done.1.two, f32[64,128]{1,0:T(8,128)S(1)} %collective-permute-done.2.three, s32[8]{0:T(128)S(1)} %get-tuple-element.14.meta), custom_call_target="tpu_custom_call" | custom-call | tf_op jit(solution)/shard_map/pallas_call | solution.py:264
  16.3 1.0 %collective-permute-start.3 = (f32[64,128]{1,0:T(8,128)S(1)}, f32[64,128]{1,0:T(8,128)S(1)}, u32[]{:S(2)}, u32[]{:S(2)}) collective-permute-start(f32[64,128]{1,0:T(8,128)S(1)} %shard_map.47), channel_id=1, source_target_pairs={{0,128},{32,160},{64,192},{96,224},{128,0},{160,32},{192,64},{224,... | collective-permute-start | bytes 98312 | tf_op jit(solution)/shard_map/ppermute | solution.py:271
  17.3 4.5 %collective-permute-done.3.mate = f32[64,128]{1,0:T(8,128)S(1)} collective-permute-done((f32[64,128]{1,0:T(8,128)S(1)}, f32[64,128]{1,0:T(8,128)S(1)}, u32[]{:S(2)}, u32[]{:S(2)}) %collective-permute-start.3) | collective-permute-done | bytes 32800 | tf_op jit(solution)/shard_map/ppermute | solution.py:271
  21.8 0.0 collective-permute-done.4.even_in
  21.8 0.0 collective-permute-done.5.odd_in
  21.8 0.0 copy-start.1
  21.8 1.1 %copy-done.1 = f32[1,4,16,2304]{3,2,1,0:T(8,128)S(1)} copy-done((f32[1,4,16,2304]{3,2,1,0:T(8,128)S(1)}, f32[1,4,16,2304]{3,2,1,0:T(8,128)}, u32[]{:S(2)}) %copy-start.1) | copy-done | bytes 589848
  22.9 0.0 copy-start.3
  22.9 1.3 %copy-done.3 = f32[1,9,16,2304]{3,2,1,0:T(8,128)S(1)} copy-done((f32[1,9,16,2304]{3,2,1,0:T(8,128)S(1)}, f32[1,9,16,2304]{3,2,1,0:T(8,128)}, u32[]{:S(2)}) %copy-start.3) | copy-done | bytes 1327128
  24.2 0.0 copy-start.2
  24.2 0.0 copy-start.4
  24.2 4.5 %shard_map.48 = (f32[4,16,2304]{2,1,0:T(8,128)S(1)}, f32[64,128]{1,0:T(8,128)S(1)}, f32[8,2304]{1,0:T(8,128)S(1)}, f32[8,2304]{1,0:T(8,128)S(1)}) custom-call(f32[4,16,2304]{2,1,0:T(8,128)S(1)} %bitcast.5, f32[4,16,2304]{2,1,0:T(8,128)S(1)} %bitcast.6, f32[9,16,2304]{2,1,0:T(8,128)S(1)} %bitcast.8, f32[64,128]{1,0:T(8,128)S(1)} %collective-permute-done.one, ...), custom_call_target="tpu_custom_call" | custom-call | tf_op jit(solution)/shard_map/pallas_call | solution.py:293
  28.7 0.1 collective-permute-start.10
  28.8 3.6 %collective-permute-start.11 = (f32[8,2304]{1,0:T(8,128)S(1)}, f32[8,2304]{1,0:T(8,128)S(1)}, u32[]{:S(2)}, u32[]{:S(2)}) collective-permute-start(f32[8,2304]{1,0:T(8,128)S(1)} %get-tuple-element.20), channel_id=1, source_target_pairs={{1,2},{3,4},{5,6},{7,8},{9,10},{11,12},{13,14},{15,16},{17,18},{19... | collective-permute-start | bytes 221192 | tf_op jit(solution)/shard_map/ppermute | solution.py:263
  32.4 1.5 %collective-permute-start.8 = (f32[64,128]{1,0:T(8,128)S(1)}, f32[64,128]{1,0:T(8,128)S(1)}, u32[]{:S(2)}, u32[]{:S(2)}) collective-permute-start(f32[64,128]{1,0:T(8,128)S(1)} %get-tuple-element.18.own), channel_id=1, source_target_pairs={{0,96},{32,64},{64,32},{96,0},{128,224},{160,192},{192,160},{224,1... | collective-permute-start | bytes 98312 | tf_op jit(solution)/shard_map/ppermute | solution.py:259
  33.9 0.9 %collective-permute-start.7 = (f32[64,128]{1,0:T(8,128)S(1)}, f32[64,128]{1,0:T(8,128)S(1)}, u32[]{:S(2)}, u32[]{:S(2)}) collective-permute-start(f32[64,128]{1,0:T(8,128)S(1)} %get-tuple-element.18.own), channel_id=1, source_target_pairs={{0,64},{32,96},{64,0},{96,32},{128,192},{160,224},{192,128},{224,1... | collective-permute-start | bytes 98312 | tf_op jit(solution)/shard_map/ppermute | solution.py:259
  34.8 1.8 %collective-permute-start.6 = (f32[64,128]{1,0:T(8,128)S(1)}, f32[64,128]{1,0:T(8,128)S(1)}, u32[]{:S(2)}, u32[]{:S(2)}) collective-permute-start(f32[64,128]{1,0:T(8,128)S(1)} %get-tuple-element.18.own), channel_id=1, source_target_pairs={{0,32},{32,0},{64,96},{96,64},{128,160},{160,128},{192,224},{224,1... | collective-permute-start | bytes 98312 | tf_op jit(solution)/shard_map/ppermute | solution.py:259
  36.6 1.0 %collective-permute-done.8.three = f32[64,128]{1,0:T(8,128)S(1)} collective-permute-done((f32[64,128]{1,0:T(8,128)S(1)}, f32[64,128]{1,0:T(8,128)S(1)}, u32[]{:S(2)}, u32[]{:S(2)}) %collective-permute-start.8) | collective-permute-done | bytes 32800 | tf_op jit(solution)/shard_map/ppermute | solution.py:259
  37.7 1.9 %collective-permute-done.7.two = f32[64,128]{1,0:T(8,128)S(1)} collective-permute-done((f32[64,128]{1,0:T(8,128)S(1)}, f32[64,128]{1,0:T(8,128)S(1)}, u32[]{:S(2)}, u32[]{:S(2)}) %collective-permute-start.7) | collective-permute-done | bytes 32800 | tf_op jit(solution)/shard_map/ppermute | solution.py:259
  39.5 0.0 collective-permute-done.6.one
  39.5 0.6 %shard_map.49 = f32[64,128]{1,0:T(8,128)S(1)} custom-call(f32[64,128]{1,0:T(8,128)S(1)} %get-tuple-element.18.own, f32[64,128]{1,0:T(8,128)S(1)} %collective-permute-done.6.one, f32[64,128]{1,0:T(8,128)S(1)} %collective-permute-done.7.two, f32[64,128]{1,0:T(8,128)S(1)} %collective-permute-done.8.three, s32[8]{0:T(128)S(1)} %get-tuple-element.14.meta), custom_call_target="tpu_custom_call" | custom-call | tf_op jit(solution)/shard_map/pallas_call | solution.py:264
  40.1 1.3 %collective-permute-start.9 = (f32[64,128]{1,0:T(8,128)S(1)}, f32[64,128]{1,0:T(8,128)S(1)}, u32[]{:S(2)}, u32[]{:S(2)}) collective-permute-start(f32[64,128]{1,0:T(8,128)S(1)} %shard_map.49), channel_id=1, source_target_pairs={{0,128},{32,160},{64,192},{96,224},{128,0},{160,32},{192,64},{224,... | collective-permute-start | bytes 98312 | tf_op jit(solution)/shard_map/ppermute | solution.py:271
  41.4 4.2 %collective-permute-done.9.mate = f32[64,128]{1,0:T(8,128)S(1)} collective-permute-done((f32[64,128]{1,0:T(8,128)S(1)}, f32[64,128]{1,0:T(8,128)S(1)}, u32[]{:S(2)}, u32[]{:S(2)}) %collective-permute-start.9) | collective-permute-done | bytes 32800 | tf_op jit(solution)/shard_map/ppermute | solution.py:271
  45.6 0.0 collective-permute-done.10.even_in
  45.6 0.0 collective-permute-done.11.odd_in
  45.6 0.0 copy-done.2
  45.6 0.0 copy-done.4
  45.6 5.1 %shard_map.50 = f32[4,16,2304]{2,1,0:T(8,128)} custom-call(f32[4,16,2304]{2,1,0:T(8,128)S(1)} %get-tuple-element.17.q, f32[4,16,2304]{2,1,0:T(8,128)S(1)} %bitcast.7, f32[9,16,2304]{2,1,0:T(8,128)S(1)} %bitcast.9, f32[64,128]{1,0:T(8,128)S(1)} %collective-permute-done.6.one, f32[64,128]{1,0:T(8,128)S(1)} %collective-permute-done.7.two, ...), custom_call_target="tpu_custom_call" | custom-call | tf_op jit(solution)/shard_map/pallas_call | solution.py:302
Async XLA Ops:
  0.0 1.1 %copy-start = (f32[1,4,16,2304]{3,2,1,0:T(8,128)S(1)}, f32[1,4,16,2304]{3,2,1,0:T(8,128)}, u32[]{:S(2)}) copy-start(f32[1,4,16,2304]{3,2,1,0:T(8,128)} %param.4) | copy-start | bytes 1769476
  1.1 0.7 %copy-start.5 = (s32[256,6,4]{0,2,1:T(4,128)S(1)}, s32[256,6,4]{0,2,1:T(4,128)}, u32[]{:S(2)}) copy-start(s32[256,6,4]{0,2,1:T(4,128)} %param.7) | copy-start | bytes 73732
  1.8 0.7 %copy-start.6 = (s32[256]{0:T(256)S(1)}, s32[256]{0:T(256)}, u32[]{:S(2)}) copy-start(s32[256]{0:T(256)} %block_map.1) | copy-start | bytes 3076
  4.5 17.3 %collective-permute-start.4 = (f32[8,2304]{1,0:T(8,128)S(1)}, f32[8,2304]{1,0:T(8,128)S(1)}, u32[]{:S(2)}, u32[]{:S(2)}) collective-permute-start(f32[8,2304]{1,0:T(8,128)S(1)} %get-tuple-element.15), channel_id=1, source_target_pairs={{0,1},{1,0},{2,3},{3,2},{4,5},{5,4},{6,7},{7,6},{8,9},{9,8},{10,11... | collective-permute-start | bytes 221192 | tf_op jit(solution)/shard_map/ppermute | solution.py:261
  4.6 17.2 %collective-permute-start.5 = (f32[8,2304]{1,0:T(8,128)S(1)}, f32[8,2304]{1,0:T(8,128)S(1)}, u32[]{:S(2)}, u32[]{:S(2)}) collective-permute-start(f32[8,2304]{1,0:T(8,128)S(1)} %get-tuple-element.16), channel_id=1, source_target_pairs={{1,2},{3,4},{5,6},{7,8},{9,10},{11,12},{13,14},{15,16},{17,18},{19... | collective-permute-start | bytes 221192 | tf_op jit(solution)/shard_map/ppermute | solution.py:263
  7.3 5.2 %collective-permute-start.2 = (f32[64,128]{1,0:T(8,128)S(1)}, f32[64,128]{1,0:T(8,128)S(1)}, u32[]{:S(2)}, u32[]{:S(2)}) collective-permute-start(f32[64,128]{1,0:T(8,128)S(1)} %get-tuple-element.13.own), channel_id=1, source_target_pairs={{0,96},{32,64},{64,32},{96,0},{128,224},{160,192},{192,160},{224,1... | collective-permute-start | bytes 98312 | tf_op jit(solution)/shard_map/ppermute | solution.py:259
  10.2 5.6 %collective-permute-start.1 = (f32[64,128]{1,0:T(8,128)S(1)}, f32[64,128]{1,0:T(8,128)S(1)}, u32[]{:S(2)}, u32[]{:S(2)}) collective-permute-start(f32[64,128]{1,0:T(8,128)S(1)} %get-tuple-element.13.own), channel_id=1, source_target_pairs={{0,64},{32,96},{64,0},{96,32},{128,192},{160,224},{192,128},{224,1... | collective-permute-start | bytes 98312 | tf_op jit(solution)/shard_map/ppermute | solution.py:259
  11.0 4.8 %collective-permute-start = (f32[64,128]{1,0:T(8,128)S(1)}, f32[64,128]{1,0:T(8,128)S(1)}, u32[]{:S(2)}, u32[]{:S(2)}) collective-permute-start(f32[64,128]{1,0:T(8,128)S(1)} %get-tuple-element.13.own), channel_id=1, source_target_pairs={{0,32},{32,0},{64,96},{96,64},{128,160},{160,128},{192,224},{224,1... | collective-permute-start | bytes 98312 | tf_op jit(solution)/shard_map/ppermute | solution.py:259
  16.3 5.5 %collective-permute-start.3 = (f32[64,128]{1,0:T(8,128)S(1)}, f32[64,128]{1,0:T(8,128)S(1)}, u32[]{:S(2)}, u32[]{:S(2)}) collective-permute-start(f32[64,128]{1,0:T(8,128)S(1)} %shard_map.47), channel_id=1, source_target_pairs={{0,128},{32,160},{64,192},{96,224},{128,0},{160,32},{192,64},{224,... | collective-permute-start | bytes 98312 | tf_op jit(solution)/shard_map/ppermute | solution.py:271
  21.8 1.1 %copy-start.1 = (f32[1,4,16,2304]{3,2,1,0:T(8,128)S(1)}, f32[1,4,16,2304]{3,2,1,0:T(8,128)}, u32[]{:S(2)}) copy-start(f32[1,4,16,2304]{3,2,1,0:T(8,128)} %param.4) | copy-start | bytes 1769476
  22.9 1.3 %copy-start.3 = (f32[1,9,16,2304]{3,2,1,0:T(8,128)S(1)}, f32[1,9,16,2304]{3,2,1,0:T(8,128)}, u32[]{:S(2)}) copy-start(f32[1,9,16,2304]{3,2,1,0:T(8,128)} %param.5) | copy-start | bytes 3981316
  24.2 21.4 %copy-start.2 = (f32[1,4,16,2304]{3,2,1,0:T(8,128)S(1)}, f32[1,4,16,2304]{3,2,1,0:T(8,128)}, u32[]{:S(2)}) copy-start(f32[1,4,16,2304]{3,2,1,0:T(8,128)} %param.4) | copy-start | bytes 1769476
  24.2 21.4 %copy-start.4 = (f32[1,9,16,2304]{3,2,1,0:T(8,128)S(1)}, f32[1,9,16,2304]{3,2,1,0:T(8,128)}, u32[]{:S(2)}) copy-start(f32[1,9,16,2304]{3,2,1,0:T(8,128)} %param.5) | copy-start | bytes 3981316
  28.7 16.9 %collective-permute-start.10 = (f32[8,2304]{1,0:T(8,128)S(1)}, f32[8,2304]{1,0:T(8,128)S(1)}, u32[]{:S(2)}, u32[]{:S(2)}) collective-permute-start(f32[8,2304]{1,0:T(8,128)S(1)} %get-tuple-element.19), channel_id=1, source_target_pairs={{0,1},{1,0},{2,3},{3,2},{4,5},{5,4},{6,7},{7,6},{8,9},{9,8},{10,11... | collective-permute-start | bytes 221192 | tf_op jit(solution)/shard_map/ppermute | solution.py:261
  28.8 16.8 %collective-permute-start.11 = (f32[8,2304]{1,0:T(8,128)S(1)}, f32[8,2304]{1,0:T(8,128)S(1)}, u32[]{:S(2)}, u32[]{:S(2)}) collective-permute-start(f32[8,2304]{1,0:T(8,128)S(1)} %get-tuple-element.20), channel_id=1, source_target_pairs={{1,2},{3,4},{5,6},{7,8},{9,10},{11,12},{13,14},{15,16},{17,18},{19... | collective-permute-start | bytes 221192 | tf_op jit(solution)/shard_map/ppermute | solution.py:263
  32.4 5.2 %collective-permute-start.8 = (f32[64,128]{1,0:T(8,128)S(1)}, f32[64,128]{1,0:T(8,128)S(1)}, u32[]{:S(2)}, u32[]{:S(2)}) collective-permute-start(f32[64,128]{1,0:T(8,128)S(1)} %get-tuple-element.18.own), channel_id=1, source_target_pairs={{0,96},{32,64},{64,32},{96,0},{128,224},{160,192},{192,160},{224,1... | collective-permute-start | bytes 98312 | tf_op jit(solution)/shard_map/ppermute | solution.py:259
  33.9 5.6 %collective-permute-start.7 = (f32[64,128]{1,0:T(8,128)S(1)}, f32[64,128]{1,0:T(8,128)S(1)}, u32[]{:S(2)}, u32[]{:S(2)}) collective-permute-start(f32[64,128]{1,0:T(8,128)S(1)} %get-tuple-element.18.own), channel_id=1, source_target_pairs={{0,64},{32,96},{64,0},{96,32},{128,192},{160,224},{192,128},{224,1... | collective-permute-start | bytes 98312 | tf_op jit(solution)/shard_map/ppermute | solution.py:259
  34.8 4.7 %collective-permute-start.6 = (f32[64,128]{1,0:T(8,128)S(1)}, f32[64,128]{1,0:T(8,128)S(1)}, u32[]{:S(2)}, u32[]{:S(2)}) collective-permute-start(f32[64,128]{1,0:T(8,128)S(1)} %get-tuple-element.18.own), channel_id=1, source_target_pairs={{0,32},{32,0},{64,96},{96,64},{128,160},{160,128},{192,224},{224,1... | collective-permute-start | bytes 98312 | tf_op jit(solution)/shard_map/ppermute | solution.py:259
  40.1 5.5 %collective-permute-start.9 = (f32[64,128]{1,0:T(8,128)S(1)}, f32[64,128]{1,0:T(8,128)S(1)}, u32[]{:S(2)}, u32[]{:S(2)}) collective-permute-start(f32[64,128]{1,0:T(8,128)S(1)} %shard_map.49), channel_id=1, source_target_pairs={{0,128},{32,160},{64,192},{96,224},{128,0},{160,32},{192,64},{224,... | collective-permute-start | bytes 98312 | tf_op jit(solution)/shard_map/ppermute | solution.py:271

commit v2 on v1

--- a/solution.py
+++ b/solution.py
@@ -7,6 +7,7 @@
 from jax.sharding import PartitionSpec as P
 
 LEN, CROSS, CELLS, TILES = 16, 48, 2304, 18
+HALF = 9
 SEGS, CHAIN = 8, 32
 time_step = 0.05
 viscosity = 0.2
@@ -90,8 +91,18 @@
         odd_ref[2 * c : 2 * c + 2, :] = jnp.where(even, low, high)
 
 
-def first_kernel(q, block_map, links, joint_ref, even_ref, odd_ref, meta):
+def first_kernel(q_hbm, map_hbm, links_hbm, joint_ref, meta, q, block_map, links, sem):
+    copies = [
+        pltpu.make_async_copy(source, target, sem.at[n])
+        for n, (source, target) in enumerate(
+            ((links_hbm, links), (map_hbm, block_map), (q_hbm, q))
+        )
+    ]
+    for copy in copies:
+        copy.start()
     segment, position = lax.axis_index("seg"), lax.axis_index("blk")
+    copies[0].wait()
+    copies[1].wait()
     face, partner, along, across = joined_face(segment * CHAIN + position, block_map, links)
     mate = (segment + 4) % 8
     _, mate_partner, _, _ = joined_face(mate * CHAIN + position, block_map, links)
@@ -104,8 +115,8 @@
     meta[5] = jnp.where(links[0, 0, block] >= 0, 1, 0)
     meta[6] = jnp.where(links[1, 0, block] >= 0, 1, 0)
     meta[7] = position
+    copies[2].wait()
     write_joint(lambda c, t: q[c, :, 128 * t : 128 * t + 128], joint_ref, face, along, across)
-    write_chain(q, even_ref, odd_ref, position)
 
 
 def pick_kernel(own, one, two, three, meta, out):
@@ -158,76 +169,77 @@
     return result
 
 
-def section(q, metric, joint, low, high, face, store):
+def bulk_kernel(last, tiles, q, metric, *rest):
+    first, rest = (rest[0], rest[1:]) if last else (None, rest)
+    meta, out = rest[:2]
+    if len(rest) == 4:
+        write_chain(q, rest[2], rest[3], meta[7])
     lane = lanes_of(LEN)
+    row = lax.broadcasted_iota(jnp.int32, (8, 128), 0)
+    face, ends = meta[0], (meta[5] == 0, meta[6] == 0)
     load = lambda c, t: q[c, :, 128 * t : 128 * t + 128]
-    before_first, after_last, ghosts = [], [], []
+    before_first, after_last = [], []
     for c in range(4):
-        received = joint(c)
-        ghosts.append(received)
-        source = jnp.where(face == 2, received, SIGN[c] * load(c, 0))
-        before_first.append(jnp.where(lane >= 80, pltpu.roll(source, 80, 1), pltpu.roll(source, 112, 1)))
-        last = SIGN[c] * load(c, TILES - 1)
-        wall = jnp.where(lane < CROSS, pltpu.roll(last, 48, 1), pltpu.roll(last, 16, 1))
-        after_last.append(jnp.where(face == 3, received, wall))
+        head = jnp.where(face == 2, 0.0, SIGN[c]) * load(c, 0)
+        before_first.append(jnp.where(lane >= 80, pltpu.roll(head, 80, 1), pltpu.roll(head, 112, 1)))
+        tail = jnp.where(face == 3, 0.0, SIGN[c]) * load(c, TILES - 1)
+        after_last.append(jnp.where(lane < CROSS, pltpu.roll(tail, 48, 1), pltpu.roll(tail, 16, 1)))
 
     def tile(c, t):
         return before_first[c] if t < 0 else after_last[c] if t >= TILES else load(c, t)
 
-    for t in range(TILES):
+    low_scale = jnp.where(face == 4, 0.0, 1.0)
+    high_scale = jnp.where(face == 5, 0.0, 1.0)
+    open_low = jnp.where(ends[0], 1.0, 0.0)
+    open_high = jnp.where(ends[1], 1.0, 0.0)
+    for t in tiles:
         flat = 128 * t + lane
-        j = flat // CROSS
-        k = flat - j * CROSS
-        joined = ((face == 4) & (k < 2)) | ((face == 5) & (k >= 46))
-        near = j[:8]
-        far = jnp.where((k == 0) | (k == 47), j + CROSS, j)[:8]
+        k = flat - (flat // CROSS) * CROSS
+        scale = jnp.where(k < 2, low_scale, high_scale)
         stencils = []
         for c in range(4):
             before, here, after = tile(c, t - 1), tile(c, t), tile(c, t + 1)
-            rows = jnp.concatenate([low(c, t), here, high(c, t)], axis=0)
+            top, bottom = here[0:8], here[8:16]
+            low = -SIGN[c] * open_low * jnp.where(row == 7, pltpu.roll(top, 7, 0), pltpu.roll(top, 5, 0))
+            high = -SIGN[c] * open_high * jnp.where(row == 0, pltpu.roll(bottom, 1, 0), pltpu.roll(bottom, 3, 0))
+            rows = jnp.concatenate([low, here, high], axis=0)
             along_i = [shifted_rows(rows, s) for s in (-2, -1)] + [here] + [shifted_rows(rows, s) for s in (1, 2)]
             along_j = [shifted_lanes(before, here, after, CROSS * s) if s else here for s in range(-2, 3)]
             raw = [shifted_lanes(before, here, after, s) if s else here for s in range(-2, 3)]
-            first = jnp.where(joined, gather_lanes(ghosts[c], near), SIGN[c] * here)
-            wall = SIGN[c] * jnp.where((k == 0) | (k == 46), raw[3], raw[1])
-            second = jnp.where(joined, gather_lanes(ghosts[c], far), wall)
+            factor = SIGN[c] * scale
+            nearest = factor * here
+            second = factor * jnp.where((k == 0) | (k == 46), raw[3], raw[1])
             along_k = [
                 jnp.where(k < 2, second, raw[0]),
-                jnp.where(k == 0, first, raw[1]),
+                jnp.where(k == 0, nearest, raw[1]),
                 here,
-                jnp.where(k == 47, first, raw[3]),
+                jnp.where(k == 47, nearest, raw[3]),
                 jnp.where(k >= 46, second, raw[4]),
             ]
             stencils.append((along_i, along_j, along_k))
-        store(t, advance(stencils, [metric[n, :, 128 * t : 128 * t + 128] for n in range(9)]))
-
-
-def chain_ghosts(q, even_ref, odd_ref, low_ref, high_ref, meta):
-    even = lax.rem(meta[7], 2) == 0
-    has_low, has_high = meta[5] == 1, meta[6] == 1
-    for c in range(4):
-        rows = slice(2 * c, 2 * c + 2)
-        from_even, from_odd = even_ref[rows, :], odd_ref[rows, :]
-        mirror = -SIGN[c]
-        low_ref[c, 6:8, :] = jnp.where(even, from_odd, from_even)
-        high_ref[c, 0:2, :] = jnp.where(even, from_even, from_odd)
-
-        @pl.when(jnp.logical_not(has_low))
-        def _():
-            low_ref[c, 7:8, :] = mirror * q[c, 0:1, :]
-            low_ref[c, 6:7, :] = mirror * q[c, 1:2, :]
-
-        @pl.when(jnp.logical_not(has_high))
-        def _():
-            high_ref[c, 0:1, :] = mirror * q[c, LEN - 1 : LEN, :]
-            high_ref[c, 1:2, :] = mirror * q[c, LEN - 2 : LEN - 1, :]
-
-
-def section_kernel(last, q, first, metric, one, two, three, mate, even_in, odd_in, meta, *rest):
+        where = slice(128 * t, 128 * t + 128)
+        values = advance(stencils, [metric[n, :, where] for n in range(9)])
+        for c in range(4):
+            kept = 0.5 * first[c, :, where] + 0.5 * values[c] if last else values[c]
+            out[c, :, 128 * (t - tiles[0]) : 128 * (t - tiles[0]) + 128] = kept
+
+
+def edge_terms(here, geometry, slopes, curves, scale):
+    moves = [-(scale * time_step / 12.0) * g for g in geometry]
+    speed = moves[0] * here[0] + moves[1] * here[1] + moves[2] * here[2]
+    squares = geometry[0] * geometry[0] + geometry[1] * geometry[1] + geometry[2] * geometry[2]
+    spread = (scale * viscosity * time_step / 12.0) * squares
+    added = [speed * slopes[b] + moves[b] * slopes[3] + spread * curves[b] for b in range(3)]
+    added.append(compress * (moves[0] * slopes[0] + moves[1] * slopes[1] + moves[2] * slopes[2]))
+    return added
+
+
+def edge_kernel(last, left, right, q, metric, one, two, three, mate, even_in, odd_in, meta, *rest):
     if last:
         out, low_ref, high_ref, ghost_ref = rest
     else:
-        out, joint_ref, even_ref, odd_ref, low_ref, high_ref, ghost_ref = rest
+        out, joint_ref, low_ref, high_ref, ghost_ref = rest
+    scale = 0.5 if last else 1.0
     choice = meta[3]
     for n, ref in enumerate((mate, one, two, three)):
 
@@ -236,77 +248,169 @@
             ghost_ref[...] = ref[...]
 
     face = meta[0]
-    chain_ghosts(q, even_in, odd_in, low_ref, high_ref, meta)
-
-    def store(t, values):
+    even = lax.rem(meta[7], 2) == 0
+    has_low = jnp.where(meta[5] == 1, 1.0, 0.0)
+    has_high = jnp.where(meta[6] == 1, 1.0, 0.0)
+    for c in range(4):
+        rows = slice(2 * c, 2 * c + 2)
+        from_even, from_odd = even_in[rows, :], odd_in[rows, :]
+        low_ref[c, 0:2, :] = has_low * jnp.where(even, from_odd, from_even)
+        high_ref[c, 6:8, :] = has_high * jnp.where(even, from_even, from_odd)
+
+    row = lax.broadcasted_iota(jnp.int32, (8, 128), 0)
+    for t in range(TILES):
         where = slice(128 * t, 128 * t + 128)
+        part, place = (left, where) if t < HALF else (right, slice(128 * (t - HALF), 128 * (t - HALF) + 128))
+        for high in (False, True):
+            half = slice(8, 16) if high else slice(0, 8)
+            slopes, curves = [], []
+            for c in range(4):
+                if high:
+                    ghost = high_ref[c, :, where]
+                    first = jnp.where(row == 7, pltpu.roll(ghost, 1, 0), 0.0)
+                    second = jnp.where(row >= 6, ghost, 0.0)
+                    slopes.append(8.0 * first - second)
+                else:
+                    ghost = low_ref[c, :, where]
+                    first = jnp.where(row == 0, pltpu.roll(ghost, 7, 0), 0.0)
+                    second = jnp.where(row < 2, ghost, 0.0)
+                    slopes.append(second - 8.0 * first)
+                curves.append(16.0 * first - second)
+            here = [q[c, half, where] for c in range(4)]
+            added = edge_terms(here, [metric[n, half, where] for n in range(3)], slopes, curves, scale)
+            for c in range(4):
+                out[c, half, where] = part[c, half, place] + added[c]
+
+    lane = lanes_of(LEN)
+
+    def add(t, direction, slopes, curves):
+        where = slice(128 * t, 128 * t + 128)
+        here = [q[c, :, where] for c in range(4)]
+        geometry = [metric[3 * direction + n, :, where] for n in range(3)]
+        added = edge_terms(here, geometry, slopes, curves, scale)
         for c in range(4):
-            out[c, :, where] = 0.5 * first[c, :, where] + 0.5 * values[c] if last else values[c]
-
-    tile = lambda ref: lambda c, t: ref[c, :, 128 * t : 128 * t + 128]
-    section(q, metric, lambda c: ghost_ref[16 * c : 16 * c + 16, :], tile(low_ref), tile(high_ref), face, store)
+            out[c, :, where] = out[c, :, where] + added[c]
+
+    ghost_of = lambda c: ghost_ref[16 * c : 16 * c + 16, :]
+
+    @pl.when(face == 2)
+    def _():
+        slopes, curves = [], []
+        for c in range(4):
+            ghost = ghost_of(c)
+            first = jnp.where(lane < CROSS, ghost, 0.0)
+            second = jnp.where(lane < CROSS, pltpu.roll(ghost, 80, 1), pltpu.roll(ghost, 48, 1))
+            second = jnp.where(lane < 2 * CROSS, second, 0.0)
+            slopes.append(second - 8.0 * first)
+            curves.append(16.0 * first - second)
+        add(0, 1, slopes, curves)
+
+    @pl.when(face == 3)
+    def _():
+        slopes, curves = [], []
+        for c in range(4):
+            ghost = ghost_of(c)
+            first = jnp.where(lane >= 80, pltpu.roll(ghost, 80, 1), 0.0)
+            second = jnp.where(lane >= 32, pltpu.roll(ghost, 32, 1), 0.0)
+            slopes.append(8.0 * first - second)
+            curves.append(16.0 * first - second)
+        add(TILES - 1, 1, slopes, curves)
+
+    @pl.when(face >= 4)
+    def _():
+        toward = jnp.where(face == 4, -1.0, 1.0)
+        for t in range(TILES):
+            flat = 128 * t + lane
+            j = flat // CROSS
+            k = flat - j * CROSS
+            depth = jnp.where(face == 4, k, CROSS - 1 - k)
+            far = jnp.where(depth == 0, j + CROSS, j)[:8]
+            slopes, curves = [], []
+            for c in range(4):
+                ghost = ghost_of(c)
+                first = jnp.where(depth == 0, gather_lanes(ghost, j[:8]), 0.0)
+                second = jnp.where(depth < 2, gather_lanes(ghost, far), 0.0)
+                slopes.append(toward * (8.0 * first - second))
+                curves.append(16.0 * first - second)
+            add(t, 2, slopes, curves)
+
     if not last:
         write_joint(lambda c, t: out[c, :, 128 * t : 128 * t + 128], joint_ref, face, meta[1], meta[2])
-        write_chain(out, even_ref, odd_ref, meta[7])
 
 
 f32 = functools.partial(jax.ShapeDtypeStruct, dtype=jnp.float32)
-PARAMS = pltpu.CompilerParams(vmem_limit_bytes=48 * 1024 * 1024)
-
-
-def exchange(joint, even, odd, meta):
+PARAMS = pltpu.CompilerParams(vmem_limit_bytes=24 * 1024 * 1024)
+WHOLE = pltpu.CompilerParams(vmem_limit_bytes=61 * 1024 * 1024)
+FIELD = f32((4, LEN, CELLS))
+JOINT = f32((64, 128))
+CHAINS = [f32((8, CELLS))] * 2
+HALO = [pltpu.VMEM((4, 8, CELLS), jnp.float32)] * 2 + [pltpu.VMEM((64, 128), jnp.float32)]
+
+
+def bulk(last, tiles, *operands):
+    shapes = [f32((4, LEN, 128 * len(tiles)))] + (CHAINS if tiles[0] == 0 else [])
+    return pl.pallas_call(
+        functools.partial(bulk_kernel, last, tiles),
+        out_shape=shapes,
+        in_specs=[VMEM] * (len(operands) - 1) + [SMEM],
+        out_specs=[VMEM] * len(shapes),
+        compiler_params=PARAMS,
+        cost_estimate=pl.CostEstimate(flops=6_000_000, bytes_accessed=6_000_000, transcendentals=0),
+    )(*operands)
+
+
+def edges(last, *operands):
+    shapes = [FIELD] + ([] if last else [JOINT])
+    return pl.pallas_call(
+        functools.partial(edge_kernel, last),
+        out_shape=shapes,
+        in_specs=[VMEM] * (len(operands) - 1) + [SMEM],
+        out_specs=[VMEM] * len(shapes),
+        scratch_shapes=HALO,
+        compiler_params=PARAMS,
+    )(*operands)
+
+
+def section(last, q, geometry, joint, first, meta):
+    kept = [first] if last else []
     one, two, three = (
         lax.ppermute(joint, "seg", [(i, i ^ s) for i in range(SEGS)]) for s in (1, 2, 3)
     )
+    left, even, odd = bulk(last, range(HALF), q, geometry, *kept, meta)
+    one, two, three, even, odd = lax.optimization_barrier((one, two, three, even, odd))
     from_even = lax.ppermute(even, "blk", [(i, i ^ 1) for i in range(CHAIN)])
     pairs = [(i, i + 1) for i in range(1, CHAIN - 1, 2)]
     from_odd = lax.ppermute(odd, "blk", pairs + [(b, a) for a, b in pairs])
     picked = pl.pallas_call(
         pick_kernel,
-        out_shape=f32(joint.shape),
+        out_shape=JOINT,
         in_specs=[VMEM] * 4 + [SMEM],
         out_specs=VMEM,
         compiler_params=PARAMS,
     )(joint, one, two, three, meta)
     mate = lax.ppermute(picked, "seg", [(i, i ^ 4) for i in range(SEGS)])
-    return one, two, three, mate, from_even, from_odd
+    (right,) = bulk(last, range(HALF, TILES), q, geometry, *kept, meta)
+    return edges(last, left, right, q, geometry, one, two, three, mate, from_even, from_odd, meta)
 
 
 def on_device(state, metric, block_map, links):
-    q = state.reshape(4, LEN, CELLS)
-    geometry = metric.reshape(9, LEN, CELLS)
-    links = jnp.transpose(links, (1, 2, 0))
-    messages = [f32((64, 128)), f32((8, CELLS)), f32((8, CELLS))]
-    joint, even, odd, meta = pl.pallas_call(
+    HBM = pl.BlockSpec(memory_space=pltpu.HBM)
+    q, geometry = state.reshape(4, LEN, CELLS), metric.reshape(9, LEN, CELLS)
+    joint, meta = pl.pallas_call(
         first_kernel,
-        out_shape=messages + [jax.ShapeDtypeStruct((8,), jnp.int32)],
-        in_specs=[VMEM, SMEM, SMEM],
-        out_specs=[VMEM] * 3 + [SMEM],
-        compiler_params=PARAMS,
-    )(q, block_map, links)
-    scratch = [
-        pltpu.VMEM((4, 8, CELLS), jnp.float32),
-        pltpu.VMEM((4, 8, CELLS), jnp.float32),
-        pltpu.VMEM((64, 128), jnp.float32),
-    ]
-    received = exchange(joint, even, odd, meta)
-    q1, joint, even, odd = pl.pallas_call(
-        functools.partial(section_kernel, False),
-        out_shape=[f32((4, LEN, CELLS))] + messages,
-        in_specs=[VMEM] * 9 + [SMEM],
-        out_specs=[VMEM] * 4,
-        scratch_shapes=scratch,
-        compiler_params=PARAMS,
-    )(q, q, geometry, *received, meta)
-    received = exchange(joint, even, odd, meta)
-    advanced = pl.pallas_call(
-        functools.partial(section_kernel, True),
-        out_shape=f32((4, LEN, CELLS)),
-        in_specs=[VMEM] * 9 + [SMEM],
-        out_specs=VMEM,
-        scratch_shapes=scratch,
-        compiler_params=PARAMS,
-    )(q1, q, geometry, *received, meta)
+        out_shape=[JOINT, jax.ShapeDtypeStruct((8,), jnp.int32)],
+        in_specs=[HBM] * 3,
+        out_specs=[VMEM, SMEM],
+        scratch_shapes=[
+            pltpu.VMEM((4, LEN, CELLS), jnp.float32),
+            pltpu.SMEM((SEGS * CHAIN,), jnp.int32),
+            pltpu.SMEM((6, 4, SEGS * CHAIN), jnp.int32),
+            pltpu.SemaphoreType.DMA((3,)),
+        ],
+        compiler_params=WHOLE,
+    )(q, block_map, jnp.transpose(links, (1, 2, 0)))
+    q1, joint = section(False, q, geometry, joint, None, meta)
+    (advanced,) = section(True, q1, geometry, joint, q, meta)
     return advanced.reshape(state.shape)
 
 

time: 51.1 us -> 44.1 us (0.86)
  the two profiles are of different devices: /device:TPU:184 before, /device:TPU:105 now
where the time goes in v2:
time: 44.1 us; the launch traced here: 44.2 us
  starting transfers between devices  23 us (52%)
  Pallas kernels  14.5 us (33%)
  waiting for transfers between devices  3.55 us (8%)
  local copies, waits for them, and re-layouts  3.01 us (7%)
    ppermute x2, starting transfers between devices, section(): from_odd = lax.ppermute(odd, 'blk', pairs + [(b, a) for a, b in pairs])  11.2 us
    pallas_call x4, Pallas kernels, bulk(): pl.pallas_call(functools.partial(bulk_kernel, last, tiles), out_shape=sha...  7.7 us
    ppermute x6, starting transfers between devices, section(): lax.ppermute(joint, 'seg', [(i, i ^ s) for i in range(SEGS)])  6.68 us
    pallas_call x2, Pallas kernels, edges(): pl.pallas_call(functools.partial(edge_kernel, last), out_shape=shapes, in...  3.31 us
    ppermute x2, starting transfers between devices, section(): mate = lax.ppermute(picked, 'seg', [(i, i ^ 4) for i in range(SEGS)])  3.15 us
    unnamed x12, local copies, waits for them, and re-layouts  3.01 us
    pallas_call x1, Pallas kernels, on_device(): pl.pallas_call(first_kernel, out_shape=[JOINT, jax.ShapeDtypeStruct((8,),...  2.37 us
    ppermute x2, starting transfers between devices, section(): from_even = lax.ppermute(even, 'blk', [(i, i ^ 1) for i in range(CHAIN)])  2 us
  transfers between devices with their start and end apart: 12, of which 3 were waited for; matrix products, arithmetic and copies ran while one was open for 0% of the time, Pallas kernels for 20%

profile of v2, /device:TPU:105, one launch (start us, length us, event | category | flops | bytes accessed | tf_op | source)
XLA Modules:
  0.0 44.2 jit_solution(6080841086709514965)
XLA Ops:
  0.0 0.0 copy-start.3
  0.0 2.4 %shard_map.46 = (f32[64,128]{1,0:T(8,128)}, s32[8]{0:T(128)}) custom-call(f32[4,16,2304]{2,1,0:T(8,128)} %bitcast.10, s32[256]{0:T(256)} %map_hbm.1, s32[6,4,256]{2,1,0:T(4,128)} %bitcast.16), custom_call_target="tpu_custom_call" | custom-call | tf_op jit(solution)/shard_map/pallas_call | solution.py:399
  2.4 2.6 %collective-permute-start.2 = (f32[64,128]{1,0:T(8,128)}, f32[64,128]{1,0:T(8,128)S(1)}, u32[]{:S(2)}, u32[]{:S(2)}) collective-permute-start(f32[64,128]{1,0:T(8,128)} %get-tuple-element.27.own), channel_id=1, source_target_pairs={{0,96},{32,64},{64,32},{96,0},{128,224},{160,192},{192,160},{224,1... | collective-permute-start | bytes 98312 | tf_op jit(solution)/shard_map/ppermute | solution.py:377
  4.9 0.5 %collective-permute-start.1 = (f32[64,128]{1,0:T(8,128)}, f32[64,128]{1,0:T(8,128)S(1)}, u32[]{:S(2)}, u32[]{:S(2)}) collective-permute-start(f32[64,128]{1,0:T(8,128)} %get-tuple-element.27.own), channel_id=1, source_target_pairs={{0,64},{32,96},{64,0},{96,32},{128,192},{160,224},{192,128},{224,1... | collective-permute-start | bytes 98312 | tf_op jit(solution)/shard_map/ppermute | solution.py:377
  5.5 0.3 collective-permute-start
  5.7 0.0 copy-start
  5.7 1.3 %copy-done = f32[1,9,16,2304]{3,2,1,0:T(8,128)S(1)} copy-done((f32[1,9,16,2304]{3,2,1,0:T(8,128)S(1)}, f32[1,9,16,2304]{3,2,1,0:T(8,128)}, u32[]{:S(2)}) %copy-start) | copy-done | bytes 1327128
  7.0 0.0 copy-start.2
  7.0 1.1 %copy-done.2 = f32[1,4,16,2304]{3,2,1,0:T(8,128)S(1)} copy-done((f32[1,4,16,2304]{3,2,1,0:T(8,128)S(1)}, f32[1,4,16,2304]{3,2,1,0:T(8,128)}, u32[]{:S(2)}) %copy-start.2) | copy-done | bytes 589848
  8.1 0.0 copy-start.5
  8.1 0.6 %copy-done.5 = s32[8]{0:T(128)S(1)} copy-done((s32[8]{0:T(128)S(1)}, s32[8]{0:T(128)}, u32[]{:S(2)}) %copy-start.5) | copy-done | bytes 56
  8.7 0.0 copy-start.4
  8.7 1.9 %shard_map.47 = (f32[4,16,1152]{2,1,0:T(8,128)S(1)}, f32[8,2304]{1,0:T(8,128)S(1)}, f32[8,2304]{1,0:T(8,128)S(1)}) custom-call(f32[4,16,2304]{2,1,0:T(8,128)S(1)} %bitcast.11, f32[9,16,2304]{2,1,0:T(8,128)S(1)} %bitcast.4, s32[8]{0:T(128)S(1)} %copy-done.5), custom_call_target="tpu_custom_call" | custom-call | flops 6000000 | bytes 6000000 | tf_op jit(solution)/shard_map/pallas_call | solution.py:352
  10.7 0.0 collective-permute-done.2.three
  10.7 0.0 collective-permute-done.1.two
  10.7 0.0 collective-permute-done.one
  10.7 1.6 %collective-permute-start.4 = (f32[8,2304]{1,0:T(8,128)S(1)}, f32[8,2304]{1,0:T(8,128)S(1)}, u32[]{:S(2)}, u32[]{:S(2)}) collective-permute-start(f32[8,2304]{1,0:T(8,128)S(1)} %get-tuple-element.33), channel_id=1, source_target_pairs={{0,1},{1,0},{2,3},{3,2},{4,5},{5,4},{6,7},{7,6},{8,9},{9,8},{10,11... | collective-permute-start | bytes 221192 | tf_op jit(solution)/shard_map/ppermute | solution.py:381
  12.3 4.5 %collective-permute-start.5 = (f32[8,2304]{1,0:T(8,128)S(1)}, f32[8,2304]{1,0:T(8,128)S(1)}, u32[]{:S(2)}, u32[]{:S(2)}) collective-permute-start(f32[8,2304]{1,0:T(8,128)S(1)} %get-tuple-element.34), channel_id=1, source_target_pairs={{1,2},{3,4},{5,6},{7,8},{9,10},{11,12},{13,14},{15,16},{17,18},{19... | collective-permute-start | bytes 221192 | tf_op jit(solution)/shard_map/ppermute | solution.py:383
  16.8 0.0 copy-done.4
  16.9 0.6 %shard_map.49 = f32[64,128]{1,0:T(8,128)S(1)} custom-call(f32[64,128]{1,0:T(8,128)S(1)} %copy-done.4, f32[64,128]{1,0:T(8,128)S(1)} %collective-permute-done.one, f32[64,128]{1,0:T(8,128)S(1)} %collective-permute-done.1.two, f32[64,128]{1,0:T(8,128)S(1)} %collective-permute-done.2.three, s32[8]{0:T(128)S(1)} %copy-done.5), custom_call_target="tpu_custom_call" | custom-call | tf_op jit(solution)/shard_map/pallas_call | solution.py:384
  17.4 2.4 %collective-permute-start.3 = (f32[64,128]{1,0:T(8,128)S(1)}, f32[64,128]{1,0:T(8,128)S(1)}, u32[]{:S(2)}, u32[]{:S(2)}) collective-permute-start(f32[64,128]{1,0:T(8,128)S(1)} %shard_map.49), channel_id=1, source_target_pairs={{0,128},{32,160},{64,192},{96,224},{128,0},{160,32},{192,64},{224,... | collective-permute-start | bytes 98312 | tf_op jit(solution)/shard_map/ppermute | solution.py:391
  19.8 0.0 copy-done.3
  19.8 1.9 %shard_map.48.right = f32[4,16,1152]{2,1,0:T(8,128)S(1)} custom-call(f32[4,16,2304]{2,1,0:T(8,128)S(1)} %bitcast.12, f32[9,16,2304]{2,1,0:T(8,128)S(1)} %bitcast.5, s32[8]{0:T(128)S(1)} %copy-done.5), custom_call_target="tpu_custom_call" | custom-call | flops 6000000 | bytes 6000000 | tf_op jit(solution)/shard_map/pallas_call | solution.py:352
  21.7 0.1 collective-permute-done.3.mate
  21.8 0.0 collective-permute-done.4.even_in
  21.8 0.0 collective-permute-done.5.odd_in
  21.8 1.5 %shard_map.50 = (f32[4,16,2304]{2,1,0:T(8,128)S(1)}, f32[64,128]{1,0:T(8,128)S(1)}) custom-call(f32[4,16,1152]{2,1,0:T(8,128)S(1)} %get-tuple-element.26.left, f32[4,16,1152]{2,1,0:T(8,128)S(1)} %shard_map.48.right, f32[4,16,2304]{2,1,0:T(8,128)S(1)} %bitcast.13, f32[9,16,2304]{2,1,0:T(8,128)S(1)} %bitcast.6, f32[64,128]{1,0:T(8,128)S(1)} %collective-permute-done.one, ...), custom_call_target="tpu_custom_call" | custom-call | tf_op jit(solution)/shard_map/pallas_call | solution.py:364
  23.2 2.6 %collective-permute-start.8 = (f32[64,128]{1,0:T(8,128)S(1)}, f32[64,128]{1,0:T(8,128)S(1)}, u32[]{:S(2)}, u32[]{:S(2)}) collective-permute-start(f32[64,128]{1,0:T(8,128)S(1)} %get-tuple-element.37.own), channel_id=1, source_target_pairs={{0,96},{32,64},{64,32},{96,0},{128,224},{160,192},{192,160},{224,1... | collective-permute-start | bytes 98312 | tf_op jit(solution)/shard_map/ppermute | solution.py:377
  25.8 0.5 %collective-permute-start.7 = (f32[64,128]{1,0:T(8,128)S(1)}, f32[64,128]{1,0:T(8,128)S(1)}, u32[]{:S(2)}, u32[]{:S(2)}) collective-permute-start(f32[64,128]{1,0:T(8,128)S(1)} %get-tuple-element.37.own), channel_id=1, source_target_pairs={{0,64},{32,96},{64,0},{96,32},{128,192},{160,224},{192,128},{224,1... | collective-permute-start | bytes 98312 | tf_op jit(solution)/shard_map/ppermute | solution.py:377
  26.3 0.3 collective-permute-start.6
  26.6 1.9 %shard_map.51 = (f32[4,16,1152]{2,1,0:T(8,128)S(1)}, f32[8,2304]{1,0:T(8,128)S(1)}, f32[8,2304]{1,0:T(8,128)S(1)}) custom-call(f32[4,16,2304]{2,1,0:T(8,128)S(1)} %get-tuple-element.35.q, f32[9,16,2304]{2,1,0:T(8,128)S(1)} %bitcast.7, f32[4,16,2304]{2,1,0:T(8,128)S(1)} %bitcast.14, s32[8]{0:T(128)S(1)} %copy-done.5), custom_call_target="tpu_custom_call" | custom-call | flops 6000000 | bytes 6000000 | tf_op jit(solution)/shard_map/pallas_call | solution.py:352
  28.5 0.0 collective-permute-done.8.three
  28.6 1.6 %collective-permute-done.7.two = f32[64,128]{1,0:T(8,128)S(1)} collective-permute-done((f32[64,128]{1,0:T(8,128)S(1)}, f32[64,128]{1,0:T(8,128)S(1)}, u32[]{:S(2)}, u32[]{:S(2)}) %collective-permute-start.7) | collective-permute-done | bytes 32800 | tf_op jit(solution)/shard_map/ppermute | solution.py:377
  30.2 0.0 collective-permute-done.6.one
  30.2 0.4 collective-permute-start.10
  30.6 6.6 %collective-permute-start.11 = (f32[8,2304]{1,0:T(8,128)S(1)}, f32[8,2304]{1,0:T(8,128)S(1)}, u32[]{:S(2)}, u32[]{:S(2)}) collective-permute-start(f32[8,2304]{1,0:T(8,128)S(1)} %get-tuple-element.44), channel_id=1, source_target_pairs={{1,2},{3,4},{5,6},{7,8},{9,10},{11,12},{13,14},{15,16},{17,18},{19... | collective-permute-start | bytes 221192 | tf_op jit(solution)/shard_map/ppermute | solution.py:383
  37.2 0.6 %shard_map.53 = f32[64,128]{1,0:T(8,128)S(1)} custom-call(f32[64,128]{1,0:T(8,128)S(1)} %get-tuple-element.37.own, f32[64,128]{1,0:T(8,128)S(1)} %collective-permute-done.6.one, f32[64,128]{1,0:T(8,128)S(1)} %collective-permute-done.7.two, f32[64,128]{1,0:T(8,128)S(1)} %collective-permute-done.8.three, s32[8]{0:T(128)S(1)} %copy-done.5), custom_call_target="tpu_custom_call" | custom-call | tf_op jit(solution)/shard_map/pallas_call | solution.py:384
  37.8 0.0 copy-start.1
  37.8 0.8 %collective-permute-start.9 = (f32[64,128]{1,0:T(8,128)S(1)}, f32[64,128]{1,0:T(8,128)S(1)}, u32[]{:S(2)}, u32[]{:S(2)}) collective-permute-start(f32[64,128]{1,0:T(8,128)S(1)} %shard_map.53), channel_id=1, source_target_pairs={{0,128},{32,160},{64,192},{96,224},{128,0},{160,32},{192,64},{224,... | collective-permute-start | bytes 98312 | tf_op jit(solution)/shard_map/ppermute | solution.py:391
  38.6 1.9 %shard_map.52.right = f32[4,16,1152]{2,1,0:T(8,128)S(1)} custom-call(f32[4,16,2304]{2,1,0:T(8,128)S(1)} %get-tuple-element.35.q, f32[9,16,2304]{2,1,0:T(8,128)S(1)} %bitcast.8, f32[4,16,2304]{2,1,0:T(8,128)S(1)} %bitcast.15, s32[8]{0:T(128)S(1)} %copy-done.5), custom_call_target="tpu_custom_call" | custom-call | flops 6000000 | bytes 6000000 | tf_op jit(solution)/shard_map/pallas_call | solution.py:352
  40.5 1.8 %collective-permute-done.9.mate = f32[64,128]{1,0:T(8,128)S(1)} collective-permute-done((f32[64,128]{1,0:T(8,128)S(1)}, f32[64,128]{1,0:T(8,128)S(1)}, u32[]{:S(2)}, u32[]{:S(2)}) %collective-permute-start.9) | collective-permute-done | bytes 32800 | tf_op jit(solution)/shard_map/ppermute | solution.py:391
  42.4 0.0 collective-permute-done.10.even_in
  42.4 0.0 collective-permute-done.11.odd_in
  42.4 0.0 copy-done.1
  42.4 1.9 %shard_map.54 = f32[4,16,2304]{2,1,0:T(8,128)} custom-call(f32[4,16,1152]{2,1,0:T(8,128)S(1)} %get-tuple-element.36.left, f32[4,16,1152]{2,1,0:T(8,128)S(1)} %shard_map.52.right, f32[4,16,2304]{2,1,0:T(8,128)S(1)} %get-tuple-element.35.q, f32[9,16,2304]{2,1,0:T(8,128)S(1)} %bitcast.9, f32[64,128]{1,0:T(8,128)S(1)} %collective-permute-done.6.one, ...), custom_call_target="tpu_custom_call" | custom-call | tf_op jit(solution)/shard_map/pallas_call | solution.py:364
Async XLA Ops:
  0.0 19.8 %copy-start.3 = (f32[1,4,16,2304]{3,2,1,0:T(8,128)S(1)}, f32[1,4,16,2304]{3,2,1,0:T(8,128)}, u32[]{:S(2)}) copy-start(f32[1,4,16,2304]{3,2,1,0:T(8,128)} %param.4) | copy-start | bytes 1769476
  2.4 8.3 %collective-permute-start.2 = (f32[64,128]{1,0:T(8,128)}, f32[64,128]{1,0:T(8,128)S(1)}, u32[]{:S(2)}, u32[]{:S(2)}) collective-permute-start(f32[64,128]{1,0:T(8,128)} %get-tuple-element.27.own), channel_id=1, source_target_pairs={{0,96},{32,64},{64,32},{96,0},{128,224},{160,192},{192,160},{224,1... | collective-permute-start | bytes 98312 | tf_op jit(solution)/shard_map/ppermute | solution.py:377
  4.9 5.7 %collective-permute-start.1 = (f32[64,128]{1,0:T(8,128)}, f32[64,128]{1,0:T(8,128)S(1)}, u32[]{:S(2)}, u32[]{:S(2)}) collective-permute-start(f32[64,128]{1,0:T(8,128)} %get-tuple-element.27.own), channel_id=1, source_target_pairs={{0,64},{32,96},{64,0},{96,32},{128,192},{160,224},{192,128},{224,1... | collective-permute-start | bytes 98312 | tf_op jit(solution)/shard_map/ppermute | solution.py:377
  5.5 5.2 %collective-permute-start = (f32[64,128]{1,0:T(8,128)}, f32[64,128]{1,0:T(8,128)S(1)}, u32[]{:S(2)}, u32[]{:S(2)}) collective-permute-start(f32[64,128]{1,0:T(8,128)} %get-tuple-element.27.own), channel_id=1, source_target_pairs={{0,32},{32,0},{64,96},{96,64},{128,160},{160,128},{192,224},{224,1... | collective-permute-start | bytes 98312 | tf_op jit(solution)/shard_map/ppermute | solution.py:377
  5.7 1.3 %copy-start = (f32[1,9,16,2304]{3,2,1,0:T(8,128)S(1)}, f32[1,9,16,2304]{3,2,1,0:T(8,128)}, u32[]{:S(2)}) copy-start(f32[1,9,16,2304]{3,2,1,0:T(8,128)} %param.5) | copy-start | bytes 3981316
  7.0 1.1 %copy-start.2 = (f32[1,4,16,2304]{3,2,1,0:T(8,128)S(1)}, f32[1,4,16,2304]{3,2,1,0:T(8,128)}, u32[]{:S(2)}) copy-start(f32[1,4,16,2304]{3,2,1,0:T(8,128)} %param.4) | copy-start | bytes 1769476
  8.1 0.6 %copy-start.5 = (s32[8]{0:T(128)S(1)}, s32[8]{0:T(128)}, u32[]{:S(2)}) copy-start(s32[8]{0:T(128)} %get-tuple-element.25.rest_0_.meta.rest_1_) | copy-start | bytes 100
  8.7 8.1 %copy-start.4 = (f32[64,128]{1,0:T(8,128)S(1)}, f32[64,128]{1,0:T(8,128)}, u32[]{:S(2)}) copy-start(f32[64,128]{1,0:T(8,128)} %get-tuple-element.27.own) | copy-start | bytes 98308
  10.7 11.1 %collective-permute-start.4 = (f32[8,2304]{1,0:T(8,128)S(1)}, f32[8,2304]{1,0:T(8,128)S(1)}, u32[]{:S(2)}, u32[]{:S(2)}) collective-permute-start(f32[8,2304]{1,0:T(8,128)S(1)} %get-tuple-element.33), channel_id=1, source_target_pairs={{0,1},{1,0},{2,3},{3,2},{4,5},{5,4},{6,7},{7,6},{8,9},{9,8},{10,11... | collective-permute-start | bytes 221192 | tf_op jit(solution)/shard_map/ppermute | solution.py:381
  12.3 9.5 %collective-permute-start.5 = (f32[8,2304]{1,0:T(8,128)S(1)}, f32[8,2304]{1,0:T(8,128)S(1)}, u32[]{:S(2)}, u32[]{:S(2)}) collective-permute-start(f32[8,2304]{1,0:T(8,128)S(1)} %get-tuple-element.34), channel_id=1, source_target_pairs={{1,2},{3,4},{5,6},{7,8},{9,10},{11,12},{13,14},{15,16},{17,18},{19... | collective-permute-start | bytes 221192 | tf_op jit(solution)/shard_map/ppermute | solution.py:383
  17.4 4.4 %collective-permute-start.3 = (f32[64,128]{1,0:T(8,128)S(1)}, f32[64,128]{1,0:T(8,128)S(1)}, u32[]{:S(2)}, u32[]{:S(2)}) collective-permute-start(f32[64,128]{1,0:T(8,128)S(1)} %shard_map.49), channel_id=1, source_target_pairs={{0,128},{32,160},{64,192},{96,224},{128,0},{160,32},{192,64},{224,... | collective-permute-start | bytes 98312 | tf_op jit(solution)/shard_map/ppermute | solution.py:391
  23.2 5.3 %collective-permute-start.8 = (f32[64,128]{1,0:T(8,128)S(1)}, f32[64,128]{1,0:T(8,128)S(1)}, u32[]{:S(2)}, u32[]{:S(2)}) collective-permute-start(f32[64,128]{1,0:T(8,128)S(1)} %get-tuple-element.37.own), channel_id=1, source_target_pairs={{0,96},{32,64},{64,32},{96,0},{128,224},{160,192},{192,160},{224,1... | collective-permute-start | bytes 98312 | tf_op jit(solution)/shard_map/ppermute | solution.py:377
  25.8 4.4 %collective-permute-start.7 = (f32[64,128]{1,0:T(8,128)S(1)}, f32[64,128]{1,0:T(8,128)S(1)}, u32[]{:S(2)}, u32[]{:S(2)}) collective-permute-start(f32[64,128]{1,0:T(8,128)S(1)} %get-tuple-element.37.own), channel_id=1, source_target_pairs={{0,64},{32,96},{64,0},{96,32},{128,192},{160,224},{192,128},{224,1... | collective-permute-start | bytes 98312 | tf_op jit(solution)/shard_map/ppermute | solution.py:377
  26.3 3.8 %collective-permute-start.6 = (f32[64,128]{1,0:T(8,128)S(1)}, f32[64,128]{1,0:T(8,128)S(1)}, u32[]{:S(2)}, u32[]{:S(2)}) collective-permute-start(f32[64,128]{1,0:T(8,128)S(1)} %get-tuple-element.37.own), channel_id=1, source_target_pairs={{0,32},{32,0},{64,96},{96,64},{128,160},{160,128},{192,224},{224,1... | collective-permute-start | bytes 98312 | tf_op jit(solution)/shard_map/ppermute | solution.py:377
  30.2 12.2 %collective-permute-start.10 = (f32[8,2304]{1,0:T(8,128)S(1)}, f32[8,2304]{1,0:T(8,128)S(1)}, u32[]{:S(2)}, u32[]{:S(2)}) collective-permute-start(f32[8,2304]{1,0:T(8,128)S(1)} %get-tuple-element.43), channel_id=1, source_target_pairs={{0,1},{1,0},{2,3},{3,2},{4,5},{5,4},{6,7},{7,6},{8,9},{9,8},{10,11... | collective-permute-start | bytes 221192 | tf_op jit(solution)/shard_map/ppermute | solution.py:381
  30.6 11.8 %collective-permute-start.11 = (f32[8,2304]{1,0:T(8,128)S(1)}, f32[8,2304]{1,0:T(8,128)S(1)}, u32[]{:S(2)}, u32[]{:S(2)}) collective-permute-start(f32[8,2304]{1,0:T(8,128)S(1)} %get-tuple-element.44), channel_id=1, source_target_pairs={{1,2},{3,4},{5,6},{7,8},{9,10},{11,12},{13,14},{15,16},{17,18},{19... | collective-permute-start | bytes 221192 | tf_op jit(solution)/shard_map/ppermute | solution.py:383
  37.8 4.6 %copy-start.1 = (f32[1,9,16,2304]{3,2,1,0:T(8,128)S(1)}, f32[1,9,16,2304]{3,2,1,0:T(8,128)}, u32[]{:S(2)}) copy-start(f32[1,9,16,2304]{3,2,1,0:T(8,128)} %param.5) | copy-start | bytes 3981316
  37.8 4.5 %collective-permute-start.9 = (f32[64,128]{1,0:T(8,128)S(1)}, f32[64,128]{1,0:T(8,128)S(1)}, u32[]{:S(2)}, u32[]{:S(2)}) collective-permute-start(f32[64,128]{1,0:T(8,128)S(1)} %shard_map.53), channel_id=1, source_target_pairs={{0,128},{32,160},{64,192},{96,224},{128,0},{160,32},{192,64},{224,... | collective-permute-start | bytes 98312 | tf_op jit(solution)/shard_map/ppermute | solution.py:391

commit v3 on v2

--- a/solution.py
+++ b/solution.py
@@ -91,11 +91,11 @@
         odd_ref[2 * c : 2 * c + 2, :] = jnp.where(even, low, high)
 
 
-def first_kernel(q_hbm, map_hbm, links_hbm, joint_ref, meta, q, block_map, links, sem):
+def first_kernel(q_hbm, metric_hbm, map_hbm, links_hbm, q, metric, joint_ref, meta, block_map, links, sem):
     copies = [
         pltpu.make_async_copy(source, target, sem.at[n])
         for n, (source, target) in enumerate(
-            ((links_hbm, links), (map_hbm, block_map), (q_hbm, q))
+            ((links_hbm, links), (map_hbm, block_map), (q_hbm, q), (metric_hbm, metric))
         )
     ]
     for copy in copies:
@@ -117,6 +117,7 @@
     meta[7] = position
     copies[2].wait()
     write_joint(lambda c, t: q[c, :, 128 * t : 128 * t + 128], joint_ref, face, along, across)
+    copies[3].wait()
 
 
 def pick_kernel(own, one, two, three, meta, out):
@@ -395,20 +396,20 @@
 
 def on_device(state, metric, block_map, links):
     HBM = pl.BlockSpec(memory_space=pltpu.HBM)
-    q, geometry = state.reshape(4, LEN, CELLS), metric.reshape(9, LEN, CELLS)
-    joint, meta = pl.pallas_call(
+    held = lambda x: pltpu.with_memory_space_constraint(x, pltpu.HBM)
+    arrays = (state.reshape(4, LEN, CELLS), metric.reshape(9, LEN, CELLS), block_map, jnp.transpose(links, (1, 2, 0)))
+    q, geometry, joint, meta = pl.pallas_call(
         first_kernel,
-        out_shape=[JOINT, jax.ShapeDtypeStruct((8,), jnp.int32)],
-        in_specs=[HBM] * 3,
-        out_specs=[VMEM, SMEM],
+        out_shape=[FIELD, f32((9, LEN, CELLS)), JOINT, jax.ShapeDtypeStruct((8,), jnp.int32)],
+        in_specs=[HBM] * 4,
+        out_specs=[VMEM] * 3 + [SMEM],
         scratch_shapes=[
-            pltpu.VMEM((4, LEN, CELLS), jnp.float32),
             pltpu.SMEM((SEGS * CHAIN,), jnp.int32),
             pltpu.SMEM((6, 4, SEGS * CHAIN), jnp.int32),
-            pltpu.SemaphoreType.DMA((3,)),
+            pltpu.SemaphoreType.DMA((4,)),
         ],
-        compiler_params=WHOLE,
-    )(q, block_map, jnp.transpose(links, (1, 2, 0)))
+        compiler_params=PARAMS,
+    )(*map(held, arrays))
     q1, joint = section(False, q, geometry, joint, None, meta)
     (advanced,) = section(True, q1, geometry, joint, q, meta)
     return advanced.reshape(state.shape)

time: 44.1 us -> 41.4 us (0.939)
  local copies, waits for them, and re-layouts: 3.01 us -> 0 us
  starting transfers between devices: 23 us -> 23.7 us
    unnamed x12 -> x0, local copies, waits for them, and re-layouts: 3.01 us -> none
    ppermute x2, starting transfers between devices: 2 us -> 3.29 us  [section(): from_even = lax.ppermute(even, 'blk', [(i, i ^ 1) for i in range(CHAIN)])]
    ppermute x2, starting transfers between devices: 11.2 us -> 10.5 us  [section(): from_odd = lax.ppermute(odd, 'blk', pairs + [(b, a) for a, b in pairs])]
  transfers between devices with their start and end apart: 12 -> 12, of which waited for: 3 -> 4; matrix products, arithmetic and copies ran while one was open for 0% -> 0% of each run, Pallas kernels for 20% -> 21%
where the time goes in v3:
time: 41.4 us; the launch traced here: 41.6 us
  starting transfers between devices  23.7 us (57%)
  Pallas kernels  14.2 us (34%)
  waiting for transfers between devices  3.61 us (9%)
    ppermute x2, starting transfers between devices, section(): from_odd = lax.ppermute(odd, 'blk', pairs + [(b, a) for a, b in pairs])  10.5 us
    pallas_call x4, Pallas kernels, bulk(): pl.pallas_call(functools.partial(bulk_kernel, last, tiles), out_shape=sha...  7.7 us
    ppermute x6, starting transfers between devices, section(): lax.ppermute(joint, 'seg', [(i, i ^ s) for i in range(SEGS)])  6.7 us
    ppermute x2, starting transfers between devices, section(): from_even = lax.ppermute(even, 'blk', [(i, i ^ 1) for i in range(CHAIN)])  3.29 us
    ppermute x2, starting transfers between devices, section(): mate = lax.ppermute(picked, 'seg', [(i, i ^ 4) for i in range(SEGS)])  3.22 us
    pallas_call x2, Pallas kernels, edges(): pl.pallas_call(functools.partial(edge_kernel, last), out_shape=shapes, in...  3.15 us
    pallas_call x1, Pallas kernels, on_device(): pl.pallas_call(first_kernel, out_shape=[FIELD, f32((9, LEN, CELLS)), JOIN...  2.21 us
    ppermute x2, waiting for transfers between devices, section(): mate = lax.ppermute(picked, 'seg', [(i, i ^ 4) for i in range(SEGS)])  1.85 us
  transfers between devices with their start and end apart: 12, of which 4 were waited for; matrix products, arithmetic and copies ran while one was open for 0% of the time, Pallas kernels for 21%

profile of v3, /device:TPU:105, one launch (start us, length us, event | category | flops | bytes accessed | tf_op | source)
XLA Modules:
  0.0 41.6 jit_solution(3084594852969429247)
XLA Ops:
  0.0 2.2 %shard_map.46 = (f32[4,16,2304]{2,1,0:T(8,128)S(1)}, f32[9,16,2304]{2,1,0:T(8,128)S(1)}, f32[64,128]{1,0:T(8,128)S(1)}, s32[8]{0:T(128)S(1)}) custom-call(f32[4,16,2304]{2,1,0:T(8,128)} %bitcast.5, f32[9,16,2304]{2,1,0:T(8,128)} %bitcast.4, s32[256]{0:T(256)} %map_hbm.1, s32[6,4,256]{2,1,0:T(4,128)} %bitcast.6), custom_call_target="tpu_custom_call" | custom-call | tf_op jit(solution)/shard_map/pallas_call | solution.py:401
  2.2 2.6 %collective-permute-start.2 = (f32[64,128]{1,0:T(8,128)S(1)}, f32[64,128]{1,0:T(8,128)S(1)}, u32[]{:S(2)}, u32[]{:S(2)}) collective-permute-start(f32[64,128]{1,0:T(8,128)S(1)} %get-tuple-element.31.own), channel_id=1, source_target_pairs={{0,96},{32,64},{64,32},{96,0},{128,224},{160,192},{192,160},{224,1... | collective-permute-start | bytes 98312 | tf_op jit(solution)/shard_map/ppermute | solution.py:378
  4.8 0.5 %collective-permute-start.1 = (f32[64,128]{1,0:T(8,128)S(1)}, f32[64,128]{1,0:T(8,128)S(1)}, u32[]{:S(2)}, u32[]{:S(2)}) collective-permute-start(f32[64,128]{1,0:T(8,128)S(1)} %get-tuple-element.31.own), channel_id=1, source_target_pairs={{0,64},{32,96},{64,0},{96,32},{128,192},{160,224},{192,128},{224,1... | collective-permute-start | bytes 98312 | tf_op jit(solution)/shard_map/ppermute | solution.py:378
  5.3 0.3 collective-permute-start
  5.6 1.9 %shard_map.47 = (f32[4,16,1152]{2,1,0:T(8,128)S(1)}, f32[8,2304]{1,0:T(8,128)S(1)}, f32[8,2304]{1,0:T(8,128)S(1)}) custom-call(f32[4,16,2304]{2,1,0:T(8,128)S(1)} %get-tuple-element.27.q.rest_0_, f32[9,16,2304]{2,1,0:T(8,128)S(1)} %get-tuple-element.28.metric, s32[8]{0:T(128)S(1)} %get-tuple-element.29.rest_0_.meta.rest_1_), custom_call_target="tpu_custom_call" | custom-call | flops 6000000 | bytes 6000000 | tf_op jit(solution)/shard_map/pallas_call | solution.py:353
  7.5 0.0 collective-permute-done.2.three
  7.5 1.5 %collective-permute-done.1.two = f32[64,128]{1,0:T(8,128)S(1)} collective-permute-done((f32[64,128]{1,0:T(8,128)S(1)}, f32[64,128]{1,0:T(8,128)S(1)}, u32[]{:S(2)}, u32[]{:S(2)}) %collective-permute-start.1) | collective-permute-done | bytes 32800 | tf_op jit(solution)/shard_map/ppermute | solution.py:378
  9.1 0.0 collective-permute-done.one
  9.1 2.1 %collective-permute-start.4 = (f32[8,2304]{1,0:T(8,128)S(1)}, f32[8,2304]{1,0:T(8,128)S(1)}, u32[]{:S(2)}, u32[]{:S(2)}) collective-permute-start(f32[8,2304]{1,0:T(8,128)S(1)} %get-tuple-element.37), channel_id=1, source_target_pairs={{0,1},{1,0},{2,3},{3,2},{4,5},{5,4},{6,7},{7,6},{8,9},{9,8},{10,11... | collective-permute-start | bytes 221192 | tf_op jit(solution)/shard_map/ppermute | solution.py:382
  11.2 4.5 %collective-permute-start.5 = (f32[8,2304]{1,0:T(8,128)S(1)}, f32[8,2304]{1,0:T(8,128)S(1)}, u32[]{:S(2)}, u32[]{:S(2)}) collective-permute-start(f32[8,2304]{1,0:T(8,128)S(1)} %get-tuple-element.38), channel_id=1, source_target_pairs={{1,2},{3,4},{5,6},{7,8},{9,10},{11,12},{13,14},{15,16},{17,18},{19... | collective-permute-start | bytes 221192 | tf_op jit(solution)/shard_map/ppermute | solution.py:384
  15.7 0.6 %shard_map.49 = f32[64,128]{1,0:T(8,128)S(1)} custom-call(f32[64,128]{1,0:T(8,128)S(1)} %get-tuple-element.31.own, f32[64,128]{1,0:T(8,128)S(1)} %collective-permute-done.one, f32[64,128]{1,0:T(8,128)S(1)} %collective-permute-done.1.two, f32[64,128]{1,0:T(8,128)S(1)} %collective-permute-done.2.three, s32[8]{0:T(128)S(1)} %get-tuple-element.29.rest_0_.meta.rest_1_), custom_call_target="tpu_custom_call" | custom-call | tf_op jit(solution)/shard_map/pallas_call | solution.py:385
  16.3 2.4 %collective-permute-start.3 = (f32[64,128]{1,0:T(8,128)S(1)}, f32[64,128]{1,0:T(8,128)S(1)}, u32[]{:S(2)}, u32[]{:S(2)}) collective-permute-start(f32[64,128]{1,0:T(8,128)S(1)} %shard_map.49), channel_id=1, source_target_pairs={{0,128},{32,160},{64,192},{96,224},{128,0},{160,32},{192,64},{224,... | collective-permute-start | bytes 98312 | tf_op jit(solution)/shard_map/ppermute | solution.py:392
  18.7 1.9 %shard_map.48.right = f32[4,16,1152]{2,1,0:T(8,128)S(1)} custom-call(f32[4,16,2304]{2,1,0:T(8,128)S(1)} %get-tuple-element.27.q.rest_0_, f32[9,16,2304]{2,1,0:T(8,128)S(1)} %get-tuple-element.28.metric, s32[8]{0:T(128)S(1)} %get-tuple-element.29.rest_0_.meta.rest_1_), custom_call_target="tpu_custom_call" | custom-call | flops 6000000 | bytes 6000000 | tf_op jit(solution)/shard_map/pallas_call | solution.py:353
  20.6 0.1 collective-permute-done.3.mate
  20.6 0.0 collective-permute-done.4.even_in
  20.6 0.0 collective-permute-done.5.odd_in
  20.6 1.4 %shard_map.50 = (f32[4,16,2304]{2,1,0:T(8,128)S(1)}, f32[64,128]{1,0:T(8,128)S(1)}) custom-call(f32[4,16,1152]{2,1,0:T(8,128)S(1)} %get-tuple-element.30.left, f32[4,16,1152]{2,1,0:T(8,128)S(1)} %shard_map.48.right, f32[4,16,2304]{2,1,0:T(8,128)S(1)} %get-tuple-element.27.q.rest_0_, f32[9,16,2304]{2,1,0:T(8,128)S(1)} %get-tuple-element.28.metric, ...), custom_call_target="tpu_custom_call" | custom-call | tf_op jit(solution)/shard_map/pallas_call | solution.py:365
  22.0 1.2 %collective-permute-start.8 = (f32[64,128]{1,0:T(8,128)S(1)}, f32[64,128]{1,0:T(8,128)S(1)}, u32[]{:S(2)}, u32[]{:S(2)}) collective-permute-start(f32[64,128]{1,0:T(8,128)S(1)} %get-tuple-element.41.own), channel_id=1, source_target_pairs={{0,96},{32,64},{64,32},{96,0},{128,224},{160,192},{192,160},{224,1... | collective-permute-start | bytes 98312 | tf_op jit(solution)/shard_map/ppermute | solution.py:378
  23.2 0.8 %collective-permute-start.7 = (f32[64,128]{1,0:T(8,128)S(1)}, f32[64,128]{1,0:T(8,128)S(1)}, u32[]{:S(2)}, u32[]{:S(2)}) collective-permute-start(f32[64,128]{1,0:T(8,128)S(1)} %get-tuple-element.41.own), channel_id=1, source_target_pairs={{0,64},{32,96},{64,0},{96,32},{128,192},{160,224},{192,128},{224,1... | collective-permute-start | bytes 98312 | tf_op jit(solution)/shard_map/ppermute | solution.py:378
  24.0 1.4 %collective-permute-start.6 = (f32[64,128]{1,0:T(8,128)S(1)}, f32[64,128]{1,0:T(8,128)S(1)}, u32[]{:S(2)}, u32[]{:S(2)}) collective-permute-start(f32[64,128]{1,0:T(8,128)S(1)} %get-tuple-element.41.own), channel_id=1, source_target_pairs={{0,32},{32,0},{64,96},{96,64},{128,160},{160,128},{192,224},{224,1... | collective-permute-start | bytes 98312 | tf_op jit(solution)/shard_map/ppermute | solution.py:378
  25.4 1.9 %shard_map.51 = (f32[4,16,1152]{2,1,0:T(8,128)S(1)}, f32[8,2304]{1,0:T(8,128)S(1)}, f32[8,2304]{1,0:T(8,128)S(1)}) custom-call(f32[4,16,2304]{2,1,0:T(8,128)S(1)} %get-tuple-element.39.q, f32[9,16,2304]{2,1,0:T(8,128)S(1)} %get-tuple-element.28.metric, f32[4,16,2304]{2,1,0:T(8,128)S(1)} %get-tuple-element.27.q.rest_0_, ...), custom_call_target="tpu_custom_call" | custom-call | flops 6000000 | bytes 6000000 | tf_op jit(solution)/shard_map/pallas_call | solution.py:353
  27.3 0.0 collective-permute-done.8.three
  27.3 0.2 collective-permute-done.7.two
  27.5 0.0 collective-permute-done.6.one
  27.5 1.2 %collective-permute-start.10 = (f32[8,2304]{1,0:T(8,128)S(1)}, f32[8,2304]{1,0:T(8,128)S(1)}, u32[]{:S(2)}, u32[]{:S(2)}) collective-permute-start(f32[8,2304]{1,0:T(8,128)S(1)} %get-tuple-element.47), channel_id=1, source_target_pairs={{0,1},{1,0},{2,3},{3,2},{4,5},{5,4},{6,7},{7,6},{8,9},{9,8},{10,11... | collective-permute-start | bytes 221192 | tf_op jit(solution)/shard_map/ppermute | solution.py:382
  28.7 6.0 %collective-permute-start.11 = (f32[8,2304]{1,0:T(8,128)S(1)}, f32[8,2304]{1,0:T(8,128)S(1)}, u32[]{:S(2)}, u32[]{:S(2)}) collective-permute-start(f32[8,2304]{1,0:T(8,128)S(1)} %get-tuple-element.48), channel_id=1, source_target_pairs={{1,2},{3,4},{5,6},{7,8},{9,10},{11,12},{13,14},{15,16},{17,18},{19... | collective-permute-start | bytes 221192 | tf_op jit(solution)/shard_map/ppermute | solution.py:384
  34.7 0.6 %shard_map.53 = f32[64,128]{1,0:T(8,128)S(1)} custom-call(f32[64,128]{1,0:T(8,128)S(1)} %get-tuple-element.41.own, f32[64,128]{1,0:T(8,128)S(1)} %collective-permute-done.6.one, f32[64,128]{1,0:T(8,128)S(1)} %collective-permute-done.7.two, f32[64,128]{1,0:T(8,128)S(1)} %collective-permute-done.8.three, s32[8]{0:T(128)S(1)} %get-tuple-element.29.rest_0_.meta.rest_1_), custom_call_target="tpu_custom_call" | custom-call | tf_op jit(solution)/shard_map/pallas_call | solution.py:385
  35.3 0.8 %collective-permute-start.9 = (f32[64,128]{1,0:T(8,128)S(1)}, f32[64,128]{1,0:T(8,128)S(1)}, u32[]{:S(2)}, u32[]{:S(2)}) collective-permute-start(f32[64,128]{1,0:T(8,128)S(1)} %shard_map.53), channel_id=1, source_target_pairs={{0,128},{32,160},{64,192},{96,224},{128,0},{160,32},{192,64},{224,... | collective-permute-start | bytes 98312 | tf_op jit(solution)/shard_map/ppermute | solution.py:392
  36.1 1.9 %shard_map.52.right = f32[4,16,1152]{2,1,0:T(8,128)S(1)} custom-call(f32[4,16,2304]{2,1,0:T(8,128)S(1)} %get-tuple-element.39.q, f32[9,16,2304]{2,1,0:T(8,128)S(1)} %get-tuple-element.28.metric, f32[4,16,2304]{2,1,0:T(8,128)S(1)} %get-tuple-element.27.q.rest_0_, s32[8]{0:T(128)S(1)} %get-tuple-element.29.rest_0_.meta.rest_1_), custom_call_target="tpu_custom_call" | custom-call | flops 6000000 | bytes 6000000 | tf_op jit(solution)/shard_map/pallas_call | solution.py:353
  38.1 1.8 %collective-permute-done.9.mate = f32[64,128]{1,0:T(8,128)S(1)} collective-permute-done((f32[64,128]{1,0:T(8,128)S(1)}, f32[64,128]{1,0:T(8,128)S(1)}, u32[]{:S(2)}, u32[]{:S(2)}) %collective-permute-start.9) | collective-permute-done | bytes 32800 | tf_op jit(solution)/shard_map/ppermute | solution.py:392
  39.8 0.0 collective-permute-done.10.even_in
  39.8 0.0 collective-permute-done.11.odd_in
  39.8 1.8 %shard_map.54 = f32[4,16,2304]{2,1,0:T(8,128)} custom-call(f32[4,16,1152]{2,1,0:T(8,128)S(1)} %get-tuple-element.40.left, f32[4,16,1152]{2,1,0:T(8,128)S(1)} %shard_map.52.right, f32[4,16,2304]{2,1,0:T(8,128)S(1)} %get-tuple-element.39.q, f32[9,16,2304]{2,1,0:T(8,128)S(1)} %get-tuple-element.28.metric, f32[64,128]{1,0:T(8,128)S(1)} %collective-permute-done.6.one, ...), custom_call_target="tpu_custom_call" | custom-call | tf_op jit(solution)/shard_map/pallas_call | solution.py:365
Async XLA Ops:
  2.2 5.3 %collective-permute-start.2 = (f32[64,128]{1,0:T(8,128)S(1)}, f32[64,128]{1,0:T(8,128)S(1)}, u32[]{:S(2)}, u32[]{:S(2)}) collective-permute-start(f32[64,128]{1,0:T(8,128)S(1)} %get-tuple-element.31.own), channel_id=1, source_target_pairs={{0,96},{32,64},{64,32},{96,0},{128,224},{160,192},{192,160},{224,1... | collective-permute-start | bytes 98312 | tf_op jit(solution)/shard_map/ppermute | solution.py:378
  4.8 4.3 %collective-permute-start.1 = (f32[64,128]{1,0:T(8,128)S(1)}, f32[64,128]{1,0:T(8,128)S(1)}, u32[]{:S(2)}, u32[]{:S(2)}) collective-permute-start(f32[64,128]{1,0:T(8,128)S(1)} %get-tuple-element.31.own), channel_id=1, source_target_pairs={{0,64},{32,96},{64,0},{96,32},{128,192},{160,224},{192,128},{224,1... | collective-permute-start | bytes 98312 | tf_op jit(solution)/shard_map/ppermute | solution.py:378
  5.3 3.8 %collective-permute-start = (f32[64,128]{1,0:T(8,128)S(1)}, f32[64,128]{1,0:T(8,128)S(1)}, u32[]{:S(2)}, u32[]{:S(2)}) collective-permute-start(f32[64,128]{1,0:T(8,128)S(1)} %get-tuple-element.31.own), channel_id=1, source_target_pairs={{0,32},{32,0},{64,96},{96,64},{128,160},{160,128},{192,224},{224,1... | collective-permute-start | bytes 98312 | tf_op jit(solution)/shard_map/ppermute | solution.py:378
  9.1 11.6 %collective-permute-start.4 = (f32[8,2304]{1,0:T(8,128)S(1)}, f32[8,2304]{1,0:T(8,128)S(1)}, u32[]{:S(2)}, u32[]{:S(2)}) collective-permute-start(f32[8,2304]{1,0:T(8,128)S(1)} %get-tuple-element.37), channel_id=1, source_target_pairs={{0,1},{1,0},{2,3},{3,2},{4,5},{5,4},{6,7},{7,6},{8,9},{9,8},{10,11... | collective-permute-start | bytes 221192 | tf_op jit(solution)/shard_map/ppermute | solution.py:382
  11.2 9.5 %collective-permute-start.5 = (f32[8,2304]{1,0:T(8,128)S(1)}, f32[8,2304]{1,0:T(8,128)S(1)}, u32[]{:S(2)}, u32[]{:S(2)}) collective-permute-start(f32[8,2304]{1,0:T(8,128)S(1)} %get-tuple-element.38), channel_id=1, source_target_pairs={{1,2},{3,4},{5,6},{7,8},{9,10},{11,12},{13,14},{15,16},{17,18},{19... | collective-permute-start | bytes 221192 | tf_op jit(solution)/shard_map/ppermute | solution.py:384
  16.3 4.4 %collective-permute-start.3 = (f32[64,128]{1,0:T(8,128)S(1)}, f32[64,128]{1,0:T(8,128)S(1)}, u32[]{:S(2)}, u32[]{:S(2)}) collective-permute-start(f32[64,128]{1,0:T(8,128)S(1)} %shard_map.49), channel_id=1, source_target_pairs={{0,128},{32,160},{64,192},{96,224},{128,0},{160,32},{192,64},{224,... | collective-permute-start | bytes 98312 | tf_op jit(solution)/shard_map/ppermute | solution.py:392
  22.0 5.3 %collective-permute-start.8 = (f32[64,128]{1,0:T(8,128)S(1)}, f32[64,128]{1,0:T(8,128)S(1)}, u32[]{:S(2)}, u32[]{:S(2)}) collective-permute-start(f32[64,128]{1,0:T(8,128)S(1)} %get-tuple-element.41.own), channel_id=1, source_target_pairs={{0,96},{32,64},{64,32},{96,0},{128,224},{160,192},{192,160},{224,1... | collective-permute-start | bytes 98312 | tf_op jit(solution)/shard_map/ppermute | solution.py:378
  23.2 4.3 %collective-permute-start.7 = (f32[64,128]{1,0:T(8,128)S(1)}, f32[64,128]{1,0:T(8,128)S(1)}, u32[]{:S(2)}, u32[]{:S(2)}) collective-permute-start(f32[64,128]{1,0:T(8,128)S(1)} %get-tuple-element.41.own), channel_id=1, source_target_pairs={{0,64},{32,96},{64,0},{96,32},{128,192},{160,224},{192,128},{224,1... | collective-permute-start | bytes 98312 | tf_op jit(solution)/shard_map/ppermute | solution.py:378
  24.0 3.5 %collective-permute-start.6 = (f32[64,128]{1,0:T(8,128)S(1)}, f32[64,128]{1,0:T(8,128)S(1)}, u32[]{:S(2)}, u32[]{:S(2)}) collective-permute-start(f32[64,128]{1,0:T(8,128)S(1)} %get-tuple-element.41.own), channel_id=1, source_target_pairs={{0,32},{32,0},{64,96},{96,64},{128,160},{160,128},{192,224},{224,1... | collective-permute-start | bytes 98312 | tf_op jit(solution)/shard_map/ppermute | solution.py:378
  27.5 12.3 %collective-permute-start.10 = (f32[8,2304]{1,0:T(8,128)S(1)}, f32[8,2304]{1,0:T(8,128)S(1)}, u32[]{:S(2)}, u32[]{:S(2)}) collective-permute-start(f32[8,2304]{1,0:T(8,128)S(1)} %get-tuple-element.47), channel_id=1, source_target_pairs={{0,1},{1,0},{2,3},{3,2},{4,5},{5,4},{6,7},{7,6},{8,9},{9,8},{10,11... | collective-permute-start | bytes 221192 | tf_op jit(solution)/shard_map/ppermute | solution.py:382
  28.7 11.1 %collective-permute-start.11 = (f32[8,2304]{1,0:T(8,128)S(1)}, f32[8,2304]{1,0:T(8,128)S(1)}, u32[]{:S(2)}, u32[]{:S(2)}) collective-permute-start(f32[8,2304]{1,0:T(8,128)S(1)} %get-tuple-element.48), channel_id=1, source_target_pairs={{1,2},{3,4},{5,6},{7,8},{9,10},{11,12},{13,14},{15,16},{17,18},{19... | collective-permute-start | bytes 221192 | tf_op jit(solution)/shard_map/ppermute | solution.py:384
  35.3 4.5 %collective-permute-start.9 = (f32[64,128]{1,0:T(8,128)S(1)}, f32[64,128]{1,0:T(8,128)S(1)}, u32[]{:S(2)}, u32[]{:S(2)}) collective-permute-start(f32[64,128]{1,0:T(8,128)S(1)} %shard_map.53), channel_id=1, source_target_pairs={{0,128},{32,160},{64,192},{96,224},{128,0},{160,32},{192,64},{224,... | collective-permute-start | bytes 98312 | tf_op jit(solution)/shard_map/ppermute | solution.py:392

commit v4 on v3

--- a/solution.py
+++ b/solution.py
@@ -8,6 +8,9 @@
 
 LEN, CROSS, CELLS, TILES = 16, 48, 2304, 18
 HALF = 9
+DEEP, GEOMETRY, BELOW, ABOVE, ROWS = 64, 128, 272, 280, 288
+FACE, ALONG, ACROSS, POSITION, HAS_LOW, HAS_HIGH, OWN, MATE = 0, 1, 2, 3, 4, 5, 6, 9
+PARTS = ((0, BELOW), (BELOW, ABOVE), (ABOVE, ROWS))
 SEGS, CHAIN = 8, 32
 time_step = 0.05
 viscosity = 0.2
@@ -62,33 +65,27 @@
     return jnp.where(face <= 3, depth * CROSS + place, place * CROSS + depth)
 
 
-def extract_faces(load, names, source, store, along):
-    for name in names:
-        found = jnp.zeros((LEN, 128), jnp.float32)
-        for t in range(TILES):
-            local = source - 128 * t
-            inside = (local >= 0) & (local < 128)
-            local = jnp.clip(local, 0, 127)
-            tile = load(name, t)
-            picked = gather_lanes(tile, local)
-            found = jnp.where(jnp.concatenate([inside, inside], axis=0), picked, found)
-        found = jnp.where(along == 1, reversed_rows(found), found)
-        store(name, found)
-
-
-def write_joint(load, joint_ref, face, along, across):
-    def store(c, values):
-        joint_ref[16 * c : 16 * c + 16, :] = values
-
-    extract_faces(load, range(4), face_source(face, across, 0), store, along)
+def gather_face(load, source):
+    index, owner = source & 127, source >> 7
+    found = None
+    for t in range(TILES):
+        picked = gather_lanes(load(t), index)
+        if found is None:
+            found = picked
+        else:
+            inside = owner == t
+            if picked.shape[0] == LEN:
+                inside = jnp.concatenate([inside, inside], axis=0)
+            found = jnp.where(inside, picked, found)
+    return found
 
 
 def write_chain(field, even_ref, odd_ref, position):
     even = lax.rem(position, 2) == 0
     for c in range(4):
         low, high = field[c, 0:2, :], field[c, LEN - 2 : LEN, :]
-        even_ref[2 * c : 2 * c + 2, :] = jnp.where(even, high, low)
-        odd_ref[2 * c : 2 * c + 2, :] = jnp.where(even, low, high)
+        even_ref[2 * c : 2 * c + 2, 0:CELLS] = jnp.where(even, high, low)
+        odd_ref[2 * c : 2 * c + 2, 0:CELLS] = jnp.where(even, low, high)
 
 
 def first_kernel(q_hbm, metric_hbm, map_hbm, links_hbm, q, metric, joint_ref, meta, block_map, links, sem):
@@ -103,30 +100,61 @@
     segment, position = lax.axis_index("seg"), lax.axis_index("blk")
     copies[0].wait()
     copies[1].wait()
-    face, partner, along, across = joined_face(segment * CHAIN + position, block_map, links)
-    mate = (segment + 4) % 8
-    _, mate_partner, _, _ = joined_face(mate * CHAIN + position, block_map, links)
-    meta[0] = face
-    meta[1] = along
-    meta[2] = across
-    meta[3] = jnp.where(partner // 4 == segment // 4, (partner ^ segment) & 3, 0)
-    meta[4] = (mate_partner ^ segment) & 3
-    block = block_map[segment * CHAIN + position]
-    meta[5] = jnp.where(links[0, 0, block] >= 0, 1, 0)
-    meta[6] = jnp.where(links[1, 0, block] >= 0, 1, 0)
-    meta[7] = position
+    here = segment * CHAIN + position
+    other = (segment ^ 4) * CHAIN + position
+    before, after = jnp.where(position > 0, -1, 0), jnp.where(position < CHAIN - 1, 1, 0)
+    face, partner, along, across = joined_face(here, block_map, links)
+    low_face, low_partner, _, low_across = joined_face(here + before, block_map, links)
+    high_face, high_partner, _, high_across = joined_face(here + after, block_map, links)
+    own = (partner, low_partner, high_partner)
+    mates = [joined_face(other + shift, block_map, links)[1] for shift in (0, before, after)]
+    meta[FACE] = face
+    meta[ALONG] = along
+    meta[ACROSS] = across
+    meta[POSITION] = position
+    block = block_map[here]
+    meta[HAS_LOW] = jnp.where(links[0, 0, block] >= 0, 1, 0)
+    meta[HAS_HIGH] = jnp.where(links[1, 0, block] >= 0, 1, 0)
+    for n in range(3):
+        meta[OWN + n] = jnp.where(own[n] // 4 == segment // 4, (own[n] ^ segment) & 3, 0)
+        meta[MATE + n] = (mates[n] ^ segment) & 3
     copies[2].wait()
-    write_joint(lambda c, t: q[c, :, 128 * t : 128 * t + 128], joint_ref, face, along, across)
+
+    def put(start, values):
+        joint_ref[start : start + LEN, :] = jnp.where(along == 1, reversed_rows(values), values)
+
+    where = lambda t: slice(128 * t, 128 * t + 128)
+    near, deep = face_source(face, across, 0), face_source(face, across, 2)
+    below, above = face_source(low_face, low_across, 0), face_source(high_face, high_across, 0)
+    for c in range(4):
+        put(LEN * c, gather_face(lambda t: q[c, :, where(t)], near))
+        put(DEEP + LEN * c, gather_face(lambda t: q[c, :, where(t)], deep))
+        low_rows = gather_face(lambda t: q[c, 0:8, where(t)], below)
+        joint_ref[BELOW + 2 * c : BELOW + 2 * c + 2, :] = low_rows[0:2]
+        high_rows = gather_face(lambda t: q[c, 8:16, where(t)], above)
+        joint_ref[ABOVE + 2 * c : ABOVE + 2 * c + 2, :] = high_rows[6:8]
     copies[3].wait()
-
-
-def pick_kernel(own, one, two, three, meta, out):
-    choice = meta[4]
-    for n, ref in enumerate((own, one, two, three)):
+    normal = jnp.where(face <= 3, 1, 2)
+    inward = jnp.where((face == 3) | (face == 5), -1.0, 1.0)
+    forward = jnp.where(along == 1, -1.0, 1.0)
+    sideways = jnp.where(across == 1, -1.0, 1.0)
+    for a, (row, sign) in enumerate(((0, forward), (3 * normal, inward), (3 * (3 - normal), sideways))):
+        for b in range(3):
+            found = gather_face(lambda t: metric[row + b, :, where(t)], near)
+            put(GEOMETRY + LEN * (3 * a + b), sign * found)
+
+
+def copy_part(choice, refs, rows, out):
+    for n, ref in enumerate(refs):
 
         @pl.when(choice == n)
         def _(ref=ref):
-            out[...] = ref[...]
+            out[...] = ref[rows[0] : rows[1], :]
+
+
+def pick_kernel(own, one, two, three, meta, out):
+    for n, rows in enumerate(PARTS):
+        copy_part(meta[MATE + n], (own, one, two, three), rows, out.at[rows[0] : rows[1], :])
 
 
 def shifted_lanes(before, here, after, shift):
@@ -174,10 +202,10 @@
     first, rest = (rest[0], rest[1:]) if last else (None, rest)
     meta, out = rest[:2]
     if len(rest) == 4:
-        write_chain(q, rest[2], rest[3], meta[7])
+        write_chain(q, rest[2], rest[3], meta[POSITION])
     lane = lanes_of(LEN)
     row = lax.broadcasted_iota(jnp.int32, (8, 128), 0)
-    face, ends = meta[0], (meta[5] == 0, meta[6] == 0)
+    face, ends = meta[FACE], (meta[HAS_LOW] == 0, meta[HAS_HIGH] == 0)
     load = lambda c, t: q[c, :, 128 * t : 128 * t + 128]
     before_first, after_last = [], []
     for c in range(4):
@@ -235,33 +263,85 @@
     return added
 
 
-def edge_kernel(last, left, right, q, metric, one, two, three, mate, even_in, odd_in, meta, *rest):
+def partner_face(sent, main, low_ref, high_ref, from_low, from_high, meta, ghost_ref):
+    lane = lanes_of(LEN)
+    place = jnp.where(lane >= CROSS, lane - CROSS, lane)
+    along, across = meta[ALONG] == 1, meta[ACROSS] == 1
+    missing_low = jnp.where(along, meta[HAS_HIGH], meta[HAS_LOW]) == 0
+    missing_high = jnp.where(along, meta[HAS_LOW], meta[HAS_HIGH]) == 0
+    mirrored = jnp.where(lane < CROSS, CROSS - 1 - lane, jnp.where(lane < 2 * CROSS, 3 * CROSS - 1 - lane, lane))[:8]
+    stencils = []
+    for c in range(4):
+        mine = sent[LEN * c : LEN * c + LEN, :]
+        mine = jnp.where(across, gather_lanes(mine, mirrored), mine)
+        mine = jnp.where(along, reversed_rows(mine), mine)
+        here = main[LEN * c : LEN * c + LEN, :]
+        deep = main[DEEP + LEN * c : DEEP + LEN * c + LEN, :]
+        below, above = from_low[2 * c : 2 * c + 2, :], from_high[2 * c : 2 * c + 2, :]
+        low_ref[6:7, :] = jnp.where(missing_low, -SIGN[c] * here[1:2], jnp.where(along, above[1:2], below[0:1]))
+        low_ref[7:8, :] = jnp.where(missing_low, -SIGN[c] * here[0:1], jnp.where(along, above[0:1], below[1:2]))
+        high_ref[0:1, :] = jnp.where(missing_high, -SIGN[c] * here[15:16], jnp.where(along, below[1:2], above[0:1]))
+        high_ref[1:2, :] = jnp.where(missing_high, -SIGN[c] * here[14:15], jnp.where(along, below[0:1], above[1:2]))
+        rows = jnp.concatenate([low_ref[...], here, high_ref[...]], axis=0)
+        along_i = [shifted_rows(rows, s) for s in (-2, -1)] + [here] + [shifted_rows(rows, s) for s in (1, 2)]
+        outer = lane < CROSS
+        normal = [
+            jnp.where(outer, pltpu.roll(mine, 80, 1), pltpu.roll(mine, 48, 1)),
+            jnp.where(outer, mine, pltpu.roll(here, 48, 1)),
+            here,
+            jnp.where(outer, pltpu.roll(here, 80, 1), pltpu.roll(deep, 48, 1)),
+            deep,
+        ]
+        raw = [pltpu.roll(here, (-s) % 128, 1) if s else here for s in range(-2, 3)]
+        wall = SIGN[c] * here
+        second = SIGN[c] * jnp.where((place == 0) | (place == 46), raw[3], raw[1])
+        sideways = [
+            jnp.where(place < 2, second, raw[0]),
+            jnp.where(place == 0, wall, raw[1]),
+            here,
+            jnp.where(place == 47, wall, raw[3]),
+            jnp.where(place >= 46, second, raw[4]),
+        ]
+        stencils.append((along_i, normal, sideways))
+    geometry = [main[GEOMETRY + LEN * n : GEOMETRY + LEN * n + LEN, :] for n in range(9)]
+    for c, values in enumerate(advance(stencils, geometry)):
+        ghost_ref[LEN * c : LEN * c + LEN, :] = values
+
+
+def edge_kernel(last, q, metric, one, two, three, mate, even_in, odd_in, meta, *rest):
+    face = meta[FACE]
+    even = lax.rem(meta[POSITION], 2) == 0
+    received = (mate, one, two, three)
     if last:
-        out, low_ref, high_ref, ghost_ref = rest
+        bulk, sent, out, low_ref, high_ref, ghost_ref, main, first_low, first_high = rest
+        copy_part(meta[OWN], received, PARTS[0], main)
+        spare = slice(CELLS, CELLS + 128)
+        from_even, from_odd = even_in[:, spare], odd_in[:, spare]
+        partner_face(
+            sent, main, first_low, first_high,
+            jnp.where(even, from_odd, from_even), jnp.where(even, from_even, from_odd), meta, ghost_ref,
+        )
     else:
-        out, joint_ref, low_ref, high_ref, ghost_ref = rest
+        left, right, out, even_ref, odd_ref, low_ref, high_ref, ghost_ref, below, above = rest
+        copy_part(meta[OWN], received, (0, DEEP), ghost_ref)
+        copy_part(meta[OWN + 1], received, PARTS[1], below)
+        copy_part(meta[OWN + 2], received, PARTS[2], above)
     scale = 0.5 if last else 1.0
-    choice = meta[3]
-    for n, ref in enumerate((mate, one, two, three)):
-
-        @pl.when(choice == n)
-        def _(ref=ref):
-            ghost_ref[...] = ref[...]
-
-    face = meta[0]
-    even = lax.rem(meta[7], 2) == 0
-    has_low = jnp.where(meta[5] == 1, 1.0, 0.0)
-    has_high = jnp.where(meta[6] == 1, 1.0, 0.0)
+    has_low = jnp.where(meta[HAS_LOW] == 1, 1.0, 0.0)
+    has_high = jnp.where(meta[HAS_HIGH] == 1, 1.0, 0.0)
     for c in range(4):
         rows = slice(2 * c, 2 * c + 2)
-        from_even, from_odd = even_in[rows, :], odd_in[rows, :]
+        from_even, from_odd = even_in[rows, 0:CELLS], odd_in[rows, 0:CELLS]
         low_ref[c, 0:2, :] = has_low * jnp.where(even, from_odd, from_even)
         high_ref[c, 6:8, :] = has_high * jnp.where(even, from_even, from_odd)
 
     row = lax.broadcasted_iota(jnp.int32, (8, 128), 0)
     for t in range(TILES):
         where = slice(128 * t, 128 * t + 128)
-        part, place = (left, where) if t < HALF else (right, slice(128 * (t - HALF), 128 * (t - HALF) + 128))
+        if last:
+            part, place = bulk, where
+        else:
+            part, place = (left, where) if t < HALF else (right, slice(128 * (t - HALF), 128 * (t - HALF) + 128))
         for high in (False, True):
             half = slice(8, 16) if high else slice(0, 8)
             slopes, curves = [], []
@@ -336,62 +416,42 @@
             add(t, 2, slopes, curves)
 
     if not last:
-        write_joint(lambda c, t: out[c, :, 128 * t : 128 * t + 128], joint_ref, face, meta[1], meta[2])
+        write_chain(out, even_ref, odd_ref, meta[POSITION])
+        spare = slice(CELLS, CELLS + 128)
+        even_ref[:, spare] = jnp.where(even, above[...], below[...])
+        odd_ref[:, spare] = jnp.where(even, below[...], above[...])
 
 
 f32 = functools.partial(jax.ShapeDtypeStruct, dtype=jnp.float32)
 PARAMS = pltpu.CompilerParams(vmem_limit_bytes=24 * 1024 * 1024)
-WHOLE = pltpu.CompilerParams(vmem_limit_bytes=61 * 1024 * 1024)
 FIELD = f32((4, LEN, CELLS))
-JOINT = f32((64, 128))
-CHAINS = [f32((8, CELLS))] * 2
+JOINT = f32((ROWS, 128))
 HALO = [pltpu.VMEM((4, 8, CELLS), jnp.float32)] * 2 + [pltpu.VMEM((64, 128), jnp.float32)]
-
-
-def bulk(last, tiles, *operands):
-    shapes = [f32((4, LEN, 128 * len(tiles)))] + (CHAINS if tiles[0] == 0 else [])
+TILE = pltpu.VMEM((8, 128), jnp.float32)
+
+
+def local(kernel, shapes, operands, scratch=(), flops=1_000_000):
     return pl.pallas_call(
-        functools.partial(bulk_kernel, last, tiles),
+        kernel,
         out_shape=shapes,
         in_specs=[VMEM] * (len(operands) - 1) + [SMEM],
         out_specs=[VMEM] * len(shapes),
+        scratch_shapes=list(scratch),
         compiler_params=PARAMS,
-        cost_estimate=pl.CostEstimate(flops=6_000_000, bytes_accessed=6_000_000, transcendentals=0),
+        cost_estimate=pl.CostEstimate(flops=flops, bytes_accessed=flops, transcendentals=0),
     )(*operands)
 
 
-def edges(last, *operands):
-    shapes = [FIELD] + ([] if last else [JOINT])
-    return pl.pallas_call(
-        functools.partial(edge_kernel, last),
-        out_shape=shapes,
-        in_specs=[VMEM] * (len(operands) - 1) + [SMEM],
-        out_specs=[VMEM] * len(shapes),
-        scratch_shapes=HALO,
-        compiler_params=PARAMS,
-    )(*operands)
-
-
-def section(last, q, geometry, joint, first, meta):
-    kept = [first] if last else []
-    one, two, three = (
-        lax.ppermute(joint, "seg", [(i, i ^ s) for i in range(SEGS)]) for s in (1, 2, 3)
-    )
-    left, even, odd = bulk(last, range(HALF), q, geometry, *kept, meta)
-    one, two, three, even, odd = lax.optimization_barrier((one, two, three, even, odd))
+def bulk(last, tiles, chains, *operands):
+    shapes = [f32((4, LEN, 128 * len(tiles)))] + ([f32((8, CELLS))] * 2 if chains else [])
+    kernel = functools.partial(bulk_kernel, last, tiles)
+    return local(kernel, shapes, operands, flops=660_000 * len(tiles))
+
+
+def along_chain(even, odd):
     from_even = lax.ppermute(even, "blk", [(i, i ^ 1) for i in range(CHAIN)])
     pairs = [(i, i + 1) for i in range(1, CHAIN - 1, 2)]
-    from_odd = lax.ppermute(odd, "blk", pairs + [(b, a) for a, b in pairs])
-    picked = pl.pallas_call(
-        pick_kernel,
-        out_shape=JOINT,
-        in_specs=[VMEM] * 4 + [SMEM],
-        out_specs=VMEM,
-        compiler_params=PARAMS,
-    )(joint, one, two, three, meta)
-    mate = lax.ppermute(picked, "seg", [(i, i ^ 4) for i in range(SEGS)])
-    (right,) = bulk(last, range(HALF, TILES), q, geometry, *kept, meta)
-    return edges(last, left, right, q, geometry, one, two, three, mate, from_even, from_odd, meta)
+    return from_even, lax.ppermute(odd, "blk", pairs + [(b, a) for a, b in pairs])
 
 
 def on_device(state, metric, block_map, links):
@@ -400,7 +460,7 @@
     arrays = (state.reshape(4, LEN, CELLS), metric.reshape(9, LEN, CELLS), block_map, jnp.transpose(links, (1, 2, 0)))
     q, geometry, joint, meta = pl.pallas_call(
         first_kernel,
-        out_shape=[FIELD, f32((9, LEN, CELLS)), JOINT, jax.ShapeDtypeStruct((8,), jnp.int32)],
+        out_shape=[FIELD, f32((9, LEN, CELLS)), JOINT, jax.ShapeDtypeStruct((16,), jnp.int32)],
         in_specs=[HBM] * 4,
         out_specs=[VMEM] * 3 + [SMEM],
         scratch_shapes=[
@@ -410,8 +470,38 @@
         ],
         compiler_params=PARAMS,
     )(*map(held, arrays))
-    q1, joint = section(False, q, geometry, joint, None, meta)
-    (advanced,) = section(True, q1, geometry, joint, q, meta)
+    one, two, three = (
+        lax.ppermute(joint, "seg", [(i, i ^ s) for i in range(SEGS)]) for s in (1, 2, 3)
+    )
+    left, even, odd = bulk(False, range(HALF), True, q, geometry, meta)
+    one, two, three, even, odd = lax.optimization_barrier((one, two, three, even, odd))
+    from_even, from_odd = along_chain(even, odd)
+    (picked,) = local(pick_kernel, [JOINT], (joint, one, two, three, meta))
+    mate = lax.ppermute(picked, "seg", [(i, i ^ 4) for i in range(SEGS)])
+    (right,) = bulk(False, range(HALF, TILES), False, q, geometry, meta)
+    kernel = functools.partial(edge_kernel, False)
+
+    def first_edges(left, right, *operands):
+        return kernel(*operands[:9], left, right, *operands[9:])
+
+    q1, even, odd = local(
+        first_edges,
+        [FIELD] + [f32((8, CELLS + 128))] * 2,
+        (left, right, q, geometry, one, two, three, mate, from_even, from_odd, meta),
+        HALO + [TILE] * 2,
+    )
+    from_even, from_odd = along_chain(even, odd)
+    (part,) = bulk(True, range(TILES), False, q1, geometry, q, meta)
+
+    def last_edges(part, sent, *operands):
+        return edge_kernel(True, *operands[:9], part, sent, *operands[9:])
+
+    (advanced,) = local(
+        last_edges,
+        [FIELD],
+        (part, joint, q1, geometry, one, two, three, mate, from_even, from_odd, meta),
+        HALO + [pltpu.VMEM((BELOW, 128), jnp.float32)] + [TILE] * 2,
+    )
     return advanced.reshape(state.shape)
 
 

time: 41.4 us -> 37.2 us (0.90); the launches traced: 41.6 us -> 36.8 us
  starting transfers between devices: 23.7 us -> 18.9 us
  Pallas kernels: 14.2 us -> 13.1 us
  waiting for transfers between devices: 3.61 us -> 4.66 us
    ppermute x12 -> x8, starting transfers between devices: 23.7 us -> 18.9 us  [the longest x2 10.9 us: along_chain(): lax.ppermute(odd, 'blk', pairs + [(b, a) for a, b in pairs])]
    pallas_call x8 -> x6, Pallas kernels: 12 us -> 10.6 us  [local(): pl.pallas_call(kernel, out_shape=shapes, in_specs=[VMEM] * (len(operands)...]
    ppermute x12 -> x8, waiting for transfers between devices: 3.61 us -> 4.66 us  [the longest x3 4.22 us: on_device(): lax.ppermute(joint, 'seg', [(i, i ^ s) for i in range(SEGS)])]
  transfers between devices with their start and end apart: 12 -> 8, of which waited for: 4 -> 3; matrix products, arithmetic and copies ran while one was open for 0% -> 0% of each run, Pallas kernels for 21% -> 19%
where the time goes in v4:
time: 37.2 us; the launch traced here: 36.8 us
  starting transfers between devices  18.9 us (51%)
  Pallas kernels  13.1 us (35%)
  waiting for transfers between devices  4.66 us (13%)
    ppermute x2, starting transfers between devices, along_chain(): lax.ppermute(odd, 'blk', pairs + [(b, a) for a, b in pairs])  10.9 us
    pallas_call x6, Pallas kernels, local(): pl.pallas_call(kernel, out_shape=shapes, in_specs=[VMEM] * (len(operands)...  10.6 us
    ppermute x3, waiting for transfers between devices, on_device(): lax.ppermute(joint, 'seg', [(i, i ^ s) for i in range(SEGS)])  4.22 us
    ppermute x3, starting transfers between devices, on_device(): lax.ppermute(joint, 'seg', [(i, i ^ s) for i in range(SEGS)])  3.34 us
    ppermute x2, starting transfers between devices, along_chain(): from_even = lax.ppermute(even, 'blk', [(i, i ^ 1) for i in range(CHAIN)])  2.65 us
    pallas_call x1, Pallas kernels, on_device(): pl.pallas_call(first_kernel, out_shape=[FIELD, f32((9, LEN, CELLS)), JOIN...  2.45 us
    ppermute x1, starting transfers between devices, on_device(): mate = lax.ppermute(picked, 'seg', [(i, i ^ 4) for i in range(SEGS)])  2.1 us
  transfers between devices with their start and end apart: 8, of which 3 were waited for; matrix products, arithmetic and copies ran while one was open for 0% of the time, Pallas kernels for 19%

profile of v4, /device:TPU:105, one launch (start us, length us, event | category | flops | bytes accessed | tf_op | source)
XLA Modules:
  0.0 36.8 jit_solution(15101909772407685293)
XLA Ops:
  0.0 2.5 %shard_map.46 = (f32[4,16,2304]{2,1,0:T(8,128)S(1)}, f32[9,16,2304]{2,1,0:T(8,128)S(1)}, f32[288,128]{1,0:T(8,128)S(1)}, s32[16]{0:T(128)S(1)}) custom-call(f32[4,16,2304]{2,1,0:T(8,128)} %bitcast.5, f32[9,16,2304]{2,1,0:T(8,128)} %bitcast.4, s32[256]{0:T(256)} %map_hbm.1, s32[6,4,256]{2,1,0:T(4,128)} %bitcast.6), custom_call_target="tpu_custom_call" | custom-call | tf_op jit(solution)/shard_map/pallas_call | solution.py:461
  2.5 2.6 %collective-permute-start.2 = (f32[288,128]{1,0:T(8,128)S(1)}, f32[288,128]{1,0:T(8,128)S(1)}, u32[]{:S(2)}, u32[]{:S(2)}) collective-permute-start(f32[288,128]{1,0:T(8,128)S(1)} %get-tuple-element.24.own.sent), channel_id=1, source_target_pairs={{0,96},{32,64},{64,32},{96,0},{128,224},{160,192},{192,160},{224,1... | collective-permute-start | bytes 442376 | tf_op jit(solution)/shard_map/ppermute | solution.py:474
  5.0 0.5 %collective-permute-start.1 = (f32[288,128]{1,0:T(8,128)S(1)}, f32[288,128]{1,0:T(8,128)S(1)}, u32[]{:S(2)}, u32[]{:S(2)}) collective-permute-start(f32[288,128]{1,0:T(8,128)S(1)} %get-tuple-element.24.own.sent), channel_id=1, source_target_pairs={{0,64},{32,96},{64,0},{96,32},{128,192},{160,224},{192,128},{224,1... | collective-permute-start | bytes 442376 | tf_op jit(solution)/shard_map/ppermute | solution.py:474
  5.5 0.3 collective-permute-start
  5.8 2.0 %shard_map.47 = (f32[4,16,1152]{2,1,0:T(8,128)S(1)}, f32[8,2304]{1,0:T(8,128)S(1)}, f32[8,2304]{1,0:T(8,128)S(1)}) custom-call(f32[4,16,2304]{2,1,0:T(8,128)S(1)} %get-tuple-element.20.q.operands_0_.rest_0_, f32[9,16,2304]{2,1,0:T(8,128)S(1)} %get-tuple-element.21.metric.operands_1_, s32[16]{0:T(128)S(1)} %get-tuple-element.22.rest_0_.meta.operands_8_.rest_1_), custom_call_target="tpu_custom_call" | custom-call | flops 5940000 | bytes 5940000 | tf_op jit(solution)/shard_map/pallas_call | solution.py:434
  7.8 3.3 %collective-permute-done.2.three.operands_4_ = f32[288,128]{1,0:T(8,128)S(1)} collective-permute-done((f32[288,128]{1,0:T(8,128)S(1)}, f32[288,128]{1,0:T(8,128)S(1)}, u32[]{:S(2)}, u32[]{:S(2)}) %collective-permute-start.2) | collective-permute-done | bytes 147488 | tf_op jit(solution)/shard_map/ppermute | solution.py:474
  11.1 0.0 collective-permute-done.1.two.operands_3_
  11.1 0.9 %collective-permute-done.one.operands_2_ = f32[288,128]{1,0:T(8,128)S(1)} collective-permute-done((f32[288,128]{1,0:T(8,128)S(1)}, f32[288,128]{1,0:T(8,128)S(1)}, u32[]{:S(2)}, u32[]{:S(2)}) %collective-permute-start) | collective-permute-done | bytes 147488 | tf_op jit(solution)/shard_map/ppermute | solution.py:474
  12.0 0.6 %shard_map.49 = f32[288,128]{1,0:T(8,128)S(1)} custom-call(f32[288,128]{1,0:T(8,128)S(1)} %get-tuple-element.24.own.sent, f32[288,128]{1,0:T(8,128)S(1)} %collective-permute-done.one.operands_2_, f32[288,128]{1,0:T(8,128)S(1)} %collective-permute-done.1.two.operands_3_, f32[288,128]{1,0:T(8,128)S(1)} %collective-permute-done.2.three.operands_4_, ...), custom_call_target="tpu_custom_call" | custom-call | flops 1000000 | bytes 1000000 | tf_op jit(solution)/shard_map/pallas_call | solution.py:434
  12.6 2.1 %collective-permute-start.3 = (f32[288,128]{1,0:T(8,128)S(1)}, f32[288,128]{1,0:T(8,128)S(1)}, u32[]{:S(2)}, u32[]{:S(2)}) collective-permute-start(f32[288,128]{1,0:T(8,128)S(1)} %shard_map.49), channel_id=1, source_target_pairs={{0,128},{32,160},{64,192},{96,224},{128,0},{160,32},{192,64},{224,... | collective-permute-start | bytes 442376 | tf_op jit(solution)/shard_map/ppermute | solution.py:480
  14.7 2.6 %collective-permute-start.4 = (f32[8,2304]{1,0:T(8,128)S(1)}, f32[8,2304]{1,0:T(8,128)S(1)}, u32[]{:S(2)}, u32[]{:S(2)}) collective-permute-start(f32[8,2304]{1,0:T(8,128)S(1)} %get-tuple-element.30), channel_id=1, source_target_pairs={{0,1},{1,0},{2,3},{3,2},{4,5},{5,4},{6,7},{7,6},{8,9},{9,8},{10,11... | collective-permute-start | bytes 221192 | tf_op jit(solution)/shard_map/ppermute | solution.py:452
  17.3 5.4 %collective-permute-start.5 = (f32[8,2304]{1,0:T(8,128)S(1)}, f32[8,2304]{1,0:T(8,128)S(1)}, u32[]{:S(2)}, u32[]{:S(2)}) collective-permute-start(f32[8,2304]{1,0:T(8,128)S(1)} %get-tuple-element.31), channel_id=1, source_target_pairs={{1,2},{3,4},{5,6},{7,8},{9,10},{11,12},{13,14},{15,16},{17,18},{19... | collective-permute-start | bytes 221192 | tf_op jit(solution)/shard_map/ppermute | solution.py:454
  22.7 1.9 %shard_map.48.right = f32[4,16,1152]{2,1,0:T(8,128)S(1)} custom-call(f32[4,16,2304]{2,1,0:T(8,128)S(1)} %get-tuple-element.20.q.operands_0_.rest_0_, f32[9,16,2304]{2,1,0:T(8,128)S(1)} %get-tuple-element.21.metric.operands_1_, s32[16]{0:T(128)S(1)} %get-tuple-element.22.rest_0_.meta.operands_8_.rest_1_), custom_call_target="tpu_custom_call" | custom-call | flops 5940000 | bytes 5940000 | tf_op jit(solution)/shard_map/pallas_call | solution.py:434
  24.6 0.0 collective-permute-done.4.operands_6_
  24.6 0.4 %collective-permute-done.5.operands_7_ = f32[8,2304]{1,0:T(8,128)S(1)} collective-permute-done((f32[8,2304]{1,0:T(8,128)S(1)}, f32[8,2304]{1,0:T(8,128)S(1)}, u32[]{:S(2)}, u32[]{:S(2)}) %collective-permute-start.5) | collective-permute-done | bytes 73760 | tf_op jit(solution)/shard_map/ppermute | solution.py:454
  25.0 0.0 collective-permute-done.3.operands_5_
  25.0 1.1 %shard_map.50 = (f32[4,16,2304]{2,1,0:T(8,128)S(1)}, f32[8,2432]{1,0:T(8,128)S(1)}, f32[8,2432]{1,0:T(8,128)S(1)}) custom-call(f32[4,16,1152]{2,1,0:T(8,128)S(1)} %get-tuple-element.23.left, f32[4,16,1152]{2,1,0:T(8,128)S(1)} %shard_map.48.right, f32[4,16,2304]{2,1,0:T(8,128)S(1)} %get-tuple-element.20.q.operands_0_.rest_0_, ...), custom_call_target="tpu_custom_call" | custom-call | flops 1000000 | bytes 1000000 | tf_op jit(solution)/shard_map/pallas_call | solution.py:434
  26.1 0.1 collective-permute-start.6
  26.2 5.4 %collective-permute-start.7 = (f32[8,2432]{1,0:T(8,128)S(1)}, f32[8,2432]{1,0:T(8,128)S(1)}, u32[]{:S(2)}, u32[]{:S(2)}) collective-permute-start(f32[8,2432]{1,0:T(8,128)S(1)} %get-tuple-element.34), channel_id=1, source_target_pairs={{1,2},{3,4},{5,6},{7,8},{9,10},{11,12},{13,14},{15,16},{17,18},{19... | collective-permute-start | bytes 233480 | tf_op jit(solution)/shard_map/ppermute | solution.py:454
  31.7 3.2 %shard_map.51.part = f32[4,16,2304]{2,1,0:T(8,128)S(1)} custom-call(f32[4,16,2304]{2,1,0:T(8,128)S(1)} %get-tuple-element.32.q.operands_0_, f32[9,16,2304]{2,1,0:T(8,128)S(1)} %get-tuple-element.21.metric.operands_1_, f32[4,16,2304]{2,1,0:T(8,128)S(1)} %get-tuple-element.20.q.operands_0_.rest_0_, s32[16]{0:T(128)S(1)} %get-tuple-element.22.rest_0_.meta.operands_8_.rest_1_), custom_call_target="tpu_custom_call" | custom-call | flops 11880000 | bytes 11880000 | tf_op jit(solution)/shard_map/pallas_call | solution.py:434
  34.8 0.0 collective-permute-done.6.operands_6_
  34.8 0.0 collective-permute-done.7.operands_7_
  34.9 1.9 %shard_map.52 = f32[4,16,2304]{2,1,0:T(8,128)} custom-call(f32[4,16,2304]{2,1,0:T(8,128)S(1)} %shard_map.51.part, f32[288,128]{1,0:T(8,128)S(1)} %get-tuple-element.24.own.sent, f32[4,16,2304]{2,1,0:T(8,128)S(1)} %get-tuple-element.32.q.operands_0_, f32[9,16,2304]{2,1,0:T(8,128)S(1)} %get-tuple-element.21.metric.operands_1_, ...), custom_call_target="tpu_custom_call" | custom-call | flops 1000000 | bytes 1000000 | tf_op jit(solution)/shard_map/pallas_call | solution.py:434
Async XLA Ops:
  2.5 8.6 %collective-permute-start.2 = (f32[288,128]{1,0:T(8,128)S(1)}, f32[288,128]{1,0:T(8,128)S(1)}, u32[]{:S(2)}, u32[]{:S(2)}) collective-permute-start(f32[288,128]{1,0:T(8,128)S(1)} %get-tuple-element.24.own.sent), channel_id=1, source_target_pairs={{0,96},{32,64},{64,32},{96,0},{128,224},{160,192},{192,160},{224,1... | collective-permute-start | bytes 442376 | tf_op jit(solution)/shard_map/ppermute | solution.py:474
  5.0 6.1 %collective-permute-start.1 = (f32[288,128]{1,0:T(8,128)S(1)}, f32[288,128]{1,0:T(8,128)S(1)}, u32[]{:S(2)}, u32[]{:S(2)}) collective-permute-start(f32[288,128]{1,0:T(8,128)S(1)} %get-tuple-element.24.own.sent), channel_id=1, source_target_pairs={{0,64},{32,96},{64,0},{96,32},{128,192},{160,224},{192,128},{224,1... | collective-permute-start | bytes 442376 | tf_op jit(solution)/shard_map/ppermute | solution.py:474
  5.5 6.4 %collective-permute-start = (f32[288,128]{1,0:T(8,128)S(1)}, f32[288,128]{1,0:T(8,128)S(1)}, u32[]{:S(2)}, u32[]{:S(2)}) collective-permute-start(f32[288,128]{1,0:T(8,128)S(1)} %get-tuple-element.24.own.sent), channel_id=1, source_target_pairs={{0,32},{32,0},{64,96},{96,64},{128,160},{160,128},{192,224},{224,1... | collective-permute-start | bytes 442376 | tf_op jit(solution)/shard_map/ppermute | solution.py:474
  12.6 12.4 %collective-permute-start.3 = (f32[288,128]{1,0:T(8,128)S(1)}, f32[288,128]{1,0:T(8,128)S(1)}, u32[]{:S(2)}, u32[]{:S(2)}) collective-permute-start(f32[288,128]{1,0:T(8,128)S(1)} %shard_map.49), channel_id=1, source_target_pairs={{0,128},{32,160},{64,192},{96,224},{128,0},{160,32},{192,64},{224,... | collective-permute-start | bytes 442376 | tf_op jit(solution)/shard_map/ppermute | solution.py:480
  14.7 9.9 %collective-permute-start.4 = (f32[8,2304]{1,0:T(8,128)S(1)}, f32[8,2304]{1,0:T(8,128)S(1)}, u32[]{:S(2)}, u32[]{:S(2)}) collective-permute-start(f32[8,2304]{1,0:T(8,128)S(1)} %get-tuple-element.30), channel_id=1, source_target_pairs={{0,1},{1,0},{2,3},{3,2},{4,5},{5,4},{6,7},{7,6},{8,9},{9,8},{10,11... | collective-permute-start | bytes 221192 | tf_op jit(solution)/shard_map/ppermute | solution.py:452
  17.3 7.8 %collective-permute-start.5 = (f32[8,2304]{1,0:T(8,128)S(1)}, f32[8,2304]{1,0:T(8,128)S(1)}, u32[]{:S(2)}, u32[]{:S(2)}) collective-permute-start(f32[8,2304]{1,0:T(8,128)S(1)} %get-tuple-element.31), channel_id=1, source_target_pairs={{1,2},{3,4},{5,6},{7,8},{9,10},{11,12},{13,14},{15,16},{17,18},{19... | collective-permute-start | bytes 221192 | tf_op jit(solution)/shard_map/ppermute | solution.py:454
  26.1 8.7 %collective-permute-start.6 = (f32[8,2432]{1,0:T(8,128)S(1)}, f32[8,2432]{1,0:T(8,128)S(1)}, u32[]{:S(2)}, u32[]{:S(2)}) collective-permute-start(f32[8,2432]{1,0:T(8,128)S(1)} %get-tuple-element.33), channel_id=1, source_target_pairs={{0,1},{1,0},{2,3},{3,2},{4,5},{5,4},{6,7},{7,6},{8,9},{9,8},{10,11... | collective-permute-start | bytes 233480 | tf_op jit(solution)/shard_map/ppermute | solution.py:452
  26.2 8.6 %collective-permute-start.7 = (f32[8,2432]{1,0:T(8,128)S(1)}, f32[8,2432]{1,0:T(8,128)S(1)}, u32[]{:S(2)}, u32[]{:S(2)}) collective-permute-start(f32[8,2432]{1,0:T(8,128)S(1)} %get-tuple-element.34), channel_id=1, source_target_pairs={{1,2},{3,4},{5,6},{7,8},{9,10},{11,12},{13,14},{15,16},{17,18},{19... | collective-permute-start | bytes 233480 | tf_op jit(solution)/shard_map/ppermute | solution.py:454

commit v5 on v4

--- a/solution.py
+++ b/solution.py
@@ -7,8 +7,9 @@
 from jax.sharding import PartitionSpec as P
 
 LEN, CROSS, CELLS, TILES = 16, 48, 2304, 18
-HALF = 9
-DEEP, GEOMETRY, BELOW, ABOVE, ROWS = 64, 128, 272, 280, 288
+GROUP = 6
+GEOMETRY, BELOW, ABOVE, ROWS = 64, 208, 216, 224
+USED, SPARE = 96, 32
 FACE, ALONG, ACROSS, POSITION, HAS_LOW, HAS_HIGH, OWN, MATE = 0, 1, 2, 3, 4, 5, 6, 9
 PARTS = ((0, BELOW), (BELOW, ABOVE), (ABOVE, ROWS))
 SEGS, CHAIN = 8, 32
@@ -120,15 +121,20 @@
         meta[MATE + n] = (mates[n] ^ segment) & 3
     copies[2].wait()
 
-    def put(start, values):
-        joint_ref[start : start + LEN, :] = jnp.where(along == 1, reversed_rows(values), values)
-
     where = lambda t: slice(128 * t, 128 * t + 128)
+    lane = lanes_of(LEN)
     near, deep = face_source(face, across, 0), face_source(face, across, 2)
     below, above = face_source(low_face, low_across, 0), face_source(high_face, high_across, 0)
+    deeper = [gather_face(lambda t: q[c, :, where(t)], deep) for c in range(4)]
+
+    def put(n, values):
+        if n < 12:
+            third = pltpu.roll(deeper[n // 3], USED - SPARE * (n % 3), 1)
+            values = jnp.where(lane < USED, values, third)
+        joint_ref[LEN * n : LEN * n + LEN, :] = jnp.where(along == 1, reversed_rows(values), values)
+
     for c in range(4):
-        put(LEN * c, gather_face(lambda t: q[c, :, where(t)], near))
-        put(DEEP + LEN * c, gather_face(lambda t: q[c, :, where(t)], deep))
+        put(c, gather_face(lambda t: q[c, :, where(t)], near))
         low_rows = gather_face(lambda t: q[c, 0:8, where(t)], below)
         joint_ref[BELOW + 2 * c : BELOW + 2 * c + 2, :] = low_rows[0:2]
         high_rows = gather_face(lambda t: q[c, 8:16, where(t)], above)
@@ -141,7 +147,7 @@
     for a, (row, sign) in enumerate(((0, forward), (3 * normal, inward), (3 * (3 - normal), sideways))):
         for b in range(3):
             found = gather_face(lambda t: metric[row + b, :, where(t)], near)
-            put(GEOMETRY + LEN * (3 * a + b), sign * found)
+            put(4 + 3 * a + b, sign * found)
 
 
 def copy_part(choice, refs, rows, out):
@@ -198,7 +204,7 @@
     return result
 
 
-def bulk_kernel(last, tiles, q, metric, *rest):
+def bulk_kernel(last, q, metric, *rest):
     first, rest = (rest[0], rest[1:]) if last else (None, rest)
     meta, out = rest[:2]
     if len(rest) == 4:
@@ -221,7 +227,7 @@
     high_scale = jnp.where(face == 5, 0.0, 1.0)
     open_low = jnp.where(ends[0], 1.0, 0.0)
     open_high = jnp.where(ends[1], 1.0, 0.0)
-    for t in tiles:
+    for t in range(TILES):
         flat = 128 * t + lane
         k = flat - (flat // CROSS) * CROSS
         scale = jnp.where(k < 2, low_scale, high_scale)
@@ -250,7 +256,7 @@
         values = advance(stencils, [metric[n, :, where] for n in range(9)])
         for c in range(4):
             kept = 0.5 * first[c, :, where] + 0.5 * values[c] if last else values[c]
-            out[c, :, 128 * (t - tiles[0]) : 128 * (t - tiles[0]) + 128] = kept
+            out[c, :, where] = kept
 
 
 def edge_terms(here, geometry, slopes, curves, scale):
@@ -276,7 +282,10 @@
         mine = jnp.where(across, gather_lanes(mine, mirrored), mine)
         mine = jnp.where(along, reversed_rows(mine), mine)
         here = main[LEN * c : LEN * c + LEN, :]
-        deep = main[DEEP + LEN * c : DEEP + LEN * c + LEN, :]
+        thirds = [
+            pltpu.roll(main[LEN * n : LEN * n + LEN, :], (SPARE * (n % 3) - USED) % 128, 1) for n in range(3 * c, 3 * c + 3)
+        ]
+        deep = jnp.where(lane < SPARE, thirds[0], jnp.where(lane < 2 * SPARE, thirds[1], thirds[2]))
         below, above = from_low[2 * c : 2 * c + 2, :], from_high[2 * c : 2 * c + 2, :]
         low_ref[6:7, :] = jnp.where(missing_low, -SIGN[c] * here[1:2], jnp.where(along, above[1:2], below[0:1]))
         low_ref[7:8, :] = jnp.where(missing_low, -SIGN[c] * here[0:1], jnp.where(along, above[0:1], below[1:2]))
@@ -308,40 +317,10 @@
         ghost_ref[LEN * c : LEN * c + LEN, :] = values
 
 
-def edge_kernel(last, q, metric, one, two, three, mate, even_in, odd_in, meta, *rest):
-    face = meta[FACE]
-    even = lax.rem(meta[POSITION], 2) == 0
-    received = (mate, one, two, three)
-    if last:
-        bulk, sent, out, low_ref, high_ref, ghost_ref, main, first_low, first_high = rest
-        copy_part(meta[OWN], received, PARTS[0], main)
-        spare = slice(CELLS, CELLS + 128)
-        from_even, from_odd = even_in[:, spare], odd_in[:, spare]
-        partner_face(
-            sent, main, first_low, first_high,
-            jnp.where(even, from_odd, from_even), jnp.where(even, from_even, from_odd), meta, ghost_ref,
-        )
-    else:
-        left, right, out, even_ref, odd_ref, low_ref, high_ref, ghost_ref, below, above = rest
-        copy_part(meta[OWN], received, (0, DEEP), ghost_ref)
-        copy_part(meta[OWN + 1], received, PARTS[1], below)
-        copy_part(meta[OWN + 2], received, PARTS[2], above)
-    scale = 0.5 if last else 1.0
-    has_low = jnp.where(meta[HAS_LOW] == 1, 1.0, 0.0)
-    has_high = jnp.where(meta[HAS_HIGH] == 1, 1.0, 0.0)
-    for c in range(4):
-        rows = slice(2 * c, 2 * c + 2)
-        from_even, from_odd = even_in[rows, 0:CELLS], odd_in[rows, 0:CELLS]
-        low_ref[c, 0:2, :] = has_low * jnp.where(even, from_odd, from_even)
-        high_ref[c, 6:8, :] = has_high * jnp.where(even, from_even, from_odd)
-
+def chain_terms(q, metric, low_ref, high_ref, scale, tiles, base, out):
     row = lax.broadcasted_iota(jnp.int32, (8, 128), 0)
-    for t in range(TILES):
+    for t in tiles:
         where = slice(128 * t, 128 * t + 128)
-        if last:
-            part, place = bulk, where
-        else:
-            part, place = (left, where) if t < HALF else (right, slice(128 * (t - HALF), 128 * (t - HALF) + 128))
         for high in (False, True):
             half = slice(8, 16) if high else slice(0, 8)
             slopes, curves = [], []
@@ -360,8 +339,10 @@
             here = [q[c, half, where] for c in range(4)]
             added = edge_terms(here, [metric[n, half, where] for n in range(3)], slopes, curves, scale)
             for c in range(4):
-                out[c, half, where] = part[c, half, place] + added[c]
-
+                out[c, half, where] = base[c, half, where] + added[c]
+
+
+def joint_terms(q, metric, ghost_ref, face, scale, tiles, out):
     lane = lanes_of(LEN)
 
     def add(t, direction, slopes, curves):
@@ -373,34 +354,37 @@
             out[c, :, where] = out[c, :, where] + added[c]
 
     ghost_of = lambda c: ghost_ref[16 * c : 16 * c + 16, :]
-
-    @pl.when(face == 2)
-    def _():
-        slopes, curves = [], []
-        for c in range(4):
-            ghost = ghost_of(c)
-            first = jnp.where(lane < CROSS, ghost, 0.0)
-            second = jnp.where(lane < CROSS, pltpu.roll(ghost, 80, 1), pltpu.roll(ghost, 48, 1))
-            second = jnp.where(lane < 2 * CROSS, second, 0.0)
-            slopes.append(second - 8.0 * first)
-            curves.append(16.0 * first - second)
-        add(0, 1, slopes, curves)
-
-    @pl.when(face == 3)
-    def _():
-        slopes, curves = [], []
-        for c in range(4):
-            ghost = ghost_of(c)
-            first = jnp.where(lane >= 80, pltpu.roll(ghost, 80, 1), 0.0)
-            second = jnp.where(lane >= 32, pltpu.roll(ghost, 32, 1), 0.0)
-            slopes.append(8.0 * first - second)
-            curves.append(16.0 * first - second)
-        add(TILES - 1, 1, slopes, curves)
+    if tiles[0] == 0:
+
+        @pl.when(face == 2)
+        def _():
+            slopes, curves = [], []
+            for c in range(4):
+                ghost = ghost_of(c)
+                first = jnp.where(lane < CROSS, ghost, 0.0)
+                second = jnp.where(lane < CROSS, pltpu.roll(ghost, 80, 1), pltpu.roll(ghost, 48, 1))
+                second = jnp.where(lane < 2 * CROSS, second, 0.0)
+                slopes.append(second - 8.0 * first)
+                curves.append(16.0 * first - second)
+            add(0, 1, slopes, curves)
+
+    if tiles[-1] == TILES - 1:
+
+        @pl.when(face == 3)
+        def _():
+            slopes, curves = [], []
+            for c in range(4):
+                ghost = ghost_of(c)
+                first = jnp.where(lane >= 80, pltpu.roll(ghost, 80, 1), 0.0)
+                second = jnp.where(lane >= 32, pltpu.roll(ghost, 32, 1), 0.0)
+                slopes.append(8.0 * first - second)
+                curves.append(16.0 * first - second)
+            add(TILES - 1, 1, slopes, curves)
 
     @pl.when(face >= 4)
     def _():
         toward = jnp.where(face == 4, -1.0, 1.0)
-        for t in range(TILES):
+        for t in tiles:
             flat = 128 * t + lane
             j = flat // CROSS
             k = flat - j * CROSS
@@ -415,11 +399,56 @@
                 curves.append(16.0 * first - second)
             add(t, 2, slopes, curves)
 
-    if not last:
-        write_chain(out, even_ref, odd_ref, meta[POSITION])
-        spare = slice(CELLS, CELLS + 128)
-        even_ref[:, spare] = jnp.where(even, above[...], below[...])
-        odd_ref[:, spare] = jnp.where(even, below[...], above[...])
+
+def joint_kernel(bulk, q, metric, one, two, three, mate, meta, out, below_out, above_out, ghost_ref):
+    received = (mate, one, two, three)
+    copy_part(meta[OWN], received, (0, GEOMETRY), ghost_ref)
+    copy_part(meta[OWN + 1], received, PARTS[1], below_out)
+    copy_part(meta[OWN + 2], received, PARTS[2], above_out)
+    out[...] = bulk[...]
+    joint_terms(q, metric, ghost_ref, meta[FACE], 1.0, range(TILES), out)
+
+
+def spread_ghosts(even_in, odd_in, meta, low_ref, high_ref):
+    even = lax.rem(meta[POSITION], 2) == 0
+    has_low = jnp.where(meta[HAS_LOW] == 1, 1.0, 0.0)
+    has_high = jnp.where(meta[HAS_HIGH] == 1, 1.0, 0.0)
+    for c in range(4):
+        rows = slice(2 * c, 2 * c + 2)
+        from_even, from_odd = even_in[rows, 0:CELLS], odd_in[rows, 0:CELLS]
+        low_ref[c, 0:2, :] = has_low * jnp.where(even, from_odd, from_even)
+        high_ref[c, 6:8, :] = has_high * jnp.where(even, from_even, from_odd)
+
+
+def chain_kernel(part, q, metric, below, above, even_in, odd_in, meta, out, even_ref, odd_ref, low_ref, high_ref):
+    spread_ghosts(even_in, odd_in, meta, low_ref, high_ref)
+    chain_terms(q, metric, low_ref, high_ref, 1.0, range(TILES), part, out)
+    write_chain(out, even_ref, odd_ref, meta[POSITION])
+    even = lax.rem(meta[POSITION], 2) == 0
+    spare = slice(CELLS, CELLS + 128)
+    even_ref[:, spare] = jnp.where(even, above[...], below[...])
+    odd_ref[:, spare] = jnp.where(even, below[...], above[...])
+
+
+def last_kernel(part, sent, q, metric, one, two, three, mate, even_in, odd_in, meta, out_hbm, *scratch):
+    low_ref, high_ref, ghost_ref, main, first_low, first_high, out, sem = scratch
+    even = lax.rem(meta[POSITION], 2) == 0
+    copy_part(meta[OWN], (mate, one, two, three), PARTS[0], main)
+    spare = slice(CELLS, CELLS + 128)
+    from_even, from_odd = even_in[:, spare], odd_in[:, spare]
+    from_low, from_high = jnp.where(even, from_odd, from_even), jnp.where(even, from_even, from_odd)
+    partner_face(sent, main, first_low, first_high, from_low, from_high, meta, ghost_ref)
+    spread_ghosts(even_in, odd_in, meta, low_ref, high_ref)
+    copies = []
+    for n in range(TILES // GROUP):
+        tiles = range(GROUP * n, GROUP * n + GROUP)
+        chain_terms(q, metric, low_ref, high_ref, 0.5, tiles, part, out)
+        joint_terms(q, metric, ghost_ref, meta[FACE], 0.5, tiles, out)
+        where = slice(128 * GROUP * n, 128 * GROUP * (n + 1))
+        copies.append(pltpu.make_async_copy(out.at[:, :, where], out_hbm.at[:, :, where], sem.at[n]))
+        copies[-1].start()
+    for copy in copies:
+        copy.wait()
 
 
 f32 = functools.partial(jax.ShapeDtypeStruct, dtype=jnp.float32)
@@ -430,22 +459,22 @@
 TILE = pltpu.VMEM((8, 128), jnp.float32)
 
 
-def local(kernel, shapes, operands, scratch=(), flops=1_000_000):
+def local(kernel, shapes, operands, scratch=(), flops=1_000_000, **options):
+    options.setdefault("out_specs", [VMEM] * len(shapes))
     return pl.pallas_call(
         kernel,
         out_shape=shapes,
         in_specs=[VMEM] * (len(operands) - 1) + [SMEM],
-        out_specs=[VMEM] * len(shapes),
         scratch_shapes=list(scratch),
         compiler_params=PARAMS,
         cost_estimate=pl.CostEstimate(flops=flops, bytes_accessed=flops, transcendentals=0),
+        **options,
     )(*operands)
 
 
-def bulk(last, tiles, chains, *operands):
-    shapes = [f32((4, LEN, 128 * len(tiles)))] + ([f32((8, CELLS))] * 2 if chains else [])
-    kernel = functools.partial(bulk_kernel, last, tiles)
-    return local(kernel, shapes, operands, flops=660_000 * len(tiles))
+def bulk(last, chains, *operands):
+    shapes = [FIELD] + ([f32((8, CELLS))] * 2 if chains else [])
+    return local(functools.partial(bulk_kernel, last), shapes, operands, flops=12_000_000)
 
 
 def along_chain(even, odd):
@@ -473,34 +502,33 @@
     one, two, three = (
         lax.ppermute(joint, "seg", [(i, i ^ s) for i in range(SEGS)]) for s in (1, 2, 3)
     )
-    left, even, odd = bulk(False, range(HALF), True, q, geometry, meta)
-    one, two, three, even, odd = lax.optimization_barrier((one, two, three, even, odd))
-    from_even, from_odd = along_chain(even, odd)
+    part, even, odd = bulk(False, True, q, geometry, meta)
+    one, two, three, even, odd, part = lax.optimization_barrier((one, two, three, even, odd, part))
     (picked,) = local(pick_kernel, [JOINT], (joint, one, two, three, meta))
     mate = lax.ppermute(picked, "seg", [(i, i ^ 4) for i in range(SEGS)])
-    (right,) = bulk(False, range(HALF, TILES), False, q, geometry, meta)
-    kernel = functools.partial(edge_kernel, False)
-
-    def first_edges(left, right, *operands):
-        return kernel(*operands[:9], left, right, *operands[9:])
-
+    from_even, from_odd = along_chain(even, odd)
+    part, below, above = local(
+        joint_kernel,
+        [FIELD] + [f32((8, 128))] * 2,
+        (part, q, geometry, one, two, three, mate, meta),
+        HALO[2:],
+    )
     q1, even, odd = local(
-        first_edges,
+        chain_kernel,
         [FIELD] + [f32((8, CELLS + 128))] * 2,
-        (left, right, q, geometry, one, two, three, mate, from_even, from_odd, meta),
-        HALO + [TILE] * 2,
+        (part, q, geometry, below, above, from_even, from_odd, meta),
+        HALO[:2],
     )
     from_even, from_odd = along_chain(even, odd)
-    (part,) = bulk(True, range(TILES), False, q1, geometry, q, meta)
-
-    def last_edges(part, sent, *operands):
-        return edge_kernel(True, *operands[:9], part, sent, *operands[9:])
-
+    (part,) = bulk(True, False, q1, geometry, q, meta)
     (advanced,) = local(
-        last_edges,
+        last_kernel,
         [FIELD],
         (part, joint, q1, geometry, one, two, three, mate, from_even, from_odd, meta),
-        HALO + [pltpu.VMEM((BELOW, 128), jnp.float32)] + [TILE] * 2,
+        HALO
+        + [pltpu.VMEM((BELOW, 128), jnp.float32), TILE, TILE, pltpu.VMEM((4, LEN, CELLS), jnp.float32)]
+        + [pltpu.SemaphoreType.DMA((TILES // GROUP,))],
+        out_specs=[HBM],
     )
     return advanced.reshape(state.shape)
 

time: 37.2 us -> 36 us (0.968)
  waiting for transfers between devices: 4.66 us -> 2.85 us
  starting transfers between devices: 18.9 us -> 19.7 us
    ppermute x3, waiting for transfers between devices: 4.22 us -> 1.27 us  [on_device(): lax.ppermute(joint, 'seg', [(i, i ^ s) for i in range(SEGS)])]
    ppermute x2, waiting for transfers between devices: 0.43 us -> 1.58 us  [along_chain(): lax.ppermute(odd, 'blk', pairs + [(b, a) for a, b in pairs])]
    ppermute x2, starting transfers between devices: 2.65 us -> 3.41 us  [along_chain(): from_even = lax.ppermute(even, 'blk', [(i, i ^ 1) for i in range(CHAIN)])]
  transfers between devices with their start and end apart: 8 -> 8, of which waited for: 3 -> 4; matrix products, arithmetic and copies ran while one was open for 0% -> 0% of each run, Pallas kernels for 19% -> 20%
where the time goes in v5:
time: 36 us; the launch traced here: 35.8 us
  starting transfers between devices  19.7 us (55%)
  Pallas kernels  13.1 us (36%)
  waiting for transfers between devices  2.85 us (8%)
    ppermute x2, starting transfers between devices, along_chain(): lax.ppermute(odd, 'blk', pairs + [(b, a) for a, b in pairs])  10.9 us
    pallas_call x6, Pallas kernels, local(): pl.pallas_call(kernel, out_shape=shapes, in_specs=[VMEM] * (len(operands)...  10.7 us
    ppermute x2, starting transfers between devices, along_chain(): from_even = lax.ppermute(even, 'blk', [(i, i ^ 1) for i in range(CHAIN)])  3.41 us
    ppermute x3, starting transfers between devices, on_device(): lax.ppermute(joint, 'seg', [(i, i ^ s) for i in range(SEGS)])  3.34 us
    pallas_call x1, Pallas kernels, on_device(): pl.pallas_call(first_kernel, out_shape=[FIELD, f32((9, LEN, CELLS)), JOIN...  2.45 us
    ppermute x1, starting transfers between devices, on_device(): mate = lax.ppermute(picked, 'seg', [(i, i ^ 4) for i in range(SEGS)])  2.1 us
    ppermute x2, waiting for transfers between devices, along_chain(): lax.ppermute(odd, 'blk', pairs + [(b, a) for a, b in pairs])  1.58 us
    ppermute x3, waiting for transfers between devices, on_device(): lax.ppermute(joint, 'seg', [(i, i ^ s) for i in range(SEGS)])  1.27 us
  transfers between devices with their start and end apart: 8, of which 4 were waited for; matrix products, arithmetic and copies ran while one was open for 0% of the time, Pallas kernels for 20%

profile of v5, /device:TPU:105, one launch (start us, length us, event | category | flops | bytes accessed | tf_op | source)
XLA Modules:
  0.0 35.8 jit_solution(1291535452986878917)
XLA Ops:
  0.0 2.5 %shard_map.46 = (f32[4,16,2304]{2,1,0:T(8,128)S(1)}, f32[9,16,2304]{2,1,0:T(8,128)S(1)}, f32[224,128]{1,0:T(8,128)S(1)}, s32[16]{0:T(128)S(1)}) custom-call(f32[4,16,2304]{2,1,0:T(8,128)} %bitcast.5, f32[9,16,2304]{2,1,0:T(8,128)} %bitcast.4, s32[256]{0:T(256)} %map_hbm.1, s32[6,4,256]{2,1,0:T(4,128)} %bitcast.6), custom_call_target="tpu_custom_call" | custom-call | tf_op jit(solution)/shard_map/pallas_call | solution.py:490
  2.5 2.6 %collective-permute-start.2 = (f32[224,128]{1,0:T(8,128)S(1)}, f32[224,128]{1,0:T(8,128)S(1)}, u32[]{:S(2)}, u32[]{:S(2)}) collective-permute-start(f32[224,128]{1,0:T(8,128)S(1)} %get-tuple-element.24.own.sent), channel_id=1, source_target_pairs={{0,96},{32,64},{64,32},{96,0},{128,224},{160,192},{192,160},{224,1... | collective-permute-start | bytes 344072 | tf_op jit(solution)/shard_map/ppermute | solution.py:503
  5.0 0.5 %collective-permute-start.1 = (f32[224,128]{1,0:T(8,128)S(1)}, f32[224,128]{1,0:T(8,128)S(1)}, u32[]{:S(2)}, u32[]{:S(2)}) collective-permute-start(f32[224,128]{1,0:T(8,128)S(1)} %get-tuple-element.24.own.sent), channel_id=1, source_target_pairs={{0,64},{32,96},{64,0},{96,32},{128,192},{160,224},{192,128},{224,1... | collective-permute-start | bytes 344072 | tf_op jit(solution)/shard_map/ppermute | solution.py:503
  5.5 0.3 collective-permute-start
  5.8 3.2 %shard_map.47 = (f32[4,16,2304]{2,1,0:T(8,128)S(1)}, f32[8,2304]{1,0:T(8,128)S(1)}, f32[8,2304]{1,0:T(8,128)S(1)}) custom-call(f32[4,16,2304]{2,1,0:T(8,128)S(1)} %get-tuple-element.25.q.rest_0_, f32[9,16,2304]{2,1,0:T(8,128)S(1)} %get-tuple-element.26.metric, s32[16]{0:T(128)S(1)} %get-tuple-element.27.rest_0_.meta.rest_1_), custom_call_target="tpu_custom_call" | custom-call | flops 12000000 | bytes 12000000 | tf_op jit(solution)/shard_map/pallas_call | solution.py:464
  9.0 0.2 collective-permute-done.2.three
  9.2 0.9 %collective-permute-done.1.two = f32[224,128]{1,0:T(8,128)S(1)} collective-permute-done((f32[224,128]{1,0:T(8,128)S(1)}, f32[224,128]{1,0:T(8,128)S(1)}, u32[]{:S(2)}, u32[]{:S(2)}) %collective-permute-start.1) | collective-permute-done | bytes 114720 | tf_op jit(solution)/shard_map/ppermute | solution.py:503
  10.2 0.1 collective-permute-done.one
  10.3 0.6 %shard_map.48 = f32[224,128]{1,0:T(8,128)S(1)} custom-call(f32[224,128]{1,0:T(8,128)S(1)} %get-tuple-element.24.own.sent, f32[224,128]{1,0:T(8,128)S(1)} %collective-permute-done.one, f32[224,128]{1,0:T(8,128)S(1)} %collective-permute-done.1.two, f32[224,128]{1,0:T(8,128)S(1)} %collective-permute-done.2.three, s32[16]{0:T(128)S(1)} %get-tuple-element.27.rest_0_.meta.rest_1_), custom_call_target="tpu_custom_call" | custom-call | flops 1000000 | bytes 1000000 | tf_op jit(solution)/shard_map/pallas_call | solution.py:464
  10.9 2.1 %collective-permute-start.3 = (f32[224,128]{1,0:T(8,128)S(1)}, f32[224,128]{1,0:T(8,128)S(1)}, u32[]{:S(2)}, u32[]{:S(2)}) collective-permute-start(f32[224,128]{1,0:T(8,128)S(1)} %shard_map.48), channel_id=1, source_target_pairs={{0,128},{32,160},{64,192},{96,224},{128,0},{160,32},{192,64},{224,... | collective-permute-start | bytes 344072 | tf_op jit(solution)/shard_map/ppermute | solution.py:508
  13.0 3.3 %collective-permute-start.4 = (f32[8,2304]{1,0:T(8,128)S(1)}, f32[8,2304]{1,0:T(8,128)S(1)}, u32[]{:S(2)}, u32[]{:S(2)}) collective-permute-start(f32[8,2304]{1,0:T(8,128)S(1)} %get-tuple-element.38), channel_id=1, source_target_pairs={{0,1},{1,0},{2,3},{3,2},{4,5},{5,4},{6,7},{7,6},{8,9},{9,8},{10,11... | collective-permute-start | bytes 221192 | tf_op jit(solution)/shard_map/ppermute | solution.py:481
  16.3 5.4 %collective-permute-start.5 = (f32[8,2304]{1,0:T(8,128)S(1)}, f32[8,2304]{1,0:T(8,128)S(1)}, u32[]{:S(2)}, u32[]{:S(2)}) collective-permute-start(f32[8,2304]{1,0:T(8,128)S(1)} %get-tuple-element.39), channel_id=1, source_target_pairs={{1,2},{3,4},{5,6},{7,8},{9,10},{11,12},{13,14},{15,16},{17,18},{19... | collective-permute-start | bytes 221192 | tf_op jit(solution)/shard_map/ppermute | solution.py:483
  21.7 0.0 collective-permute-done.3.mate
  21.8 0.7 %shard_map.49 = (f32[4,16,2304]{2,1,0:T(8,128)S(1)}, f32[8,128]{1,0:T(8,128)S(1)}, f32[8,128]{1,0:T(8,128)S(1)}) custom-call(f32[4,16,2304]{2,1,0:T(8,128)S(1)} %get-tuple-element.31.bulk, f32[4,16,2304]{2,1,0:T(8,128)S(1)} %get-tuple-element.25.q.rest_0_, f32[9,16,2304]{2,1,0:T(8,128)S(1)} %get-tuple-element.26.metric, ...), custom_call_target="tpu_custom_call" | custom-call | flops 1000000 | bytes 1000000 | tf_op jit(solution)/shard_map/pallas_call | solution.py:464
  22.5 0.0 collective-permute-done.4.even_in
  22.5 1.6 %collective-permute-done.5.odd_in = f32[8,2304]{1,0:T(8,128)S(1)} collective-permute-done((f32[8,2304]{1,0:T(8,128)S(1)}, f32[8,2304]{1,0:T(8,128)S(1)}, u32[]{:S(2)}, u32[]{:S(2)}) %collective-permute-start.5) | collective-permute-done | bytes 73760 | tf_op jit(solution)/shard_map/ppermute | solution.py:483
  24.1 1.0 %shard_map.50 = (f32[4,16,2304]{2,1,0:T(8,128)S(1)}, f32[8,2432]{1,0:T(8,128)S(1)}, f32[8,2432]{1,0:T(8,128)S(1)}) custom-call(f32[4,16,2304]{2,1,0:T(8,128)S(1)} %get-tuple-element.35.part, f32[4,16,2304]{2,1,0:T(8,128)S(1)} %get-tuple-element.25.q.rest_0_, f32[9,16,2304]{2,1,0:T(8,128)S(1)} %get-tuple-element.26.metric, ...), custom_call_target="tpu_custom_call" | custom-call | flops 1000000 | bytes 1000000 | tf_op jit(solution)/shard_map/pallas_call | solution.py:464
  25.1 0.1 collective-permute-start.6
  25.2 5.4 %collective-permute-start.7 = (f32[8,2432]{1,0:T(8,128)S(1)}, f32[8,2432]{1,0:T(8,128)S(1)}, u32[]{:S(2)}, u32[]{:S(2)}) collective-permute-start(f32[8,2432]{1,0:T(8,128)S(1)} %get-tuple-element.42), channel_id=1, source_target_pairs={{1,2},{3,4},{5,6},{7,8},{9,10},{11,12},{13,14},{15,16},{17,18},{19... | collective-permute-start | bytes 233480 | tf_op jit(solution)/shard_map/ppermute | solution.py:483
  30.7 3.2 %shard_map.51.part = f32[4,16,2304]{2,1,0:T(8,128)S(1)} custom-call(f32[4,16,2304]{2,1,0:T(8,128)S(1)} %get-tuple-element.40.q, f32[9,16,2304]{2,1,0:T(8,128)S(1)} %get-tuple-element.26.metric, f32[4,16,2304]{2,1,0:T(8,128)S(1)} %get-tuple-element.25.q.rest_0_, s32[16]{0:T(128)S(1)} %get-tuple-element.27.rest_0_.meta.rest_1_), custom_call_target="tpu_custom_call" | custom-call | flops 12000000 | bytes 12000000 | tf_op jit(solution)/shard_map/pallas_call | solution.py:464
  33.8 0.0 collective-permute-done.6.even_in
  33.8 0.0 collective-permute-done.7.odd_in
  33.9 1.9 %shard_map.52 = f32[4,16,2304]{2,1,0:T(8,128)} custom-call(f32[4,16,2304]{2,1,0:T(8,128)S(1)} %shard_map.51.part, f32[224,128]{1,0:T(8,128)S(1)} %get-tuple-element.24.own.sent, f32[4,16,2304]{2,1,0:T(8,128)S(1)} %get-tuple-element.40.q, f32[9,16,2304]{2,1,0:T(8,128)S(1)} %get-tuple-element.26.metric, f32[224,128]{1,0:T(8,128)S(1)} %collective-permute-done.one, ...), custom_call_target="tpu_custom_call" | custom-call | flops 1000000 | bytes 1000000 | tf_op jit(solution)/shard_map/pallas_call | solution.py:464
Async XLA Ops:
  2.5 6.8 %collective-permute-start.2 = (f32[224,128]{1,0:T(8,128)S(1)}, f32[224,128]{1,0:T(8,128)S(1)}, u32[]{:S(2)}, u32[]{:S(2)}) collective-permute-start(f32[224,128]{1,0:T(8,128)S(1)} %get-tuple-element.24.own.sent), channel_id=1, source_target_pairs={{0,96},{32,64},{64,32},{96,0},{128,224},{160,192},{192,160},{224,1... | collective-permute-start | bytes 344072 | tf_op jit(solution)/shard_map/ppermute | solution.py:503
  5.0 5.1 %collective-permute-start.1 = (f32[224,128]{1,0:T(8,128)S(1)}, f32[224,128]{1,0:T(8,128)S(1)}, u32[]{:S(2)}, u32[]{:S(2)}) collective-permute-start(f32[224,128]{1,0:T(8,128)S(1)} %get-tuple-element.24.own.sent), channel_id=1, source_target_pairs={{0,64},{32,96},{64,0},{96,32},{128,192},{160,224},{192,128},{224,1... | collective-permute-start | bytes 344072 | tf_op jit(solution)/shard_map/ppermute | solution.py:503
  5.5 4.7 %collective-permute-start = (f32[224,128]{1,0:T(8,128)S(1)}, f32[224,128]{1,0:T(8,128)S(1)}, u32[]{:S(2)}, u32[]{:S(2)}) collective-permute-start(f32[224,128]{1,0:T(8,128)S(1)} %get-tuple-element.24.own.sent), channel_id=1, source_target_pairs={{0,32},{32,0},{64,96},{96,64},{128,160},{160,128},{192,224},{224,1... | collective-permute-start | bytes 344072 | tf_op jit(solution)/shard_map/ppermute | solution.py:503
  10.9 10.9 %collective-permute-start.3 = (f32[224,128]{1,0:T(8,128)S(1)}, f32[224,128]{1,0:T(8,128)S(1)}, u32[]{:S(2)}, u32[]{:S(2)}) collective-permute-start(f32[224,128]{1,0:T(8,128)S(1)} %shard_map.48), channel_id=1, source_target_pairs={{0,128},{32,160},{64,192},{96,224},{128,0},{160,32},{192,64},{224,... | collective-permute-start | bytes 344072 | tf_op jit(solution)/shard_map/ppermute | solution.py:508
  13.0 9.5 %collective-permute-start.4 = (f32[8,2304]{1,0:T(8,128)S(1)}, f32[8,2304]{1,0:T(8,128)S(1)}, u32[]{:S(2)}, u32[]{:S(2)}) collective-permute-start(f32[8,2304]{1,0:T(8,128)S(1)} %get-tuple-element.38), channel_id=1, source_target_pairs={{0,1},{1,0},{2,3},{3,2},{4,5},{5,4},{6,7},{7,6},{8,9},{9,8},{10,11... | collective-permute-start | bytes 221192 | tf_op jit(solution)/shard_map/ppermute | solution.py:481
  16.3 7.8 %collective-permute-start.5 = (f32[8,2304]{1,0:T(8,128)S(1)}, f32[8,2304]{1,0:T(8,128)S(1)}, u32[]{:S(2)}, u32[]{:S(2)}) collective-permute-start(f32[8,2304]{1,0:T(8,128)S(1)} %get-tuple-element.39), channel_id=1, source_target_pairs={{1,2},{3,4},{5,6},{7,8},{9,10},{11,12},{13,14},{15,16},{17,18},{19... | collective-permute-start | bytes 221192 | tf_op jit(solution)/shard_map/ppermute | solution.py:483
  25.1 8.7 %collective-permute-start.6 = (f32[8,2432]{1,0:T(8,128)S(1)}, f32[8,2432]{1,0:T(8,128)S(1)}, u32[]{:S(2)}, u32[]{:S(2)}) collective-permute-start(f32[8,2432]{1,0:T(8,128)S(1)} %get-tuple-element.41), channel_id=1, source_target_pairs={{0,1},{1,0},{2,3},{3,2},{4,5},{5,4},{6,7},{7,6},{8,9},{9,8},{10,11... | collective-permute-start | bytes 233480 | tf_op jit(solution)/shard_map/ppermute | solution.py:481
  25.2 8.6 %collective-permute-start.7 = (f32[8,2432]{1,0:T(8,128)S(1)}, f32[8,2432]{1,0:T(8,128)S(1)}, u32[]{:S(2)}, u32[]{:S(2)}) collective-permute-start(f32[8,2432]{1,0:T(8,128)S(1)} %get-tuple-element.42), channel_id=1, source_target_pairs={{1,2},{3,4},{5,6},{7,8},{9,10},{11,12},{13,14},{15,16},{17,18},{19... | collective-permute-start | bytes 233480 | tf_op jit(solution)/shard_map/ppermute | solution.py:483
